TPU v7x, 128 devices: a whole 4x4x4 slice. The times are simulated.
128 devices in a mesh: cube: 16 (over y_lo, x, core), row: 4 (over z), col: 2 (over y_hi).
Axes of the slice: x: 4, y: 4 (y_hi: 2, y_lo: 2; y = y_hi * 2 + y_lo), z: 4, core: 2. Of those that a mesh axis runs over, the one named last changes fastest.
Arguments:
- update_tiles: float32 [16, 4, 2, 128, 128, 128], P('cube', 'row', 'col'), may hold values from -1.5 to 1.5
- split_order: int32 [16, 4, 2, 4, 128], P('cube', 'row', 'col'), may hold values from 0 to 127, each once within a row
- first_source: int32 [16, 4, 2, 4, 128], P('cube', 'row', 'col'), may hold values from 0 to 127, each once within a row
- second_source: int32 [16, 4, 2, 4, 128], P('cube', 'row', 'col'), may hold values from 0 to 127
- pivot_inverse: float32 [512, 512], replicated, may hold values from -0.01171875 to 0.01171875
Outputs:
- schur: float32 [16, 4, 2, 512, 4096], P('cube', 'row', 'col')
Inputs may be any that keep to these rules, and one draw needn't show every extreme that they name: Each level's list of split_order on a device holds every tile number once. Each level's list of first_source on a device holds every joined tile number once.
All inputs are finite; a program needn't handle non-finite values.
Results may differ from a plain program's by a relative error of at most 0.00013.
Values sent between devices are 32-bit elements; how exact they have to be, the bound alone decides.
No kernel may reach another device: no remote copies, remote signals or barrier semaphores. Data moves between devices by JAX's collectives and lax.ppermute only.
A program may use at most 128 MiB of HBM per device.

v0:
```python
import jax
import jax.numpy as jnp
from jax import lax
from jax.sharding import PartitionSpec as P

KR = 4
PW = 512
LEVELS = 4


def partner(block, axis, apart):
    count = lax.axis_size(axis)
    route = []
    for low in range(count):
        high = low | 1 << apart
        if high != low and high < count:
            route += [(low, high), (high, low)]
    return lax.ppermute(block, axis, route)


def spread(value, axis, root):
    mine = lax.axis_index(axis) == root
    return lax.psum(jnp.where(mine, value, jnp.zeros_like(value)), axis)


def body(update_tiles, split_order, first_source, second_source, pivot_inverse):
    front_tiles = update_tiles[0, 0, 0]
    tile_count = front_tiles.shape[0]
    tile_size = front_tiles.shape[1]
    half_count = tile_count // 2
    bit_count = lax.axis_size("cube").bit_length() - 1
    for level_index in range(LEVELS):
        sent_order = split_order[0, 0, 0, level_index]
        arranged = jnp.take(front_tiles, sent_order, axis=0)
        received = partner(arranged[:half_count], "cube", level_index % bit_count)
        joined = jnp.concatenate([arranged[half_count:], received], axis=0)
        front_tiles = jnp.take(joined, first_source[0, 0, 0, level_index], axis=0) + jnp.take(
            joined, second_source[0, 0, 0, level_index], axis=0
        )
    column_tiles = tile_count // KR
    front_block = (
        front_tiles.reshape(KR, column_tiles, tile_size, tile_size)
        .transpose(0, 2, 1, 3)
        .reshape(KR * tile_size, column_tiles * tile_size)
    )
    pivot_cols = spread(front_block[:, :PW], "col", 0)
    row_block = spread(front_block, ("cube", "row"), 0)
    panel_left = jnp.dot(pivot_cols, pivot_inverse, precision=lax.Precision.HIGHEST)
    update = jnp.dot(panel_left, row_block, precision=lax.Precision.HIGHEST)
    schur = front_block - update
    return schur[None, None, None]


def solution(mesh):
    return jax.shard_map(
        body,
        mesh=mesh,
        in_specs=(
            P("cube", "row", "col", None, None, None),
            P("cube", "row", "col", None, None),
            P("cube", "row", "col", None, None),
            P("cube", "row", "col", None, None),
            P(),
        ),
        out_specs=P("cube", "row", "col", None, None),
        check_vma=False,
    )
```

profile of v0, /device:TPU:0, one launch (start us, length us, event | category | flops | bytes accessed | tf_op | source)
XLA Modules:
  0.0 1139.8 jit_solution(8327487011511299149)
XLA Ops:
  7.4 7.9 gather_fusion
  15.3 4.0 broadcast_select_fusion.3
  20.6 7.1 collective-permute-done
  27.6 4.0 pad_maximum_fusion
  31.6 7.7 gather_fusion.1
  39.3 7.7 gather_fusion.2
  47.0 10.0 select_add_fusion.3
  57.0 7.7 gather_fusion.3
  64.7 4.0 broadcast_select_fusion.2
  71.5 91.0 %collective-permute-done.1 = f32[64,128,128]{2,1,0:T(8,128)S(1)} collective-permute-done((f32[64,128,128]{2,1,0:T(8,128)S(1)}, f32[64,128,128]{2,1,0:T(8,128)S(1)}, u32[]{:S(2)}, u32[]{:S(2)}) %collective-permute-start.1) | collective-permute-done | bytes 4194336 | tf_op jit(solution)/shard_map/ppermute | solution.py:18
  166.5 7.7 gather_fusion.4
  174.2 7.7 gather_fusion.5
  181.9 10.0 select_add_fusion.2
  191.9 7.7 gather_fusion.6
  199.6 4.0 broadcast_select_fusion
  208.4 90.2 %collective-permute-done.2 = f32[64,128,128]{2,1,0:T(8,128)S(1)} collective-permute-done((f32[64,128,128]{2,1,0:T(8,128)S(1)}, f32[64,128,128]{2,1,0:T(8,128)S(1)}, u32[]{:S(2)}, u32[]{:S(2)}) %collective-permute-start.2) | collective-permute-done | bytes 4194336 | tf_op jit(solution)/shard_map/ppermute | solution.py:18
  302.6 7.7 gather_fusion.7
  310.3 7.7 gather_fusion.8
  318.0 10.0 select_add_fusion.1
  328.0 7.7 gather_fusion.9
  335.7 4.0 broadcast_select_fusion.1
  345.3 89.5 %collective-permute-done.3 = f32[64,128,128]{2,1,0:T(8,128)} collective-permute-done((f32[64,128,128]{2,1,0:T(8,128)}, f32[64,128,128]{2,1,0:T(8,128)}, u32[]{:S(2)}, u32[]{:S(2)}) %collective-permute-start.3) | collective-permute-done | bytes 4194336 | tf_op jit(solution)/shard_map/ppermute | solution.py:18
  434.8 8.0 pad_maximum_fusion.3
  442.8 7.7 gather_fusion.10
  450.5 7.7 gather_fusion.11
  458.2 6.7 select_add_fusion
  464.9 4.9 copy.6
  469.8 8.5 copy.13
  479.5 15.0 %broadcast_select_fusion.4 = f32[512,4096]{1,0:T(8,128)} fusion(pred[]{:T(512)S(6)} %eq.7, f32[64,8,32,128]{3,2,1,0:T(8,128)} %bitcast.55), kind=kLoop, calls=%fused_computation.26 | loop fusion | flops 2097152 | bytes 16777216 | tf_op jit(solution)/shard_map/jit(_where)/select_n | solution.py:23
  494.5 35.7 %all-reduce.3.cloned.1.call-done = f32[512,512]{1,0:T(8,128)} async-done(((f32[512,512]{1,0:T(8,128)}), f32[512,512]{1,0:T(8,128)}) %all-reduce.3.cloned.1.call-update) | async-done | bytes 1048592 | tf_op jit(solution)/shard_map/psum | solution.py:23
  533.3 577.4 %all-reduce.5.cloned.1.call-done = f32[512,4096]{1,0:T(8,128)} async-done(((f32[512,4096]{1,0:T(8,128)}), f32[512,4096]{1,0:T(8,128)}) %all-reduce.5.cloned.1.call-update) | async-done | bytes 8388624 | tf_op jit(solution)/shard_map/psum | solution.py:23
  1110.6 21.9 %subtract_bitcast_fusion = f32[1,1,1,512,4096]{4,3,2,1,0:T(8,128)} fusion(f32[512,512]{1,0:T(8,128)S(1)} %fusion.4, f32[512,4096]{1,0:T(8,128)} %all-reduce.5.cloned.1.call-done, f32[64,8,32,128]{3,2,1,0:T(8,128)} %bitcast.56), kind=kOutput, calls=%fused_computation.21 | convolution fusion | flops 12886999040 | bytes 26214400 | tf_op jit(solution)/shard_map/dot_general | solution.py:49
  (36 shorter events, 27.4 us)
Async XLA Ops:
  6.5 523.7 %copy-start = (f32[512,512]{1,0:T(8,128)S(1)}, f32[512,512]{1,0:T(8,128)}, u32[]{:S(2)}) copy-start(f32[512,512]{1,0:T(8,128)} %param.11) | copy-start | bytes 3145732
  6.5 523.7 %all-reduce.3.cloned.1.call-start = ((), (), s32[]{:S(2)}) async-start(), calls=%async_computation | async-start | bytes 2097152 | tf_op jit(solution)/shard_map/psum | solution.py:23
  19.3 1.2 copy-start.2
  19.3 1.2 copy-start.3
  20.4 7.2 collective-permute-start
  69.8 92.7 %collective-permute-start.1 = (f32[64,128,128]{2,1,0:T(8,128)S(1)}, f32[64,128,128]{2,1,0:T(8,128)S(1)}, u32[]{:S(2)}, u32[]{:S(2)}) collective-permute-start(f32[64,128,128]{2,1,0:T(8,128)S(1)} %get-tuple-element.35), channel_id=1, source_target_pairs={{0,16},{16,0},{8,24},{24,8},{32,48},{48,32},{40,56},{56,40},{64,80... | collective-permute-start | bytes 12582920 | tf_op jit(solution)/shard_map/ppermute | solution.py:18
  204.8 93.8 %collective-permute-start.2 = (f32[64,128,128]{2,1,0:T(8,128)S(1)}, f32[64,128,128]{2,1,0:T(8,128)S(1)}, u32[]{:S(2)}, u32[]{:S(2)}) collective-permute-start(f32[64,128,128]{2,1,0:T(8,128)S(1)} %get-tuple-element.33), channel_id=1, source_target_pairs={{0,32},{32,0},{8,40},{40,8},{16,48},{48,16},{24,56},{56,24},{64,96... | collective-permute-start | bytes 12582920 | tf_op jit(solution)/shard_map/ppermute | solution.py:18
  343.7 91.2 %collective-permute-start.3 = (f32[64,128,128]{2,1,0:T(8,128)}, f32[64,128,128]{2,1,0:T(8,128)}, u32[]{:S(2)}, u32[]{:S(2)}) collective-permute-start(f32[64,128,128]{2,1,0:T(8,128)} %get-tuple-element.31), channel_id=1, source_target_pairs={{0,64},{64,0},{8,72},{72,8},{16,80},{80,16},{24,88},{88,24},{32,96... | collective-permute-start | bytes 12582920 | tf_op jit(solution)/shard_map/ppermute | solution.py:18
  469.8 8.6 copy-start.1
  479.5 631.2 %all-reduce.5.cloned.1.call-start = ((), (), s32[]{:S(2)}) async-start(), calls=%async_computation.1 | async-start | bytes 16777216 | tf_op jit(solution)/shard_map/psum | solution.py:23
Sparse Core Ops, SparseCore 0:
  479.6 50.5 all-reduce.2
  532.9 577.7 all-reduce.4
where the time goes:
time: 1150 us; the launch traced here: 1140 us
  waiting for transfers between devices  891 us (77%)
  local copies, waits for them, and re-layouts  113 us (10%)
  other arithmetic  89.6 us (8%)
  matrix products  25 us (2%)
  between operations  14 us (1%)
    psum x2, waiting for transfers between devices, spread(): return lax.psum(jnp.where(mine, value, jnp.zeros_like(value)), axis)  613 us
    ppermute x4, waiting for transfers between devices, partner(): return lax.ppermute(block, axis, route)  278 us
    add x4, other arithmetic, body(): jnp.take(joined, first_source[0, 0, 0, level_index], axis=0)  36.7 us
    gather x4, local copies, waits for them, and re-layouts, body(): arranged = jnp.take(front_tiles, sent_order, axis=0)  31 us
    gather x4, local copies, waits for them, and re-layouts, body(): jnp.take(joined, first_source[0, 0, 0, level_index], axis=0)  30.8 us
    gather x4, local copies, waits for them, and re-layouts, body(): jnp.take(joined, second_source[0, 0, 0, level_index], axis=0)  30.8 us
  transfers between devices with their start and end apart: 6, of which 6 were waited for; matrix products, arithmetic and copies ran while one was open for 2% of the time, Pallas kernels for 0%

commit v1 on v0

v1 whole, which is shorter than its diff:
```python
import jax
import jax.numpy as jnp
from jax import lax
from jax.experimental import pallas as pl
from jax.experimental.pallas import tpu as pltpu
from jax.sharding import PartitionSpec as P

TB = 128
KR = 4
KC = 32
PW = 512
K = 128
HALF = 64
LEVELS = 4
F32 = jnp.float32
BF16 = jnp.bfloat16

CHUNKS = ((96, 16), (0, 32), (32, 32), (64, 32), (112, 16))
PARTS = ((0, 64), (64, 64))

ANY = pl.BlockSpec(memory_space=pl.ANY)
SMEM = pl.BlockSpec(memory_space=pltpu.SMEM)
VMEM = pl.BlockSpec(memory_space=pltpu.VMEM)
DMA = pltpu.SemaphoreType.DMA


def nt(a, b):
    return lax.dot_general(a, b, (((1,), (1,)), ((), ())), preferred_element_type=F32)


def split2(x):
    high = x.astype(BF16)
    return high, (x - high.astype(F32)).astype(BF16)


def run(body, ins, outs, scratch, limit=32, **more):
    return pl.pallas_call(
        body,
        in_specs=[s for _, s in ins],
        out_specs=[s for _, _, s in outs],
        out_shape=[jax.ShapeDtypeStruct(s, d) for s, d, _ in outs],
        scratch_shapes=scratch,
        compiler_params=pltpu.CompilerParams(vmem_limit_bytes=limit << 20),
        **more,
    )(*[a for a, _ in ins])


def first_send(row, rows, tiles, split, tok):
    def body(split_ref, tiles_ref, _, send_ref, pool, buf, sem):
        get = pltpu.make_async_copy(tiles_ref.at[:, pl.ds(row, rows), :], pool, sem.at[0])
        get.start()
        get.wait()

        def step(i, c):
            buf[i] = pool[split_ref[0, i]]
            return c

        lax.fori_loop(0, HALF, step, 0, unroll=8)
        put = pltpu.make_async_copy(buf, send_ref, sem.at[1])
        put.start()
        put.wait()

    return run(
        body,
        [(split, SMEM), (tiles, ANY), (tok, ANY)],
        [((HALF, rows, TB), F32, ANY)],
        [pltpu.VMEM((K, rows, TB), F32), pltpu.VMEM((HALF, rows, TB), F32), DMA((2,))],
    )


def fetch(level, row, rows, kept_ref, recv_ref, pool, sem):
    own = kept_ref.at[:, pl.ds(row, rows), :] if level == 0 else kept_ref
    n = K if level == 0 else HALF
    one = pltpu.make_async_copy(own, pool.at[pl.ds(0, n)], sem.at[0])
    two = pltpu.make_async_copy(recv_ref, pool.at[pl.ds(n, HALF)], sem.at[1])
    one.start()
    two.start()
    one.wait()
    two.wait()


def place(level, split_ref, j):
    if level == 0:
        return jnp.where(j < HALF, split_ref[0, (j + HALF) & (K - 1)], j + HALF)
    return j


def next_level(level, row, rows, kept, recv, split, first, second, tok):
    n = K if level == 0 else HALF

    def body(split_ref, first_ref, second_ref, kept_ref, recv_ref, _, send_ref, keep_ref, pool, buf, sem):
        fetch(level, row, rows, kept_ref, recv_ref, pool, sem)

        def step(i, c):
            t = split_ref[level + 1, i]
            a = place(level, split_ref, first_ref[level, t])
            b = place(level, split_ref, second_ref[level, t])
            buf[i] = pool[a] + pool[b]
            return c

        lax.fori_loop(0, HALF, step, 0, unroll=8)
        one = pltpu.make_async_copy(buf.at[pl.ds(0, HALF)], send_ref, sem.at[2])
        one.start()
        lax.fori_loop(HALF, K, step, 0, unroll=8)
        two = pltpu.make_async_copy(buf.at[pl.ds(HALF, HALF)], keep_ref, sem.at[3])
        two.start()
        one.wait()
        two.wait()

    return run(
        body,
        [(split, SMEM), (first, SMEM), (second, SMEM), (kept, ANY), (recv, ANY), (tok, ANY)],
        [((HALF, rows, TB), F32, ANY)] * 2,
        [pltpu.VMEM((n + HALF, rows, TB), F32), pltpu.VMEM((K, rows, TB), F32), DMA((4,))],
    )


def last_level(rows, kept, recv, first, second, tok):
    def body(first_ref, second_ref, kept_ref, recv_ref, _, cols_ref, front_ref, pool, buf, cbuf, sem):
        level = LEVELS - 1
        fetch(level, 0, rows, kept_ref, recv_ref, pool, sem)
        for i in range(KR):
            for j in range(PW // TB):
                t = i * KC + j
                tile = pool[first_ref[level, t]] + pool[second_ref[level, t]]
                buf[i, :, j * TB:(j + 1) * TB] = tile
                cbuf[i, :, j * TB:(j + 1) * TB] = tile
        one = pltpu.make_async_copy(cbuf, cols_ref, sem.at[2])
        one.start()
        for i in range(KR):

            def step(j, c):
                t = i * KC + j
                at = pl.ds(pl.multiple_of(j * TB, TB), TB)
                buf[i, :, at] = pool[first_ref[level, t]] + pool[second_ref[level, t]]
                return c

            lax.fori_loop(PW // TB, KC, step, 0, unroll=4)
        two = pltpu.make_async_copy(buf, front_ref, sem.at[3])
        two.start()
        one.wait()
        two.wait()

    return run(
        body,
        [(first, SMEM), (second, SMEM), (kept, ANY), (recv, ANY), (tok, ANY)],
        [((KR, rows, PW), F32, ANY), ((KR, rows, KC * TB), F32, ANY)],
        [
            pltpu.VMEM((K, rows, TB), F32),
            pltpu.VMEM((KR, rows, KC * TB), F32),
            pltpu.VMEM((KR, rows, PW), F32),
            DMA((4,)),
        ],
    )


def joined_weights(own, other):
    lane = lax.broadcasted_iota(jnp.int32, (K, K), 1)
    return jnp.where(lane < HALF, own, other)


def weights_back(level, own, other, place_ids, lists, tok):
    top = level == LEVELS - 1

    def body(ids_ref, lists_ref, *refs):
        out_ref = refs[-1]
        row = lax.broadcasted_iota(jnp.int32, (K, K), 0)
        lane = lax.broadcasted_iota(jnp.int32, (K, K), 1)
        if top:
            root = jnp.logical_and(ids_ref[0] == 0, ids_ref[1] == 0)
            weight = jnp.where(jnp.logical_and(row == lane, root), 1.0, 0.0)
        else:
            order = lists_ref[12 + level + 1: 13 + level + 1, :]
            joined = joined_weights(refs[0][...], refs[1][...])
            weight = nt(joined.astype(BF16), jnp.where(row == order, 1.0, 0.0).astype(BF16))
        one = jnp.where(row == lists_ref[4 + level: 5 + level, :], 1.0, 0.0)
        two = jnp.where(row == lists_ref[8 + level: 9 + level, :], 1.0, 0.0)
        out_ref[...] = jnp.dot(weight.astype(BF16), (one + two).T.astype(BF16), preferred_element_type=F32)

    ins = [(place_ids, SMEM), (lists, VMEM)]
    if not top:
        ins += [(own, VMEM), (other, VMEM)]
    return run(body, ins + [(tok, ANY)], [((K, K), F32, VMEM)], [])


def parts_of(row, rows, own, other, place_ids, lists, tiles, tok):
    def body(ids_ref, lists_ref, own_ref, other_ref, tiles_ref, _, keep_ref, send_ref, pool, buf, sem):
        get = pltpu.make_async_copy(tiles_ref.at[:, pl.ds(row, rows), :], pool, sem.at[0])
        get.start()
        r = lax.broadcasted_iota(jnp.int32, (K, K), 0)
        c = lax.broadcasted_iota(jnp.int32, (K, K), 1)
        joined = joined_weights(own_ref[...], other_ref[...]).astype(BF16)
        weight = nt(joined, jnp.where(r == lists_ref[12:13, :], 1.0, 0.0).astype(BF16)).astype(BF16)
        turn = jnp.where(c == jnp.bitwise_xor(r, ids_ref[3]), 1.0, 0.0).astype(BF16)
        weight = jnp.dot(turn, weight, preferred_element_type=F32).astype(BF16)
        get.wait()
        flat = pool.reshape(K * rows, TB)
        out = buf.reshape(K * rows, TB)

        def step(at, carry):
            high, low = split2(flat[pl.ds(at, K, stride=rows), :])
            out[pl.ds(at, K, stride=rows), :] = jnp.dot(weight, high, preferred_element_type=F32) + jnp.dot(
                weight, low, preferred_element_type=F32
            )
            return carry

        lax.fori_loop(0, rows, step, 0, unroll=4)
        one = pltpu.make_async_copy(buf.at[pl.ds(0, HALF)], keep_ref, sem.at[1])
        two = pltpu.make_async_copy(buf.at[pl.ds(HALF, HALF)], send_ref, sem.at[2])
        one.start()
        two.start()
        one.wait()
        two.wait()

    return run(
        body,
        [(place_ids, SMEM), (lists, VMEM), (own, VMEM), (other, VMEM), (tiles, ANY), (tok, ANY)],
        [((HALF, rows, TB), F32, ANY)] * 2,
        [pltpu.VMEM((K, rows, TB), F32), pltpu.VMEM((K, rows, TB), F32), DMA((3,))],
    )


def add_cut(terms, cuts, rows, tok):
    def body(*refs):
        total = refs[0][...]
        for term in refs[1:len(terms)]:
            total = total + term[...]
        at = 0
        for cut, ref in zip(cuts, refs[len(terms) + 1:]):
            ref[...] = total[at:at + cut]
            at += cut

    return run(
        body, [(t, VMEM) for t in terms] + [(tok, ANY)], [((cut, rows, TB), F32, VMEM) for cut in cuts], []
    )


def lay(pieces, rows, tok):
    count = sum(p.shape[0] for p in pieces)

    def body(*refs):
        out_ref, sem = refs[-2:]
        copies = []
        at = 0
        for n, piece in enumerate(pieces):
            copies.append(
                pltpu.make_async_copy(refs[n], out_ref.at[pl.ds(at, piece.shape[0])], sem.at[n])
            )
            at += piece.shape[0]
        for copy in copies:
            copy.start()
        for copy in copies:
            copy.wait()

    return run(body, [(p, ANY) for p in pieces] + [(tok, ANY)], [((count, rows, TB), F32, ANY)], [DMA((len(pieces),))])


def panel(row, rows, low, high, place_ids, inverse, before, last, tok):
    wide = 4
    width = wide * TB

    def body(*refs):
        ids_ref, inv_ref, low_ref, high_ref = refs[:4]
        before_ref = refs[4] if before is not None else None
        at = 5 if before is not None else 4
        outs = refs[at + 1: at + (3 if last else 2)]
        pool, rhs_h, rhs_l, sem = refs[-4:]
        one = pltpu.make_async_copy(low_ref, pool.at[pl.ds(0, HALF)], sem.at[0])
        two = pltpu.make_async_copy(high_ref, pool.at[pl.ds(HALF, HALF)], sem.at[1])
        one.start()
        two.start()
        mask = ids_ref[3]
        pieces = [split2(inv_ref[:, i * TB + row: i * TB + row + rows]) for i in range(KR)]
        inv_h = jnp.concatenate([p[0] for p in pieces], axis=1)
        inv_l = jnp.concatenate([p[1] for p in pieces], axis=1)
        one.wait()
        two.wait()

        def step(n, c):
            for j in range(wide):
                for i in range(KR):
                    s = jnp.bitwise_xor(i * KC + n * wide + j, mask)
                    slot = (s & 64) + ((s >> 3) & 3) * 16 + ((s >> 5) & 1) * 8 + (s & 7)
                    h, lo = split2(pool[slot])
                    rhs_h[i * rows:(i + 1) * rows, j * TB:(j + 1) * TB] = h
                    rhs_l[i * rows:(i + 1) * rows, j * TB:(j + 1) * TB] = lo
            h = rhs_h[...]
            total = jnp.dot(inv_h, h, preferred_element_type=F32)
            total += jnp.dot(inv_l, h, preferred_element_type=F32)
            total += jnp.dot(inv_h, rhs_l[...], preferred_element_type=F32)
            cols = pl.ds(pl.multiple_of(n * width, width), width)
            if before is not None:
                total += before_ref[:, cols]
            if last:
                outs[0][:, cols], outs[1][:, cols] = split2(total)
            else:
                outs[0][:, cols] = total
            return c

        lax.fori_loop(0, KC // wide, step, 0)

    ins = [(place_ids, SMEM), (inverse, VMEM), (low, ANY), (high, ANY)]
    if before is not None:
        ins.append((before, VMEM))
    shape = (PW, KC * TB)
    return run(
        body,
        ins + [(tok, ANY)],
        [(shape, BF16, VMEM)] * 2 if last else [(shape, F32, VMEM)],
        [
            pltpu.VMEM((K, rows, TB), F32),
            pltpu.VMEM((KR * rows, width), BF16),
            pltpu.VMEM((KR * rows, width), BF16),
            DMA((2,)),
        ],
        limit=48,
    )


def update(row, rows, front, cols, cols_sent, place_ids, high, low, out, tok):
    width = 1024

    def body(ids_ref, cols_ref, sent_ref, front_ref, high_ref, low_ref, *rest):
        out_ref = rest[-1]
        own = jnp.where(ids_ref[2] == 0, cols_ref[...], sent_ref[...]).reshape(KR * rows, PW)
        h, lo = split2(own)
        q = high_ref[...]
        total = jnp.dot(h, q, preferred_element_type=F32)
        total += jnp.dot(lo, q, preferred_element_type=F32)
        total += jnp.dot(h, low_ref[...], preferred_element_type=F32)
        out_ref[...] = front_ref[...] - total.reshape(KR, rows, width)

    pivot = pl.BlockSpec((KR, rows, PW), lambda n: (0, 0, 0))
    ins = [
        (place_ids, SMEM),
        (cols, pivot),
        (cols_sent, pivot),
        (front, pl.BlockSpec((KR, rows, width), lambda n: (0, 0, n))),
        (high, pl.BlockSpec((PW, width), lambda n: (0, n))),
        (low, pl.BlockSpec((PW, width), lambda n: (0, n))),
        (tok, ANY),
    ]
    more = {}
    if out is not None:
        ins.append((out, ANY))
        more["input_output_aliases"] = {len(ins) - 1: 0}
    return run(
        body,
        ins,
        [((KR, TB, KC * TB), F32, pl.BlockSpec((KR, rows, width), lambda n: (0, row // rows, n)))],
        [],
        grid=(KC * TB // width,),
        **more,
    )


class Plan:
    def __init__(self):
        self.steps = []

    def kernel(self, name, need, give, cost, call):
        self.steps.append((name, "kernel", need, give, cost, call))

    def permute(self, name, need, give, links, cost, call):
        self.steps.append((name, "permute", [need], [give], (links, cost), call))

    def order(self):
        ready, links = {}, {}
        todo = [s for s in self.steps if s[1] == "kernel"]
        moves = [s for s in self.steps if s[1] == "permute"]
        at, result = 0.0, []

        def move():
            nonlocal at
            for m in list(moves):
                if m[2][0] in ready:
                    moves.remove(m)
                    names, cost = m[4]
                    at += 1.0
                    begin = max([at] + [links.get(n, 0.0) for n in names])
                    for n in names:
                        links[n] = begin + cost
                    ready[m[3][0]] = begin + cost + 2.5
                    result.append(m)

        while todo or moves:
            move()
            known = [s for s in todo if all(n in ready for n in s[2])]
            best = min(known, key=lambda s: (max([at] + [ready[n] for n in s[2]]), todo.index(s)))
            todo.remove(best)
            at = max([at] + [ready[n] for n in best[2]]) + best[4]
            for n in best[3]:
                ready[n] = at
            result.append(best)
        self.end = at
        return result


def body(update_tiles, split_order, first_source, second_source, pivot_inverse):
    tiles = update_tiles.reshape(K, TB, TB)
    split, first, second = (x.reshape(LEVELS, K) for x in (split_order, first_source, second_source))
    cube, row_at, col = lax.axis_index("cube"), lax.axis_index("row"), lax.axis_index("col")
    x_at = (cube >> 1) & 3
    mask = (
        (cube & 1) * 64
        + (cube >> 3) * 32
        + row_at * 8
        + jnp.where((x_at == 1) | (x_at == 2), 4, 0)
        + jnp.where(x_at >= 2, 2, 0)
    )
    ids = jnp.stack([cube, row_at, col, mask]).astype(jnp.int32)
    lists = jnp.concatenate([split, first, second, jnp.roll(split, HALF, axis=1)], axis=0)

    def flip(axis, bits):
        return lambda v: lax.ppermute(v, axis, [(i, i ^ bits) for i in range(lax.axis_size(axis))])

    def toward(to):
        return lambda v: lax.ppermute(v, "row", [(0, to)])

    level_links = (("core",), ("xa",), ("xa", "xb"), ("y",))
    link_time = (3.5, 22.8, 22.8, 22.8)
    plan = Plan()
    kernel, permute = plan.kernel, plan.permute

    def level_steps(row, rows):
        n = f"c{row}"
        share = rows / 32
        kernel(f"{n}k0", [], [f"{n}s0"], 1.5 + 1.5 * share, lambda v, tok: first_send(row, rows, tiles, split, tok))
        for level in range(LEVELS):
            permute(f"{n}p{level}", f"{n}s{level}", f"{n}r{level}", level_links[level], link_time[level] * share, flip("cube", 1 << level))
            need = [f"{n}r{level}"] + ([f"{n}h{level}"] if level else [])
            if level < LEVELS - 1:
                kernel(
                    f"{n}k{level + 1}",
                    need,
                    [f"{n}s{level + 1}", f"{n}h{level + 1}"],
                    2 + 2 * share,
                    lambda v, tok, level=level: next_level(
                        level, row, rows, v[f"{n}h{level}"] if level else tiles, v[f"{n}r{level}"], split, first, second, tok
                    ),
                )
            else:
                kernel(
                    f"{n}k4",
                    need,
                    [f"{n}cols", f"{n}front"],
                    2 + 2 * share,
                    lambda v, tok, level=level: last_level(rows, v[f"{n}h3"], v[f"{n}r3"], first, second, tok),
                )
        permute(
            f"{n}pc",
            f"{n}cols",
            f"{n}sent",
            ("y2",),
            5.7 * share,
            lambda v: lax.ppermute(v, "col", [(0, 1)]),
        )

    def weight_steps():
        for level in range(LEVELS - 1, -1, -1):
            up = level + 1
            kernel(
                f"w{level}",
                [f"wo{up}", f"wr{up}"] if up < LEVELS else [],
                [f"wo{level}"],
                1.5,
                lambda v, tok, level=level, up=up: weights_back(level, v.get(f"wo{up}"), v.get(f"wr{up}"), ids, lists, tok),
            )
            permute(f"wp{level}", f"wo{level}", f"wr{level}", level_links[level], 1.0, flip("cube", 1 << level))

    def part_steps(index, row, rows):
        n = f"q{index}"
        m = rows / 128

        def add(name, terms, cuts, cost):
            kernel(
                f"{n}{name}", [f"{n}{t}" for t in terms], [f"{n}{name}{i}" for i in range(len(cuts))], cost,
                lambda v, tok: add_cut([v[f"{n}{t}"] for t in terms], cuts, rows, tok),
            )

        def move(name, what, axis, bits, links, cost):
            permute(f"{n}{name}", f"{n}{what}", f"{n}{name}", links, cost, flip(axis, bits))

        def join(name, pieces, cost):
            kernel(f"{n}{name}", [f"{n}{p}" for p in pieces], [f"{n}{name}"], cost, lambda v, tok: lay([v[f"{n}{p}"] for p in pieces], rows, tok))

        kernel(
            f"{n}t", ["wo0", "wr0"], [f"{n}keep", f"{n}send"], 3 + 10 * m,
            lambda v, tok: parts_of(row, rows, v["wo0"], v["wr0"], ids, lists, tiles, tok),
        )
        move("core", "send", "cube", 1, ("core",), 7 * m)
        add("a", ["keep", "core"], (32, 32), 1 + 4 * m)
        move("y", "a1", "cube", 8, ("y",), 45 * m)
        add("b", ["a0", "y"], (8, 8, 8, 8), 1 + 2 * m)
        for to in (1, 2, 3):
            permute(f"{n}z{to}", f"{n}b{to}", f"{n}z{to}", (("zp",), ("zp", "zm"), ("zm",))[to - 1], 11.4 * m, toward(to))
        add("c", ["b0", "z1", "z2", "z3"], (4, 4), 1.5)
        move("xa", "c1", "cube", 2, ("xa",), 5.7 * m)
        add("d", ["c0", "xa"], (2, 2), 1)
        move("xb", "d1", "cube", 6, ("xb",), 2.9 * m)
        add("e", ["d0", "xb"], (2,), 1)
        move("gb", "e0", "cube", 6, ("xb",), 2.9 * m)
        join("f", ["e0", "gb"], 1)
        move("ga", "f", "cube", 2, ("xa",), 5.7 * m)
        join("g", ["f", "ga"], 1)
        move("gy", "g", "cube", 8, ("y",), 11.4 * m)
        join("h", ["g", "gy"], 1.5)
        for bits in (1, 2, 3):
            move(f"gz{bits}", "h", "row", bits, (("zp",), ("zp", "zm"), ("zm",))[bits - 1], 23 * m)
        join("low", ["h", "gz1", "gz2", "gz3"], 1.5 + 4 * m)
        move("high", "low", "cube", 1, ("core",), 7 * m)
        last = index == len(PARTS) - 1
        kernel(
            f"{n}panel", [f"{n}low", f"{n}high"] + ([f"q{index - 1}panel"] if index else []),
            ["qh", "ql"] if last else [f"{n}panel"], 10,
            lambda v, tok: panel(row, rows, v[f"{n}low"], v[f"{n}high"], ids, pivot_inverse, v.get(f"q{index - 1}panel"), last, tok),
        )

    level_steps(*CHUNKS[0])
    weight_steps()
    for chunk in CHUNKS[1:]:
        level_steps(*chunk)
    for index, part in enumerate(PARTS):
        part_steps(index, *part)
    for index, (row, rows) in enumerate(CHUNKS):
        n = f"c{row}"
        kernel(
            f"{n}u", [f"{n}front", f"{n}cols", f"{n}sent", "qh", "ql"] + ([f"out{index - 1}"] if index else []), [f"out{index}"], 4,
            lambda v, tok, n=n, row=row, rows=rows, index=index: update(
                row, rows, v[f"{n}front"], v[f"{n}cols"], v[f"{n}sent"], ids, v["qh"], v["ql"], v.get(f"out{index - 1}"), tok
            ),
        )

    values = {}
    tok = ids
    for name, kind, need, give, _, call in plan.order():
        if kind == "kernel":
            results = call(values, tok)
            if not give[0].startswith("out"):
                tok = results[0]
            values.update(zip(give, results))
        else:
            values[give[0]] = call(values[need[0]])
    return values[f"out{len(CHUNKS) - 1}"].reshape(1, 1, 1, KR * TB, KC * TB)


def solution(mesh):
    return jax.shard_map(
        body,
        mesh=mesh,
        in_specs=(
            P("cube", "row", "col", None, None, None),
            P("cube", "row", "col", None, None),
            P("cube", "row", "col", None, None),
            P("cube", "row", "col", None, None),
            P(),
        ),
        out_specs=P("cube", "row", "col", None, None),
        check_vma=False,
    )
```

time: 1150 us -> 401 us (0.35)
  waiting for transfers between devices: 891 us -> 192 us
  Pallas kernels: 0 us -> 110 us
  local copies, waits for them, and re-layouts: 113 us -> 14.3 us
  other arithmetic: 89.6 us -> 0.16 us
  starting transfers between devices: 7.09 us -> 82.4 us
  matrix products: 25 us -> 0 us
  between operations: 14 us -> 0.71 us
    psum x2 -> x0, waiting for transfers between devices: 613 us -> none  [spread(): return lax.psum(jnp.where(mine, value, jnp.zeros_like(value)), axis)]
    pallas_call x0 -> x56, Pallas kernels: none -> 110 us  [run(): pl.pallas_call(body, in_specs=[s for _, s in ins], out_specs=[s for _, _,...]
    gather x12 -> x0, local copies, waits for them, and re-layouts: 92.6 us -> none  [the longest x4 31 us: body(): arranged = jnp.take(front_tiles, sent_order, axis=0)]
    ppermute x4 -> x57, waiting for transfers between devices: 278 us -> 192 us  [the longest x46 186 us: flip(): lax.ppermute(v, axis, [(i, i ^ bits) for i in range(lax.axis_size(axis))])]
    ppermute x4 -> x57, starting transfers between devices: 7.05 us -> 82.4 us  [the longest x46 48.2 us: flip(): lax.ppermute(v, axis, [(i, i ^ bits) for i in range(lax.axis_size(axis))])]
    add x4 -> x0, other arithmetic: 36.7 us -> none  [body(): jnp.take(joined, first_source[0, 0, 0, level_index], axis=0)]
    select_n x6 -> x0, other arithmetic: 32.1 us -> none  [the longest x2 16.1 us: spread(): return lax.psum(jnp.where(mine, value, jnp.zeros_like(value)), axis)]
    dot_general x2 -> x0, matrix products: 25 us -> none  [the longest x1 21.9 us: body(): update = jnp.dot(panel_left, row_block, precision=lax.Precision.HIGHEST)]
  transfers between devices with their start and end apart: 6 -> 57, of which waited for: 6 -> 30; matrix products, arithmetic and copies ran while one was open for 2% -> 0% of each run, Pallas kernels for 0% -> 25%
where the time goes in v1:
time: 401 us; the launch traced here: 400 us
  waiting for transfers between devices  192 us (48%)
  Pallas kernels  110 us (27%)
  starting transfers between devices  82.4 us (21%)
  local copies, waits for them, and re-layouts  14.3 us (4%)
    ppermute x46, waiting for transfers between devices, flip(): lax.ppermute(v, axis, [(i, i ^ bits) for i in range(lax.axis_size(axis))])  186 us
    pallas_call x56, Pallas kernels, run(): pl.pallas_call(body, in_specs=[s for _, s in ins], out_specs=[s for _, _,...  110 us
    ppermute x46, starting transfers between devices, flip(): lax.ppermute(v, axis, [(i, i ^ bits) for i in range(lax.axis_size(axis))])  48.2 us
    ppermute x6, starting transfers between devices, toward(): return lambda v: lax.ppermute(v, 'row', [(0, to)])  23.5 us
    unnamed x26, local copies, waits for them, and re-layouts  13.5 us
    ppermute x5, starting transfers between devices, level_steps(): lax.ppermute(v, 'col', [(0, 1)])  10.7 us
  transfers between devices with their start and end apart: 57, of which 30 were waited for; matrix products, arithmetic and copies ran while one was open for 0% of the time, Pallas kernels for 25%

profile of v1, /device:TPU:0, one launch (start us, length us, event | category | flops | bytes accessed | tf_op | source)
XLA Modules:
  0.0 399.7 jit_solution(1851156374875113671)
XLA Ops:
  25.6 9.6 %collective-permute-done.6.recv_ref = f32[64,16,128]{2,1,0:T(8,128)S(1)} collective-permute-done((f32[64,16,128]{2,1,0:T(8,128)S(1)}, f32[64,16,128]{2,1,0:T(8,128)S(1)}, u32[]{:S(2)}, u32[]{:S(2)}) %collective-permute-start.6) | collective-permute-done | bytes 524320 | tf_op jit(solution)/shard_map/ppermute | solution.py:415
  36.8 23.8 %collective-permute-done.5.refs_1_ = f32[128,128]{1,0:T(8,128)S(1)} collective-permute-done((f32[128,128]{1,0:T(8,128)S(1)}, f32[128,128]{1,0:T(8,128)S(1)}, u32[]{:S(2)}, u32[]{:S(2)}) %collective-permute-start.5) | collective-permute-done | bytes 65568 | tf_op jit(solution)/shard_map/ppermute | solution.py:415
  71.8 11.1 %collective-permute-done.12.recv_ref = f32[64,16,128]{2,1,0:T(8,128)S(1)} collective-permute-done((f32[64,16,128]{2,1,0:T(8,128)S(1)}, f32[64,16,128]{2,1,0:T(8,128)S(1)}, u32[]{:S(2)}, u32[]{:S(2)}) %collective-permute-start.12) | collective-permute-done | bytes 524320 | tf_op jit(solution)/shard_map/ppermute | solution.py:415
  87.1 10.0 %shard_map.72 = (f32[64,64,128]{2,1,0:T(8,128)S(1)}, f32[64,64,128]{2,1,0:T(8,128)}) custom-call(s32[4]{0:T(128)S(1)} %pad_add_fusion._.ids_ref.refs_0_, s32[16,128]{1,0:T(8,128)S(1)} %add_add_fusion.lists_ref, f32[128,128]{1,0:T(8,128)S(1)} %shard_map.71.own_ref._, f32[128,128]{1,0:T(8,128)S(1)} %collective-permute-done.13.other_ref, ...), custom_call_target="tpu_custom_call" | custom-call | tf_op jit(solution)/shard_map/pallas_call | solution.py:37
  101.4 10.0 %shard_map.74 = (f32[64,64,128]{2,1,0:T(8,128)S(1)}, f32[64,64,128]{2,1,0:T(8,128)}) custom-call(s32[4]{0:T(128)S(1)} %pad_add_fusion._.ids_ref.refs_0_, s32[16,128]{1,0:T(8,128)S(1)} %add_add_fusion.lists_ref, f32[128,128]{1,0:T(8,128)S(1)} %shard_map.71.own_ref._, f32[128,128]{1,0:T(8,128)S(1)} %collective-permute-done.13.other_ref, ...), custom_call_target="tpu_custom_call" | custom-call | tf_op jit(solution)/shard_map/pallas_call | solution.py:37
  113.5 23.9 %collective-permute-done.15.recv_ref = f32[64,32,128]{2,1,0:T(8,128)S(1)} collective-permute-done((f32[64,32,128]{2,1,0:T(8,128)S(1)}, f32[64,32,128]{2,1,0:T(8,128)S(1)}, u32[]{:S(2)}, u32[]{:S(2)}) %collective-permute-start.15) | collective-permute-done | bytes 1048608 | tf_op jit(solution)/shard_map/ppermute | solution.py:415
  143.1 16.8 %collective-permute-done.18.recv_ref = f32[64,32,128]{2,1,0:T(8,128)S(1)} collective-permute-done((f32[64,32,128]{2,1,0:T(8,128)S(1)}, f32[64,32,128]{2,1,0:T(8,128)S(1)}, u32[]{:S(2)}, u32[]{:S(2)}) %collective-permute-start.18) | collective-permute-done | bytes 1048608 | tf_op jit(solution)/shard_map/ppermute | solution.py:415
  165.7 3.8 collective-permute-start.22
  169.6 12.7 %collective-permute-done.10.recv_ref = f32[64,32,128]{2,1,0:T(8,128)S(1)} collective-permute-done((f32[64,32,128]{2,1,0:T(8,128)S(1)}, f32[64,32,128]{2,1,0:T(8,128)S(1)}, u32[]{:S(2)}, u32[]{:S(2)}) %collective-permute-start.10) | collective-permute-done | bytes 1048608 | tf_op jit(solution)/shard_map/ppermute | solution.py:415
  185.9 7.7 %collective-permute-done.9.recv_ref = f32[64,16,128]{2,1,0:T(8,128)S(1)} collective-permute-done((f32[64,16,128]{2,1,0:T(8,128)}, f32[64,16,128]{2,1,0:T(8,128)S(1)}, u32[]{:S(2)}, u32[]{:S(2)}) %collective-permute-start.9) | collective-permute-done | bytes 524320 | tf_op jit(solution)/shard_map/ppermute | solution.py:415
  194.5 5.8 %collective-permute-start.23 = (f32[8,64,128]{2,1,0:T(8,128)S(1)}, f32[8,64,128]{2,1,0:T(8,128)S(1)}, u32[]{:S(2)}, u32[]{:S(2)}) collective-permute-start(f32[8,64,128]{2,1,0:T(8,128)S(1)} %get-tuple-element.103), channel_id=1, source_target_pairs={{0,4},{1,5},{8,12},{9,13},{16,20},{17,21},{24,28},{25,29},{32,36},... | collective-permute-start | bytes 786440 | tf_op jit(solution)/shard_map/ppermute | solution.py:418
  206.5 5.3 %collective-permute-start.30 = (f32[8,64,128]{2,1,0:T(8,128)S(1)}, f32[8,64,128]{2,1,0:T(8,128)S(1)}, u32[]{:S(2)}, u32[]{:S(2)}) collective-permute-start(f32[8,64,128]{2,1,0:T(8,128)S(1)} %get-tuple-element.113), channel_id=1, source_target_pairs={{0,4},{1,5},{8,12},{9,13},{16,20},{17,21},{24,28},{25,29},{32,36},... | collective-permute-start | bytes 786440 | tf_op jit(solution)/shard_map/ppermute | solution.py:418
  211.8 4.1 %collective-permute-done.21.recv_ref = f32[64,32,128]{2,1,0:T(8,128)S(1)} collective-permute-done((f32[64,32,128]{2,1,0:T(8,128)S(1)}, f32[64,32,128]{2,1,0:T(8,128)S(1)}, u32[]{:S(2)}, u32[]{:S(2)}) %collective-permute-start.21) | collective-permute-done | bytes 1048608 | tf_op jit(solution)/shard_map/ppermute | solution.py:415
  216.0 6.0 %collective-permute-start.31 = (f32[8,64,128]{2,1,0:T(8,128)S(1)}, f32[8,64,128]{2,1,0:T(8,128)S(1)}, u32[]{:S(2)}, u32[]{:S(2)}) collective-permute-start(f32[8,64,128]{2,1,0:T(8,128)S(1)} %get-tuple-element.114), channel_id=1, source_target_pairs={{0,6},{1,7},{8,14},{9,15},{16,22},{17,23},{24,30},{25,31},{32,38},... | collective-permute-start | bytes 786440 | tf_op jit(solution)/shard_map/ppermute | solution.py:418
  228.6 9.4 %collective-permute-done.27.recv_ref = f32[64,32,128]{2,1,0:T(8,128)S(1)} collective-permute-done((f32[64,32,128]{2,1,0:T(8,128)S(1)}, f32[64,32,128]{2,1,0:T(8,128)S(1)}, u32[]{:S(2)}, u32[]{:S(2)}) %collective-permute-start.27) | collective-permute-done | bytes 1048608 | tf_op jit(solution)/shard_map/ppermute | solution.py:415
  245.3 4.6 %collective-permute-done.26.recv_ref = f32[64,32,128]{2,1,0:T(8,128)S(1)} collective-permute-done((f32[64,32,128]{2,1,0:T(8,128)S(1)}, f32[64,32,128]{2,1,0:T(8,128)S(1)}, u32[]{:S(2)}, u32[]{:S(2)}) %collective-permute-start.26) | collective-permute-done | bytes 1048608 | tf_op jit(solution)/shard_map/ppermute | solution.py:415
  251.6 6.2 %collective-permute-done.20.recv_ref = f32[64,16,128]{2,1,0:T(8,128)S(1)} collective-permute-done((f32[64,16,128]{2,1,0:T(8,128)S(1)}, f32[64,16,128]{2,1,0:T(8,128)S(1)}, u32[]{:S(2)}, u32[]{:S(2)}) %collective-permute-start.20) | collective-permute-done | bytes 524320 | tf_op jit(solution)/shard_map/ppermute | solution.py:415
  268.3 3.7 collective-permute-done.36.refs_1_
  279.7 3.9 collective-permute-done.32.recv_ref
  293.5 4.8 %collective-permute-done.43.refs_1_ = f32[8,64,128]{2,1,0:T(8,128)S(1)} collective-permute-done((f32[8,64,128]{2,1,0:T(8,128)S(1)}, f32[8,64,128]{2,1,0:T(8,128)S(1)}, u32[]{:S(2)}, u32[]{:S(2)}) %collective-permute-start.43) | collective-permute-done | bytes 262176 | tf_op jit(solution)/shard_map/ppermute | solution.py:415
  302.1 6.4 %collective-permute-done.49.refs_2_ = f32[16,64,128]{2,1,0:T(8,128)S(1)} collective-permute-done((f32[16,64,128]{2,1,0:T(8,128)S(1)}, f32[16,64,128]{2,1,0:T(8,128)S(1)}, u32[]{:S(2)}, u32[]{:S(2)}) %collective-permute-start.49) | collective-permute-done | bytes 524320 | tf_op jit(solution)/shard_map/ppermute | solution.py:415
  308.5 4.2 %collective-permute-done.50.refs_3_ = f32[16,64,128]{2,1,0:T(8,128)S(1)} collective-permute-done((f32[16,64,128]{2,1,0:T(8,128)S(1)}, f32[16,64,128]{2,1,0:T(8,128)S(1)}, u32[]{:S(2)}, u32[]{:S(2)}) %collective-permute-start.50) | collective-permute-done | bytes 524320 | tf_op jit(solution)/shard_map/ppermute | solution.py:415
  313.1 4.4 %collective-permute-start.46 = (f32[16,64,128]{2,1,0:T(8,128)S(1)}, f32[16,64,128]{2,1,0:T(8,128)S(1)}, u32[]{:S(2)}, u32[]{:S(2)}) collective-permute-start(f32[16,64,128]{2,1,0:T(8,128)S(1)} %shard_map.101.refs_4_.refs_0_), channel_id=1, source_target_pairs={{0,4},{2,6},{4,0},{6,2},{1,5},{3,7},{5,1},{7,3},{8,12},{10,14},{12... | collective-permute-start | bytes 1572872 | tf_op jit(solution)/shard_map/ppermute | solution.py:415
  317.7 9.7 %shard_map.103.refs_4_ = f32[512,4096]{1,0:T(8,128)} custom-call(s32[4]{0:T(128)S(1)} %pad_add_fusion._.ids_ref.refs_0_, f32[512,512]{1,0:T(8,128)S(1)} %copy-done.6, f32[64,64,128]{2,1,0:T(8,128)S(1)} %shard_map.102.refs_2_.refs_4_, f32[64,64,128]{2,1,0:T(8,128)S(1)} %collective-permute-done.51.refs_3_, f32[64,64,128]{2,1,0:T(8,128)S(1)} %shard_map.102.refs_2_.refs_4_), custom_call_target="tpu_custom_call" | custom-call | tf_op jit(solution)/shard_map/pallas_call | solution.py:37
  327.8 13.3 %collective-permute-done.46.refs_2_ = f32[16,64,128]{2,1,0:T(8,128)S(1)} collective-permute-done((f32[16,64,128]{2,1,0:T(8,128)S(1)}, f32[16,64,128]{2,1,0:T(8,128)S(1)}, u32[]{:S(2)}, u32[]{:S(2)}) %collective-permute-start.46) | collective-permute-done | bytes 524320 | tf_op jit(solution)/shard_map/ppermute | solution.py:415
  347.3 5.2 %collective-permute-start.55 = (f32[4,32,512]{2,1,0:T(8,128)S(1)}, f32[4,32,512]{2,1,0:T(8,128)S(1)}, u32[]{:S(2)}, u32[]{:S(2)}) collective-permute-start(f32[4,32,512]{2,1,0:T(8,128)S(1)} %get-tuple-element.116._.cols_ref), channel_id=1, source_target_pairs={{0,1},{2,3},{4,5},{6,7},{8,9},{10,11},{12,13},{14,15},{16,17},{18,... | collective-permute-start | bytes 786440 | tf_op jit(solution)/shard_map/ppermute | solution.py:456
  358.0 12.7 %shard_map.105 = (bf16[512,4096]{1,0:T(8,128)(2,1)}, bf16[512,4096]{1,0:T(8,128)(2,1)}) custom-call(s32[4]{0:T(128)S(1)} %pad_add_fusion._.ids_ref.refs_0_, f32[512,512]{1,0:T(8,128)S(1)} %copy-done.6, f32[64,64,128]{2,1,0:T(8,128)S(1)} %shard_map.104.refs_2_.refs_5_, f32[64,64,128]{2,1,0:T(8,128)S(1)} %collective-permute-done.52.refs_3_, ...), custom_call_target="tpu_custom_call" | custom-call | tf_op jit(solution)/shard_map/pallas_call | solution.py:37
  377.6 4.5 %shard_map.106.rest_1_ = f32[4,128,4096]{2,1,0:T(8,128)} custom-call(s32[4]{0:T(128)S(1)} %pad_add_fusion._.ids_ref.refs_0_, f32[4,16,512]{2,1,0:T(8,128)S(1)} %get-tuple-element.88._.cols_ref, f32[4,16,512]{2,1,0:T(8,128)S(1)} %collective-permute-done.56.sent_ref, f32[4,16,4096]{2,1,0:T(8,128)S(1)} %copy-done.10, bf16[512,4096]{1,0:T(8,128)(2,1)S(1)} %copy-done.2, ...), custom_call_target="tpu_custom_call" | custom-call | tf_op jit(solution)/shard_map/pallas_call | solution.py:37
  382.0 4.4 %shard_map.107.rest_1_ = f32[4,128,4096]{2,1,0:T(8,128)} custom-call(s32[4]{0:T(128)S(1)} %pad_add_fusion._.ids_ref.refs_0_, f32[4,32,512]{2,1,0:T(8,128)S(1)} %get-tuple-element.116._.cols_ref, f32[4,32,512]{2,1,0:T(8,128)S(1)} %collective-permute-done.55.sent_ref, f32[4,32,4096]{2,1,0:T(8,128)S(1)} %get-tuple-element.135.front_ref, ...), custom_call_target="tpu_custom_call", output_to_operand_aliasing={{}: (7, {})} | custom-call | tf_op jit(solution)/shard_map/pallas_call | solution.py:37
  386.4 4.4 %shard_map.108.rest_1_ = f32[4,128,4096]{2,1,0:T(8,128)} custom-call(s32[4]{0:T(128)S(1)} %pad_add_fusion._.ids_ref.refs_0_, f32[4,32,512]{2,1,0:T(8,128)S(1)} %get-tuple-element.118._.cols_ref, f32[4,32,512]{2,1,0:T(8,128)S(1)} %collective-permute-done.54.sent_ref, f32[4,32,4096]{2,1,0:T(8,128)S(1)} %get-tuple-element.134.front_ref, ...), custom_call_target="tpu_custom_call", output_to_operand_aliasing={{}: (7, {})} | custom-call | tf_op jit(solution)/shard_map/pallas_call | solution.py:37
  390.9 4.4 %shard_map.109.rest_1_ = f32[4,128,4096]{2,1,0:T(8,128)} custom-call(s32[4]{0:T(128)S(1)} %pad_add_fusion._.ids_ref.refs_0_, f32[4,32,512]{2,1,0:T(8,128)S(1)} %get-tuple-element.128.refs_2_.cols_ref, f32[4,32,512]{2,1,0:T(8,128)S(1)} %collective-permute-done.53.sent_ref, ...), custom_call_target="tpu_custom_call", output_to_operand_aliasing={{}: (7, {})} | custom-call | tf_op jit(solution)/shard_map/pallas_call | solution.py:37
  395.2 4.5 %shard_map.110 = f32[4,128,4096]{2,1,0:T(8,128)} custom-call(s32[4]{0:T(128)S(1)} %pad_add_fusion._.ids_ref.refs_0_, f32[4,16,512]{2,1,0:T(8,128)S(1)} %get-tuple-element.129.refs_2_.cols_ref, f32[4,16,512]{2,1,0:T(8,128)S(1)} %collective-permute-done.41.sent_ref, f32[4,16,4096]{2,1,0:T(8,128)S(1)} %get-tuple-element.130.front_ref, ...), custom_call_target="tpu_custom_call", output_to_operand_aliasing={{}: (7, {})} | custom-call | tf_op jit(solution)/shard_map/pallas_call | solution.py:37
  (167 shorter events, 137.5 us)
Async XLA Ops:
  18.7 42.7 %collective-permute-start.4 = (f32[64,32,128]{2,1,0:T(8,128)S(1)}, f32[64,32,128]{2,1,0:T(8,128)S(1)}, u32[]{:S(2)}, u32[]{:S(2)}) collective-permute-start(f32[64,32,128]{2,1,0:T(8,128)S(1)} %shard_map.61._), channel_id=1, source_target_pairs={{0,8},{8,0},{16,24},{24,16},{32,40},{40,32},{48,56},{56,48},{64,72... | collective-permute-start | bytes 3145736 | tf_op jit(solution)/shard_map/ppermute | solution.py:415
  20.0 43.5 %collective-permute-start.3 = (f32[64,32,128]{2,1,0:T(8,128)S(1)}, f32[64,32,128]{2,1,0:T(8,128)S(1)}, u32[]{:S(2)}, u32[]{:S(2)}) collective-permute-start(f32[64,32,128]{2,1,0:T(8,128)S(1)} %shard_map.62._), channel_id=1, source_target_pairs={{0,8},{8,0},{16,24},{24,16},{32,40},{40,32},{48,56},{56,48},{64,72... | collective-permute-start | bytes 3145736 | tf_op jit(solution)/shard_map/ppermute | solution.py:415
  22.0 45.9 %collective-permute-start.8 = (f32[64,32,128]{2,1,0:T(8,128)S(1)}, f32[64,32,128]{2,1,0:T(8,128)S(1)}, u32[]{:S(2)}, u32[]{:S(2)}) collective-permute-start(f32[64,32,128]{2,1,0:T(8,128)S(1)} %get-tuple-element.72._), channel_id=1, source_target_pairs={{0,16},{8,24},{16,0},{24,8},{32,48},{40,56},{48,32},{56,40},{64,80... | collective-permute-start | bytes 3145736 | tf_op jit(solution)/shard_map/ppermute | solution.py:415
  22.5 38.1 %collective-permute-start.5 = (f32[128,128]{1,0:T(8,128)S(1)}, f32[128,128]{1,0:T(8,128)S(1)}, u32[]{:S(2)}, u32[]{:S(2)}) collective-permute-start(f32[128,128]{1,0:T(8,128)S(1)} %shard_map.59._.refs_0_), channel_id=1, source_target_pairs={{0,32},{8,40},{16,48},{24,56},{32,0},{40,8},{48,16},{56,24},{64,96... | collective-permute-start | bytes 196616 | tf_op jit(solution)/shard_map/ppermute | solution.py:415
  97.0 42.2 %collective-permute-start.14 = (f32[64,64,128]{2,1,0:T(8,128)}, f32[64,64,128]{2,1,0:T(8,128)S(1)}, u32[]{:S(2)}, u32[]{:S(2)}) collective-permute-start(f32[64,64,128]{2,1,0:T(8,128)} %get-tuple-element.85), channel_id=1, source_target_pairs={{0,8},{8,0},{16,24},{24,16},{32,40},{40,32},{48,56},{56,48},{64,72... | collective-permute-start | bytes 6291464 | tf_op jit(solution)/shard_map/ppermute | solution.py:415
  111.3 30.6 %collective-permute-start.19 = (f32[64,64,128]{2,1,0:T(8,128)}, f32[64,64,128]{2,1,0:T(8,128)S(1)}, u32[]{:S(2)}, u32[]{:S(2)}) collective-permute-start(f32[64,64,128]{2,1,0:T(8,128)} %get-tuple-element.94), channel_id=1, source_target_pairs={{0,8},{8,0},{16,24},{24,16},{32,40},{40,32},{48,56},{56,48},{64,72... | collective-permute-start | bytes 6291464 | tf_op jit(solution)/shard_map/ppermute | solution.py:415
  111.4 26.0 %collective-permute-start.15 = (f32[64,32,128]{2,1,0:T(8,128)S(1)}, f32[64,32,128]{2,1,0:T(8,128)S(1)}, u32[]{:S(2)}, u32[]{:S(2)}) collective-permute-start(f32[64,32,128]{2,1,0:T(8,128)S(1)} %get-tuple-element.75._), channel_id=1, source_target_pairs={{0,16},{8,24},{16,0},{24,8},{32,48},{40,56},{48,32},{56,40},{64,80... | collective-permute-start | bytes 3145736 | tf_op jit(solution)/shard_map/ppermute | solution.py:415
  111.7 48.2 %collective-permute-start.18 = (f32[64,32,128]{2,1,0:T(8,128)S(1)}, f32[64,32,128]{2,1,0:T(8,128)S(1)}, u32[]{:S(2)}, u32[]{:S(2)}) collective-permute-start(f32[64,32,128]{2,1,0:T(8,128)S(1)} %get-tuple-element.76._), channel_id=1, source_target_pairs={{0,16},{8,24},{16,0},{24,8},{32,48},{40,56},{48,32},{56,40},{64,80... | collective-permute-start | bytes 3145736 | tf_op jit(solution)/shard_map/ppermute | solution.py:415
  139.5 26.2 %collective-permute-start.17 = (f32[32,64,128]{2,1,0:T(8,128)S(1)}, f32[32,64,128]{2,1,0:T(8,128)S(1)}, u32[]{:S(2)}, u32[]{:S(2)}) collective-permute-start(f32[32,64,128]{2,1,0:T(8,128)S(1)} %get-tuple-element.92), channel_id=1, source_target_pairs={{0,64},{8,72},{16,80},{24,88},{32,96},{40,104},{48,112},{56,120},{... | collective-permute-start | bytes 3145736 | tf_op jit(solution)/shard_map/ppermute | solution.py:415
  141.1 41.1 %collective-permute-start.10 = (f32[64,32,128]{2,1,0:T(8,128)S(1)}, f32[64,32,128]{2,1,0:T(8,128)S(1)}, u32[]{:S(2)}, u32[]{:S(2)}) collective-permute-start(f32[64,32,128]{2,1,0:T(8,128)S(1)} %get-tuple-element.78._), channel_id=1, source_target_pairs={{0,32},{8,40},{16,48},{24,56},{32,0},{40,8},{48,16},{56,24},{64,96... | collective-permute-start | bytes 3145736 | tf_op jit(solution)/shard_map/ppermute | solution.py:415
  142.1 58.1 %collective-permute-start.25 = (f32[32,64,128]{2,1,0:T(8,128)S(1)}, f32[32,64,128]{2,1,0:T(8,128)S(1)}, u32[]{:S(2)}, u32[]{:S(2)}) collective-permute-start(f32[32,64,128]{2,1,0:T(8,128)S(1)} %get-tuple-element.105), channel_id=1, source_target_pairs={{0,64},{8,72},{16,80},{24,88},{32,96},{40,104},{48,112},{56,120},{... | collective-permute-start | bytes 3145736 | tf_op jit(solution)/shard_map/ppermute | solution.py:415
  142.7 51.0 %collective-permute-start.9 = (f32[64,16,128]{2,1,0:T(8,128)}, f32[64,16,128]{2,1,0:T(8,128)S(1)}, u32[]{:S(2)}, u32[]{:S(2)}) collective-permute-start(f32[64,16,128]{2,1,0:T(8,128)} %get-tuple-element.80._), channel_id=1, source_target_pairs={{0,16},{8,24},{16,0},{24,8},{32,48},{40,56},{48,32},{56,40},{64,80... | collective-permute-start | bytes 1572872 | tf_op jit(solution)/shard_map/ppermute | solution.py:415
  160.0 56.0 %collective-permute-start.21 = (f32[64,32,128]{2,1,0:T(8,128)S(1)}, f32[64,32,128]{2,1,0:T(8,128)S(1)}, u32[]{:S(2)}, u32[]{:S(2)}) collective-permute-start(f32[64,32,128]{2,1,0:T(8,128)S(1)} %get-tuple-element.90.refs_2_), channel_id=1, source_target_pairs={{0,32},{8,40},{16,48},{24,56},{32,0},{40,8},{48,16},{56,24},{64,96... | collective-permute-start | bytes 3145736 | tf_op jit(solution)/shard_map/ppermute | solution.py:415
  165.7 28.7 %collective-permute-start.22 = (f32[8,64,128]{2,1,0:T(8,128)S(1)}, f32[8,64,128]{2,1,0:T(8,128)S(1)}, u32[]{:S(2)}, u32[]{:S(2)}) collective-permute-start(f32[8,64,128]{2,1,0:T(8,128)S(1)} %get-tuple-element.102), channel_id=1, source_target_pairs={{0,2},{1,3},{8,10},{9,11},{16,18},{17,19},{24,26},{25,27},{32,34},... | collective-permute-start | bytes 786440 | tf_op jit(solution)/shard_map/ppermute | solution.py:418
  184.0 42.9 %collective-permute-start.28 = (f32[64,32,128]{2,1,0:T(8,128)S(1)}, f32[64,32,128]{2,1,0:T(8,128)S(1)}, u32[]{:S(2)}, u32[]{:S(2)}) collective-permute-start(f32[64,32,128]{2,1,0:T(8,128)S(1)} %get-tuple-element.98._), channel_id=1, source_target_pairs={{0,64},{8,72},{16,80},{24,88},{32,96},{40,104},{48,112},{56,120},{... | collective-permute-start | bytes 3145736 | tf_op jit(solution)/shard_map/ppermute | solution.py:415
  193.7 44.3 %collective-permute-start.27 = (f32[64,32,128]{2,1,0:T(8,128)S(1)}, f32[64,32,128]{2,1,0:T(8,128)S(1)}, u32[]{:S(2)}, u32[]{:S(2)}) collective-permute-start(f32[64,32,128]{2,1,0:T(8,128)S(1)} %get-tuple-element.96.refs_2_), channel_id=1, source_target_pairs={{0,32},{8,40},{16,48},{24,56},{32,0},{40,8},{48,16},{56,24},{64,96... | collective-permute-start | bytes 3145736 | tf_op jit(solution)/shard_map/ppermute | solution.py:415
  205.2 18.6 %collective-permute-start.29 = (f32[8,64,128]{2,1,0:T(8,128)S(1)}, f32[8,64,128]{2,1,0:T(8,128)S(1)}, u32[]{:S(2)}, u32[]{:S(2)}) collective-permute-start(f32[8,64,128]{2,1,0:T(8,128)S(1)} %get-tuple-element.112), channel_id=1, source_target_pairs={{0,2},{1,3},{8,10},{9,11},{16,18},{17,19},{24,26},{25,27},{32,34},... | collective-permute-start | bytes 786440 | tf_op jit(solution)/shard_map/ppermute | solution.py:418
  206.5 18.9 %collective-permute-start.30 = (f32[8,64,128]{2,1,0:T(8,128)S(1)}, f32[8,64,128]{2,1,0:T(8,128)S(1)}, u32[]{:S(2)}, u32[]{:S(2)}) collective-permute-start(f32[8,64,128]{2,1,0:T(8,128)S(1)} %get-tuple-element.113), channel_id=1, source_target_pairs={{0,4},{1,5},{8,12},{9,13},{16,20},{17,21},{24,28},{25,29},{32,36},... | collective-permute-start | bytes 786440 | tf_op jit(solution)/shard_map/ppermute | solution.py:418
  223.8 26.2 %collective-permute-start.26 = (f32[64,32,128]{2,1,0:T(8,128)S(1)}, f32[64,32,128]{2,1,0:T(8,128)S(1)}, u32[]{:S(2)}, u32[]{:S(2)}) collective-permute-start(f32[64,32,128]{2,1,0:T(8,128)S(1)} %get-tuple-element.109.refs_4_), channel_id=1, source_target_pairs={{0,64},{8,72},{16,80},{24,88},{32,96},{40,104},{48,112},{56,120},{... | collective-permute-start | bytes 3145736 | tf_op jit(solution)/shard_map/ppermute | solution.py:415
  239.7 34.5 %collective-permute-start.40 = (f32[64,32,128]{2,1,0:T(8,128)S(1)}, f32[64,32,128]{2,1,0:T(8,128)S(1)}, u32[]{:S(2)}, u32[]{:S(2)}) collective-permute-start(f32[64,32,128]{2,1,0:T(8,128)S(1)} %get-tuple-element.117._), channel_id=1, source_target_pairs={{0,64},{8,72},{16,80},{24,88},{32,96},{40,104},{48,112},{56,120},{... | collective-permute-start | bytes 3145736 | tf_op jit(solution)/shard_map/ppermute | solution.py:415
  243.3 17.1 %collective-permute-start.33 = (f32[4,64,128]{2,1,0:T(8,128)S(1)}, f32[4,64,128]{2,1,0:T(8,128)S(1)}, u32[]{:S(2)}, u32[]{:S(2)}) collective-permute-start(f32[4,64,128]{2,1,0:T(8,128)S(1)} %get-tuple-element.121), channel_id=1, source_target_pairs={{0,16},{8,24},{16,0},{24,8},{32,48},{40,56},{48,32},{56,40},{64,80... | collective-permute-start | bytes 393224 | tf_op jit(solution)/shard_map/ppermute | solution.py:415
  245.1 17.6 %collective-permute-start.35 = (f32[4,64,128]{2,1,0:T(8,128)S(1)}, f32[4,64,128]{2,1,0:T(8,128)S(1)}, u32[]{:S(2)}, u32[]{:S(2)}) collective-permute-start(f32[4,64,128]{2,1,0:T(8,128)S(1)} %get-tuple-element.124), channel_id=1, source_target_pairs={{0,16},{8,24},{16,0},{24,8},{32,48},{40,56},{48,32},{56,40},{64,80... | collective-permute-start | bytes 393224 | tf_op jit(solution)/shard_map/ppermute | solution.py:415
  262.2 21.4 %collective-permute-start.32 = (f32[64,16,128]{2,1,0:T(8,128)S(1)}, f32[64,16,128]{2,1,0:T(8,128)S(1)}, u32[]{:S(2)}, u32[]{:S(2)}) collective-permute-start(f32[64,16,128]{2,1,0:T(8,128)S(1)} %get-tuple-element.120.refs_2_), channel_id=1, source_target_pairs={{0,64},{8,72},{16,80},{24,88},{32,96},{40,104},{48,112},{56,120},{... | collective-permute-start | bytes 1572872 | tf_op jit(solution)/shard_map/ppermute | solution.py:415
  287.3 21.2 %collective-permute-start.49 = (f32[16,64,128]{2,1,0:T(8,128)S(1)}, f32[16,64,128]{2,1,0:T(8,128)S(1)}, u32[]{:S(2)}, u32[]{:S(2)}) collective-permute-start(f32[16,64,128]{2,1,0:T(8,128)S(1)} %shard_map.100.refs_2_.refs_0_), channel_id=1, source_target_pairs={{0,4},{2,6},{4,0},{6,2},{1,5},{3,7},{5,1},{7,3},{8,12},{10,14},{12... | collective-permute-start | bytes 1572872 | tf_op jit(solution)/shard_map/ppermute | solution.py:415
  290.5 22.1 %collective-permute-start.50 = (f32[16,64,128]{2,1,0:T(8,128)S(1)}, f32[16,64,128]{2,1,0:T(8,128)S(1)}, u32[]{:S(2)}, u32[]{:S(2)}) collective-permute-start(f32[16,64,128]{2,1,0:T(8,128)S(1)} %shard_map.100.refs_2_.refs_0_), channel_id=1, source_target_pairs={{0,6},{2,4},{4,2},{6,0},{1,7},{3,5},{5,3},{7,1},{8,14},{10,12},{12... | collective-permute-start | bytes 1572872 | tf_op jit(solution)/shard_map/ppermute | solution.py:415
  313.1 28.0 %collective-permute-start.46 = (f32[16,64,128]{2,1,0:T(8,128)S(1)}, f32[16,64,128]{2,1,0:T(8,128)S(1)}, u32[]{:S(2)}, u32[]{:S(2)}) collective-permute-start(f32[16,64,128]{2,1,0:T(8,128)S(1)} %shard_map.101.refs_4_.refs_0_), channel_id=1, source_target_pairs={{0,4},{2,6},{4,0},{6,2},{1,5},{3,7},{5,1},{7,3},{8,12},{10,14},{12... | collective-permute-start | bytes 1572872 | tf_op jit(solution)/shard_map/ppermute | solution.py:415
  317.5 26.1 %collective-permute-start.47 = (f32[16,64,128]{2,1,0:T(8,128)S(1)}, f32[16,64,128]{2,1,0:T(8,128)S(1)}, u32[]{:S(2)}, u32[]{:S(2)}) collective-permute-start(f32[16,64,128]{2,1,0:T(8,128)S(1)} %shard_map.101.refs_4_.refs_0_), channel_id=1, source_target_pairs={{0,6},{2,4},{4,2},{6,0},{1,7},{3,5},{5,3},{7,1},{8,14},{10,12},{12... | collective-permute-start | bytes 1572872 | tf_op jit(solution)/shard_map/ppermute | solution.py:415
  347.3 34.8 %collective-permute-start.55 = (f32[4,32,512]{2,1,0:T(8,128)S(1)}, f32[4,32,512]{2,1,0:T(8,128)S(1)}, u32[]{:S(2)}, u32[]{:S(2)}) collective-permute-start(f32[4,32,512]{2,1,0:T(8,128)S(1)} %get-tuple-element.116._.cols_ref), channel_id=1, source_target_pairs={{0,1},{2,3},{4,5},{6,7},{8,9},{10,11},{12,13},{14,15},{16,17},{18,... | collective-permute-start | bytes 786440 | tf_op jit(solution)/shard_map/ppermute | solution.py:456
  352.5 33.9 %collective-permute-start.54 = (f32[4,32,512]{2,1,0:T(8,128)S(1)}, f32[4,32,512]{2,1,0:T(8,128)S(1)}, u32[]{:S(2)}, u32[]{:S(2)}) collective-permute-start(f32[4,32,512]{2,1,0:T(8,128)S(1)} %get-tuple-element.118._.cols_ref), channel_id=1, source_target_pairs={{0,1},{2,3},{4,5},{6,7},{8,9},{10,11},{12,13},{14,15},{16,17},{18,... | collective-permute-start | bytes 786440 | tf_op jit(solution)/shard_map/ppermute | solution.py:456
  353.8 37.0 %collective-permute-start.53 = (f32[4,32,512]{2,1,0:T(8,128)S(1)}, f32[4,32,512]{2,1,0:T(8,128)S(1)}, u32[]{:S(2)}, u32[]{:S(2)}) collective-permute-start(f32[4,32,512]{2,1,0:T(8,128)S(1)} %get-tuple-element.128.refs_2_.cols_ref), channel_id=1, source_target_pairs={{0,1},{2,3},{4,5},{6,7},{8,9},{10,11},{12,13},{14,15},{16,17},{18,... | collective-permute-start | bytes 786440 | tf_op jit(solution)/shard_map/ppermute | solution.py:456
  355.2 18.0 %collective-permute-start.56 = (f32[4,16,512]{2,1,0:T(8,128)S(1)}, f32[4,16,512]{2,1,0:T(8,128)S(1)}, u32[]{:S(2)}, u32[]{:S(2)}) collective-permute-start(f32[4,16,512]{2,1,0:T(8,128)S(1)} %get-tuple-element.88._.cols_ref), channel_id=1, source_target_pairs={{0,1},{2,3},{4,5},{6,7},{8,9},{10,11},{12,13},{14,15},{16,17},{18,... | collective-permute-start | bytes 393224 | tf_op jit(solution)/shard_map/ppermute | solution.py:456
  356.5 38.8 %collective-permute-start.41 = (f32[4,16,512]{2,1,0:T(8,128)S(1)}, f32[4,16,512]{2,1,0:T(8,128)S(1)}, u32[]{:S(2)}, u32[]{:S(2)}) collective-permute-start(f32[4,16,512]{2,1,0:T(8,128)S(1)} %get-tuple-element.129.refs_2_.cols_ref), channel_id=1, source_target_pairs={{0,1},{2,3},{4,5},{6,7},{8,9},{10,11},{12,13},{14,15},{16,17},{18,... | collective-permute-start | bytes 393224 | tf_op jit(solution)/shard_map/ppermute | solution.py:456
  (38 other events, 299.6 us)

commit v2 on v1

v2 whole, which is shorter than its diff:
```python
import jax
import jax.numpy as jnp
from jax import lax
from jax.experimental import pallas as pl
from jax.experimental.pallas import tpu as pltpu
from jax.sharding import PartitionSpec as P

TB = 128
KR = 4
KC = 32
PW = 512
K = 128
HALF = 64
LEVELS = 4
F32 = jnp.float32
BF16 = jnp.bfloat16

GROUPS = ((0, 24, 4), (96, 16, 2))
CALLS = (1, 1)
ORDER = (
    "l0", "c0k0", "c72k0", "l1", "c0k1", "l2", "c72k1", "c48k0", "l3", "weight", "q0t", "q1t", "c72k2", "c48k1",
    "q0a", "c24k0", "c0k2", "c96k0", "q1a", "c48k2", "q0b", "c24k1", "q0c", "q0d", "c112k0", "c0k3", "q1b", "c96k1",
    "q0e", "q1c", "q0h", "q1d", "c24k2", "c96k2", "c0k4", "q1e", "c112k1", "q1h", "c24k3", "c48k3", "q0low",
    "c24k4", "c72k3", "inv", "q1low", "c48k4", "c112k2", "c96k3", "q0m", "c72k4", "c112k3", "q1m", "c96k4",
    "c112k4", "u0", "u1",
)
WORK = {
    "c0k1": 0.2, "c0k2": 0.8, "c0k4": 0.8, "l0": 0.2, "l1": 0.8, "l2": 0.05, "weight": 0.05, "c24k0": 0.1, "c24k1":
    0.1, "c24k2": 0.8, "c24k3": 0.8, "c24k4": 0.1, "c48k0": 0.1, "c48k1": 0.8, "c48k2": 0.4, "c48k3": 0.05, "c72k0":
    0.1, "c72k1": 0.4, "c72k2": 0.8, "c72k3": 0.8, "c96k0": 0.8, "c96k1": 0.2, "c96k2": 0.2, "c96k3": 0.8, "c96k4":
    0.4, "c112k1": 0.2, "c112k3": 0.8, "c112k4": 0.1, "q0a": 0.8, "q0b": 0.8, "q0d": 0.2, "q0e": 0.02, "q0m": 0.8,
    "q1a": 0.05, "q1b": 0.1, "q1d": 0.05, "q1e": 0.4, "q1h": 0.05, "q1low": 0.8, "q1m": 0.4, "inv": 0.8,
}
PARTS = ((0, 64), (64, 64))

ANY = pl.BlockSpec(memory_space=pl.ANY)
HBM = pl.BlockSpec(memory_space=pltpu.HBM)
SMEM = pl.BlockSpec(memory_space=pltpu.SMEM)
VMEM = pl.BlockSpec(memory_space=pltpu.VMEM)
DMA = pltpu.SemaphoreType.DMA


def nt(a, b):
    return lax.dot_general(a, b, (((1,), (1,)), ((), ())), preferred_element_type=F32)


def split2(x):
    high = x.astype(BF16)
    return high, (x - high.astype(F32)).astype(BF16)


FLOPS = [0]


def run(body, ins, outs, scratch, limit=32, **more):
    return pl.pallas_call(
        body,
        in_specs=[s for _, s in ins],
        out_specs=[ANY if s is HBM else s for _, _, s in outs],
        out_shape=[pltpu.HBM(s, d) if spec is HBM else jax.ShapeDtypeStruct(s, d) for s, d, spec in outs],
        scratch_shapes=scratch,
        compiler_params=pltpu.CompilerParams(vmem_limit_bytes=limit << 20),
        cost_estimate=pl.CostEstimate(flops=FLOPS[0], bytes_accessed=0, transcendentals=0),
        **more,
    )(*[a for a, _ in ins])


def first_split(row, rows, tiles, split, tok):
    def body(split_ref, tiles_ref, _, send_ref, keep_ref, pool, buf, sem):
        get = pltpu.make_async_copy(tiles_ref.at[:, pl.ds(row, rows), :], pool, sem.at[0])
        get.start()
        get.wait()

        def step(i, c):
            buf[i] = pool[split_ref[0, i]]
            return c

        lax.fori_loop(0, HALF, step, 0, unroll=8)
        one = pltpu.make_async_copy(buf.at[pl.ds(0, HALF)], send_ref, sem.at[1])
        one.start()
        lax.fori_loop(HALF, K, step, 0, unroll=8)
        two = pltpu.make_async_copy(buf.at[pl.ds(HALF, HALF)], keep_ref, sem.at[2])
        two.start()
        one.wait()
        two.wait()

    return run(
        body,
        [(split, SMEM), (tiles, ANY), (tok, ANY)],
        [((HALF, rows, TB), F32, ANY)] * 2,
        [pltpu.VMEM((K, rows, TB), F32), pltpu.VMEM((K, rows, TB), F32), DMA((3,))],
    )


def fetch(kept_ref, recv_ref, pool, sem):
    one = pltpu.make_async_copy(kept_ref, pool.at[pl.ds(0, HALF)], sem.at[0])
    two = pltpu.make_async_copy(recv_ref, pool.at[pl.ds(HALF, HALF)], sem.at[1])
    one.start()
    two.start()
    one.wait()
    two.wait()


def next_level(level, rows, kept, recv, split, first, second, tok):
    def body(split_ref, first_ref, second_ref, kept_ref, recv_ref, _, send_ref, keep_ref, pool, buf, sem):
        fetch(kept_ref, recv_ref, pool, sem)

        def step(i, c):
            t = split_ref[level + 1, i]
            buf[i] = pool[first_ref[level, t]] + pool[second_ref[level, t]]
            return c

        lax.fori_loop(0, HALF, step, 0, unroll=8)
        one = pltpu.make_async_copy(buf.at[pl.ds(0, HALF)], send_ref, sem.at[2])
        one.start()
        lax.fori_loop(HALF, K, step, 0, unroll=8)
        two = pltpu.make_async_copy(buf.at[pl.ds(HALF, HALF)], keep_ref, sem.at[3])
        two.start()
        one.wait()
        two.wait()

    return run(
        body,
        [(split, SMEM), (first, SMEM), (second, SMEM), (kept, ANY), (recv, ANY), (tok, ANY)],
        [((HALF, rows, TB), F32, ANY)] * 2,
        [pltpu.VMEM((K, rows, TB), F32), pltpu.VMEM((K, rows, TB), F32), DMA((4,))],
    )


def last_level(index, count, rows, kept, recv, first, second, before, tok):
    def body(first_ref, second_ref, kept_ref, recv_ref, *refs):
        cols_ref, front_ref, pool, buf, cbuf, sem = refs[-6:]
        level = LEVELS - 1
        fetch(kept_ref, recv_ref, pool, sem)
        for i in range(KR):
            for j in range(PW // TB):
                t = i * KC + j
                tile = pool[first_ref[level, t]] + pool[second_ref[level, t]]
                buf[i, :, j * TB:(j + 1) * TB] = tile
                cbuf[i, :, j * TB:(j + 1) * TB] = tile
        one = pltpu.make_async_copy(cbuf, cols_ref.at[index], sem.at[2])
        one.start()
        for i in range(KR):

            def step(j, c):
                t = i * KC + j
                at = pl.ds(pl.multiple_of(j * TB, TB), TB)
                buf[i, :, at] = pool[first_ref[level, t]] + pool[second_ref[level, t]]
                return c

            lax.fori_loop(PW // TB, KC, step, 0, unroll=4)
        two = pltpu.make_async_copy(buf, front_ref, sem.at[3])
        two.start()
        one.wait()
        two.wait()

    ins = [(first, SMEM), (second, SMEM), (kept, ANY), (recv, ANY), (tok, ANY)]
    more = {}
    if before is not None:
        ins.append((before, ANY))
        more["input_output_aliases"] = {len(ins) - 1: 0}
    return run(
        body,
        ins,
        [((count, KR, rows, PW), F32, ANY), ((KR, rows, KC * TB), F32, HBM)],
        [
            pltpu.VMEM((K, rows, TB), F32),
            pltpu.VMEM((KR, rows, KC * TB), F32),
            pltpu.VMEM((KR, rows, PW), F32),
            DMA((4,)),
        ],
        **more,
    )


def flips(bits):
    return ((bits >> 1) & 1) + ((bits >> 2) & 1) * 2 + ((bits >> 3) & 1) * 4 + (bits & 1) * 8


def own_lists(split, first, second, tok):
    def body(split_ref, first_ref, second_ref, _, out_ref):
        out_ref[0, 0:4, :] = split_ref[...]
        out_ref[0, 4:8, :] = first_ref[...]
        out_ref[0, 8:12, :] = second_ref[...]
        order = split_ref[...]
        out_ref[0, 12:16, :] = jnp.concatenate([order[:, HALF:], order[:, :HALF]], axis=1)

    return run(body, [(split, VMEM), (first, VMEM), (second, VMEM), (tok, ANY)], [((1, 16, K), jnp.int32, VMEM)], [])


def weights(ids, near, far, tok):
    def body(ids_ref, near_ref, far_ref, _, out_ref, lists_ref):
        lists_ref[0:8] = near_ref[...]
        lists_ref[8:16] = far_ref[...]
        cube = ids_ref[0]
        row = lax.broadcasted_iota(jnp.int32, (K, K), 0)
        lane = lax.broadcasted_iota(jnp.int32, (K, K), 1)
        mine = jnp.logical_and(lane == jnp.bitwise_xor(row, ids_ref[3]), ids_ref[1] == 0)
        weight = jnp.where(mine, 1.0, 0.0).astype(BF16)
        for level in range(LEVELS - 1, -1, -1):
            parent = lists_ref[flips(cube & ((2 << level) - 1))]
            child = lists_ref[flips(cube & ((1 << level) - 1))]
            one = jnp.where(row == parent[4 + level:5 + level, :], 1.0, 0.0)
            two = jnp.where(row == parent[8 + level:9 + level, :], 1.0, 0.0)
            joined = nt(weight, (one + two).astype(BF16))
            bit = (cube >> level) & 1
            joined = jnp.where((lane >> 6) == bit, joined, 0.0).astype(BF16)
            order = jnp.where(row == child[12 + level:13 + level, :], 1.0, 0.0).astype(BF16)
            weight = nt(joined, order).astype(BF16)
        out_ref[...] = weight.astype(F32)

    return run(
        body,
        [(ids, SMEM), (near, VMEM), (far, VMEM), (tok, ANY)],
        [((K, K), F32, VMEM)],
        [pltpu.VMEM((16, 16, K), jnp.int32)],
    )


def parts_of(row, rows, weight, tiles, tok):
    def body(weight_ref, tiles_ref, _, keep_ref, send_ref, pool, buf, sem):
        get = pltpu.make_async_copy(tiles_ref.at[:, pl.ds(row, rows), :], pool, sem.at[0])
        get.start()
        w = weight_ref[...].astype(BF16)
        w = jnp.concatenate([w, w], axis=1)
        get.wait()
        flat = pool.reshape(K * rows, TB)
        out = buf.reshape(K * rows, TB)

        def step(n, carry):
            at = n * 2
            x = jnp.concatenate(
                [flat[pl.ds(at, K, stride=rows), :], flat[pl.ds(at + 1, K, stride=rows), :]], axis=1
            )
            y = jnp.dot(w, jnp.concatenate(split2(x), axis=0), preferred_element_type=F32)
            out[pl.ds(at, K, stride=rows), :] = y[:, :TB]
            out[pl.ds(at + 1, K, stride=rows), :] = y[:, TB:]
            return carry

        lax.fori_loop(0, rows // 2, step, 0, unroll=4)
        one = pltpu.make_async_copy(buf.at[pl.ds(0, HALF)], keep_ref, sem.at[1])
        two = pltpu.make_async_copy(buf.at[pl.ds(HALF, HALF)], send_ref, sem.at[2])
        one.start()
        two.start()
        one.wait()
        two.wait()

    return run(
        body,
        [(weight, VMEM), (tiles, ANY), (tok, ANY)],
        [((HALF, rows, TB), F32, ANY)] * 2,
        [pltpu.VMEM((K, rows, TB), F32), pltpu.VMEM((K, rows, TB), F32), DMA((3,))],
    )


def add_cut(terms, cuts, rows, tok):
    def body(*refs):
        total = refs[0][...]
        for term in refs[1:len(terms)]:
            total = total + term[...]
        at = 0
        for cut, ref in zip(cuts, refs[len(terms) + 1:]):
            ref[...] = total[at:at + cut]
            at += cut

    return run(
        body, [(t, VMEM) for t in terms] + [(tok, ANY)], [((cut, rows, TB), F32, VMEM) for cut in cuts], []
    )


def lay(pieces, rows, tok):
    count = sum(p.shape[0] for p in pieces)

    def body(*refs):
        out_ref, sem = refs[-2:]
        copies = []
        at = 0
        for n, piece in enumerate(pieces):
            copies.append(
                pltpu.make_async_copy(refs[n], out_ref.at[pl.ds(at, piece.shape[0])], sem.at[n])
            )
            at += piece.shape[0]
        for copy in copies:
            copy.start()
        for copy in copies:
            copy.wait()

    return run(
        body, [(p, ANY) for p in pieces] + [(tok, ANY)], [((count, rows, TB), pieces[0].dtype, ANY)], [DMA((len(pieces),))]
    )


def prepare(rows, low, high, ids, tok):
    def body(ids_ref, low_ref, high_ref, _, top_ref, rest_ref, pool, sem):
        one = pltpu.make_async_copy(low_ref, pool.at[pl.ds(0, HALF)], sem.at[0])
        two = pltpu.make_async_copy(high_ref, pool.at[pl.ds(HALF, HALF)], sem.at[1])
        one.start()
        two.start()
        mask = ids_ref[4]
        one.wait()
        two.wait()
        for i in range(KR):

            def step(j, c):
                at = pl.ds(pl.multiple_of(j * TB, TB), TB)
                h, lo = split2(pool[jnp.bitwise_xor(i * KC + j, mask)])
                top_ref[i * rows:(i + 1) * rows, at] = h
                rest_ref[i * rows:(i + 1) * rows, at] = lo
                return c

            lax.fori_loop(0, KC, step, 0, unroll=4)

    return run(
        body,
        [(ids, SMEM), (low, ANY), (high, ANY), (tok, ANY)],
        [((KR * rows, KC * TB), BF16, VMEM)] * 2,
        [pltpu.VMEM((K, rows, TB), F32), DMA((2,))],
    )


def arrange(inverse, tok):
    def body(inv_ref, _, top_ref, rest_ref):
        pieces = [inv_ref[:, i * TB + row:i * TB + row + n] for row, n in PARTS for i in range(KR)]
        top_ref[...], rest_ref[...] = split2(jnp.concatenate(pieces, axis=1))

    return run(body, [(inverse, VMEM), (tok, ANY)], [((PW, PW), BF16, VMEM)] * 2, [])


def update(groups, cols, sent, fronts, ids, inverse, pivots, out, tok):
    width = 512
    chunks = [(top + n * rows, rows) for top, rows, count in groups for n in range(count)]
    first = chunks[0][0]
    tall = sum(rows for _, rows in chunks)
    m = KR * tall
    at_pivots = 4 + 2 * len(groups)
    at_fronts = at_pivots + len(pivots)

    def body(ids_ref, inv_ref, low_ref, *refs):
        out_ref, left = refs[-2:]
        refs = (ids_ref, inv_ref, low_ref, None) + refs

        @pl.when(pl.program_id(0) == 0)
        def _():
            at = 0
            for n, (_, rows, count) in enumerate(groups):
                size = KR * rows * count
                own, other = refs[4 + 2 * n], refs[5 + 2 * n]
                h, lo = split2(jnp.where(ids_ref[2] == 0, own[...], other[...]).reshape(size, PW))
                both = jnp.dot(jnp.concatenate([h, lo], axis=0), inv_ref[...], preferred_element_type=F32)
                total = both[:size] + both[size:] + jnp.dot(h, low_ref[...], preferred_element_type=F32)
                left[at:at + size, :], left[m + at:m + at + size, :] = split2(total)
                at += size

        at, total = 0, 0.0
        for n, (_, size) in enumerate(PARTS):
            h = left[:, at:at + KR * size]
            both = jnp.dot(h, refs[at_pivots + 2 * n][...], preferred_element_type=F32)
            total += both[:m] + both[m:] + jnp.dot(h[:m], refs[at_pivots + 2 * n + 1][...], preferred_element_type=F32)
            at += KR * size
        at = 0
        for n, (row, rows) in enumerate(chunks):
            one = total[at:at + KR * rows].reshape(KR, rows, width)
            out_ref[:, row - first:row - first + rows, :] = refs[at_fronts + n][...] - one
            at += KR * rows

    square = pl.BlockSpec((PW, PW), lambda n: (0, 0))
    ins = [(ids, SMEM), (inverse[0], square), (inverse[1], square)]
    for (_, rows, count), own, other in zip(groups, cols, sent):
        pivot = pl.BlockSpec((count, KR, rows, PW), lambda n: (0, 0, 0, 0))
        ins += [(own, pivot), (other, pivot)]
    ins += [(p, pl.BlockSpec((p.shape[0], width), lambda n: (0, n))) for p in pivots]
    ins += [(f, pl.BlockSpec((KR, f.shape[1], width), lambda n: (0, 0, n))) for f in fronts]
    ins.append((tok, ANY))
    more = {}
    if out is not None:
        ins.append((out, ANY))
        more["input_output_aliases"] = {len(ins) - 1: 0}
    return run(
        body,
        ins,
        [((KR, TB, KC * TB), F32, pl.BlockSpec((KR, tall, width), lambda n: (0, first // tall, n)))],
        [pltpu.VMEM((2 * m, PW), BF16)],
        limit=56,
        grid=(KC * TB // width,),
        **more,
    )


class Plan:
    def __init__(self):
        self.steps = []
        self.log = []

    def kernel(self, name, need, give, cost, call):
        self.steps.append((name, "kernel", need, give, cost, call))

    def permute(self, name, need, give, links, cost, call):
        self.steps.append((name, "permute", [need], [give], (links, cost), call))

    def emit(self):
        kernels = {s[0]: s for s in self.steps if s[1] == "kernel"}
        names = ORDER or [s[0] for s in self.order() if s[1] == "kernel"]
        for name in names:
            yield kernels[name]
            for s in self.steps:
                if s[1] == "permute" and s[2][0] in kernels[name][3]:
                    yield s

    def order(self, limit=5):
        ready, links, flying = {}, {}, set()
        todo = [s for s in self.steps if s[1] == "kernel"]
        moves = {}
        for s in self.steps:
            if s[1] == "permute":
                moves.setdefault(s[2][0], []).append(s)
        at, result = 0.0, []
        while todo:
            known = [s for s in todo if all(n in ready for n in s[2])]
            fits = [
                s for s in known
                if len(flying - set(s[2])) + sum(len(moves.get(n, ())) for n in s[3]) <= limit
            ] or known
            best = min(fits, key=lambda s: (max([at] + [ready[n] for n in s[2]]), todo.index(s)))
            todo.remove(best)
            at = max([at] + [ready[n] for n in best[2]]) + best[4]
            self.log.append((round(at, 1), best[0]))
            result.append(best)
            flying -= set(best[2])
            for n in best[3]:
                ready[n] = at
                for m in moves.get(n, ()):
                    names, cost = m[4]
                    at += 1.5
                    begin = max([at] + [links.get(x, 0.0) for x in names])
                    for x in names:
                        links[x] = begin + cost
                    ready[m[3][0]] = begin + cost + 2.0
                    flying.add(m[3][0])
                    result.append(m)
        self.end = at
        return result


def flip(axis, bits):
    return lambda v: lax.ppermute(v, axis, [(i, i ^ bits) for i in range(lax.axis_size(axis))])


def make_plan(tiles, split, first, second, ids, pivot_inverse):
    level_links = (("core",), ("xa",), ("xa", "xb"), ("y",))
    link_time = (3.5, 22.8, 22.8, 22.8)
    plan = Plan()
    kernel, permute = plan.kernel, plan.permute

    def level_steps(group, index):
        top, rows, count = group
        row = top + index * rows
        n, g = f"c{row}", f"g{top}"
        share = rows / 32
        kernel(f"{n}k0", [], [f"{n}s0", f"{n}h0"], 0.6 + 0.4 * share, lambda v, tok: first_split(row, rows, tiles, split, tok))
        for level in range(LEVELS):
            permute(f"{n}p{level}", f"{n}s{level}", f"{n}r{level}", level_links[level], link_time[level] * share, flip("cube", 1 << level))
            need = [f"{n}r{level}", f"{n}h{level}"]
            if level < LEVELS - 1:
                kernel(
                    f"{n}k{level + 1}",
                    need,
                    [f"{n}s{level + 1}", f"{n}h{level + 1}"],
                    0.8 + 0.9 * share,
                    lambda v, tok, level=level: next_level(
                        level, rows, v[f"{n}h{level}"], v[f"{n}r{level}"], split, first, second, tok
                    ),
                )
            else:
                kernel(
                    f"{n}k4",
                    need + ([f"{g}cols{index - 1}"] if index else []),
                    [f"{g}cols{index}", f"{n}front"],
                    0.8 + 0.9 * share,
                    lambda v, tok: last_level(
                        index, count, rows, v[f"{n}h3"], v[f"{n}r3"], first, second, v.get(f"{g}cols{index - 1}"), tok
                    ),
                )
        if index == count - 1:
            permute(
                f"{g}pc", f"{g}cols{index}", f"{g}sent", ("y2",), 5.7 * share * count,
                lambda v: lax.ppermute(v, "col", [(0, 1)]),
            )

    def part_steps(index, row, rows):
        n = f"q{index}"
        m = rows / 128

        def add(name, terms, cuts, cost):
            kernel(
                f"{n}{name}", [f"{n}{t}" for t in terms], [f"{n}{name}{i}" for i in range(len(cuts))], cost,
                lambda v, tok: add_cut([v[f"{n}{t}"] for t in terms], cuts, rows, tok),
            )

        def move(name, what, axis, bits, links, cost):
            permute(f"{n}{name}", f"{n}{what}", f"{n}{name}", links, cost, flip(axis, bits))

        def join(name, pieces, cost):
            kernel(f"{n}{name}", [f"{n}{p}" for p in pieces], [f"{n}{name}"], cost, lambda v, tok: lay([v[f"{n}{p}"] for p in pieces], rows, tok))

        kernel(f"{n}t", ["weight"], [f"{n}keep", f"{n}send"], 2 + 6 * m, lambda v, tok: parts_of(row, rows, v["weight"], tiles, tok))
        move("core", "send", "cube", 1, ("core",), 7 * m)
        add("a", ["keep", "core"], (64,), 0.5 + 2 * m)
        permute(f"{n}zs", f"{n}a0", f"{n}zs", ("gather",), 16 + 30 * m, lambda v: lax.psum_scatter(v, "row", tiled=True))
        add("b", ["zs"], (8, 8), 0.5 + m)
        move("y", "b1", "cube", 8, ("y",), 11.4 * m)
        add("c", ["b0", "y"], (8,), 0.5)
        move("xa", "c0", "cube", 2, ("xa",), 11.4 * m)
        add("d", ["c0", "xa"], (8,), 0.5)
        move("xb", "d0", "cube", 6, ("xb",), 11.4 * m)
        add("e", ["d0", "xb"], (8,), 0.5)
        move("gy", "e0", "cube", 8, ("y",), 11.4 * m)
        join("h", ["e0", "gy"], 1)
        permute(f"{n}gz", f"{n}h", f"{n}gz", ("gather",), 16 + 30 * m, lambda v: lax.all_gather(v, "row", tiled=True))
        join("low", ["gz"], 1 + 2 * m)
        move("high", "low", "cube", 1, ("core",), 7 * m)
        kernel(f"{n}m", [f"{n}low", f"{n}high"], [f"{n}m0", f"{n}m1"], 4, lambda v, tok: prepare(rows, v[f"{n}low"], v[f"{n}high"], ids, tok))

    level_steps(GROUPS[0], 0)
    kernel("l0", [], ["ls0"], 0.6, lambda v, tok: own_lists(split, first, second, tok))
    for n, bits in enumerate((2, 4, 8, 1)):
        permute(f"lp{n}", f"ls{n}", f"lr{n}", level_links[(1, 2, 3, 0)[n]], 0.2, flip("cube", bits))
        if n < 3:
            kernel(f"l{n + 1}", [f"ls{n}", f"lr{n}"], [f"ls{n + 1}"], 0.5, lambda v, tok, n=n: lay([v[f"ls{n}"], v[f"lr{n}"]], 16, tok))
    kernel("weight", ["ls3", "lr3"], ["weight"], 1.5, lambda v, tok: weights(ids, v["ls3"], v["lr3"], tok))
    for group in GROUPS:
        for index in range(group[2]):
            if group is not GROUPS[0] or index:
                level_steps(group, index)
    for index, part in enumerate(PARTS):
        part_steps(index, *part)
    kernel("inv", [], ["inv0", "inv1"], 2, lambda v, tok: arrange(pivot_inverse, tok))
    pivots = [f"q{i}m{j}" for i in range(len(PARTS)) for j in range(2)]
    start = 0
    for at, number in enumerate(CALLS):
        groups = GROUPS[start:start + number]
        start += number
        cols = [f"g{top}cols{count - 1}" for top, rows, count in groups]
        sent = [f"g{top}sent" for top, rows, count in groups]
        fronts = [f"c{top + n * rows}front" for top, rows, count in groups for n in range(count)]
        kernel(
            f"u{at}", fronts + cols + sent + pivots + ["inv0", "inv1"] + ([f"out{at - 1}"] if at else []), [f"out{at}"], 8,
            lambda v, tok, at=at, groups=groups, names=(cols, sent, fronts): update(
                groups, *[[v[n] for n in x] for x in names], ids, (v["inv0"], v["inv1"]), [v[p] for p in pivots], v.get(f"out{at - 1}"), tok
            ),
        )

    return plan


def body(update_tiles, split_order, first_source, second_source, pivot_inverse):
    tiles = pltpu.with_memory_space_constraint(update_tiles.reshape(K, TB, TB), pltpu.HBM)
    split, first, second = (x.reshape(LEVELS, K) for x in (split_order, first_source, second_source))
    cube, row_at, col = lax.axis_index("cube"), lax.axis_index("row"), lax.axis_index("col")
    mask = (cube & 1) * 64 + row_at * 16 + (cube >> 3) * 8
    ids = jnp.stack([cube, row_at, col, mask, mask - row_at * 16]).astype(jnp.int32)
    plan = make_plan(tiles, split, first, second, ids, pivot_inverse)
    values = {}
    tok = ids
    for name, kind, need, give, cost, call in plan.emit():
        if kind == "kernel":
            FLOPS[0] = int(WORK.get(name, 0) * 2.2e10)
            with jax.named_scope(name):
                results = call(values, tok)
            if not give[0].startswith("out"):
                tok = results[0]
            values.update(zip(give, results))
        else:
            with jax.named_scope(name):
                values[give[0]] = call(values[need[0]])
    return values[f"out{len(CALLS) - 1}"].reshape(1, 1, 1, KR * TB, KC * TB)


def solution(mesh):
    return jax.shard_map(
        body,
        mesh=mesh,
        in_specs=(
            P("cube", "row", "col", None, None, None),
            P("cube", "row", "col", None, None),
            P("cube", "row", "col", None, None),
            P("cube", "row", "col", None, None),
            P(),
        ),
        out_specs=P("cube", "row", "col", None, None),
        check_vma=False,
    )
```

time: 401 us -> 330 us (0.82)
  waiting for transfers between devices: 192 us -> 106 us
  starting transfers between devices: 82.4 us -> 49.7 us
  Pallas kernels: 110 us -> 130 us
  local copies, waits for them, and re-layouts: 14.3 us -> 28.2 us
  between operations: 0.71 us -> 14.2 us
    ppermute x46 -> x40, waiting for transfers between devices: 186 us -> 99.3 us  [flip(): lax.ppermute(v, axis, [(i, i ^ bits) for i in range(lax.axis_size(axis))])]
    ppermute x6 -> x0, starting transfers between devices: 23.5 us -> none  [toward(): return lambda v: lax.ppermute(v, 'row', [(0, to)])]
    pallas_call x56, Pallas kernels: 110 us -> 130 us  [run(): pl.pallas_call(body, in_specs=[s for _, s in ins], out_specs=[ANY if s is...]
    unnamed x26 -> x131, local copies, waits for them, and re-layouts: 13.5 us -> 28.1 us
    all_gather x0 -> x2, waiting for transfers between devices: none -> 6.73 us  [part_steps(): lax.all_gather(v, 'row', tiled=True)]
    ppermute x5 -> x2, starting transfers between devices: 10.7 us -> 5.98 us  [level_steps(): lax.ppermute(v, 'col', [(0, 1)])]
    ppermute x46 -> x40, starting transfers between devices: 48.2 us -> 43.6 us  [flip(): lax.ppermute(v, axis, [(i, i ^ bits) for i in range(lax.axis_size(axis))])]
  transfers between devices with their start and end apart: 57 -> 46, of which waited for: 30 -> 14; matrix products, arithmetic and copies ran while one was open for 0% -> 0% of each run, Pallas kernels for 25% -> 36%
where the time goes in v2:
time: 330 us; the launch traced here: 328 us
  Pallas kernels  130 us (39%)
  waiting for transfers between devices  106 us (32%)
  starting transfers between devices  49.7 us (15%)
  local copies, waits for them, and re-layouts  28.2 us (9%)
  between operations  14.2 us (4%)
    pallas_call x56, Pallas kernels, run(): pl.pallas_call(body, in_specs=[s for _, s in ins], out_specs=[ANY if s is...  130 us
    ppermute x40, waiting for transfers between devices, flip(): lax.ppermute(v, axis, [(i, i ^ bits) for i in range(lax.axis_size(axis))])  99.3 us
    ppermute x40, starting transfers between devices, flip(): lax.ppermute(v, axis, [(i, i ^ bits) for i in range(lax.axis_size(axis))])  43.6 us
    unnamed x131, local copies, waits for them, and re-layouts  28.1 us
    all_gather x2, waiting for transfers between devices, part_steps(): lax.all_gather(v, 'row', tiled=True)  6.73 us
  transfers between devices with their start and end apart: 46, of which 14 were waited for; matrix products, arithmetic and copies ran while one was open for 0% of the time, Pallas kernels for 36%

profile of v2, /device:TPU:0, one launch (start us, length us, event | category | flops | bytes accessed | tf_op | source)
XLA Modules:
  0.0 327.8 jit_solution(6648634055741224311)
XLA Ops:
  15.7 2.8 collective-permute-start.2
  30.1 7.9 %q0t.1 = (f32[64,64,128]{2,1,0:T(8,128)S(1)}, f32[64,64,128]{2,1,0:T(8,128)S(1)}) custom-call(f32[128,128]{1,0:T(8,128)S(1)} %weight.1.weight_ref._, f32[128,128,128]{2,1,0:T(8,128)} %bitcast.88, f32[128,128]{1,0:T(8,128)S(1)} %weight.1.weight_ref._), custom_call_target="tpu_custom_call" | custom-call | tf_op jit(solution)/shard_map/q0t/pallas_call | solution.py:56
  38.3 7.9 %q1t.1 = (f32[64,64,128]{2,1,0:T(8,128)S(1)}, f32[64,64,128]{2,1,0:T(8,128)S(1)}) custom-call(f32[128,128]{1,0:T(8,128)S(1)} %weight.1.weight_ref._, f32[128,128,128]{2,1,0:T(8,128)} %bitcast.89, f32[64,64,128]{2,1,0:T(8,128)S(1)} %get-tuple-element.87._.refs_0_), custom_call_target="tpu_custom_call" | custom-call | tf_op jit(solution)/shard_map/q1t/pallas_call | solution.py:56
  56.8 3.0 c24k0.1
  60.7 14.3 %collective-permute-done.13.recv_ref = f32[64,24,128]{2,1,0:T(8,128)S(1)} collective-permute-done((f32[64,24,128]{2,1,0:T(8,128)S(1)}, f32[64,24,128]{2,1,0:T(8,128)S(1)}, u32[]{:S(2)}, u32[]{:S(2)}) %collective-permute-start.13) | collective-permute-done | bytes 786464 | tf_op jit(solution)/shard_map/c0p1/ppermute | solution.py:445
  76.7 2.7 c96k0.1
  81.2 10.3 %collective-permute-done.11.recv_ref = f32[64,24,128]{2,1,0:T(8,128)} collective-permute-done((f32[64,24,128]{2,1,0:T(8,128)}, f32[64,24,128]{2,1,0:T(8,128)}, u32[]{:S(2)}, u32[]{:S(2)}) %collective-permute-start.11) | collective-permute-done | bytes 786464 | tf_op jit(solution)/shard_map/c48p1/ppermute | solution.py:445
  92.6 2.7 c48k2.1
  98.5 3.0 collective-permute-start.15
  106.8 19.3 %collective-permute-done.17.refs_1_ = f32[8,64,128]{2,1,0:T(8,128)S(1)} collective-permute-done((f32[8,64,128]{2,1,0:T(8,128)S(1)}, f32[8,64,128]{2,1,0:T(8,128)S(1)}, u32[]{:S(2)}, u32[]{:S(2)}) %collective-permute-start.17) | collective-permute-done | bytes 262176 | tf_op jit(solution)/shard_map/q0xa/ppermute | solution.py:445
  145.3 2.7 collective-permute-start.30
  149.2 3.9 %collective-permute-done.21.refs_1_ = f32[8,64,128]{2,1,0:T(8,128)} collective-permute-done((f32[8,64,128]{2,1,0:T(8,128)S(1)}, f32[8,64,128]{2,1,0:T(8,128)}, u32[]{:S(2)}, u32[]{:S(2)}) %collective-permute-start.21) | collective-permute-done | bytes 262176 | tf_op jit(solution)/shard_map/q1xa/ppermute | solution.py:445
  155.0 2.9 collective-permute-start.24
  157.9 3.1 c24k2.1
  161.9 14.5 %collective-permute-done.26.recv_ref = f32[64,16,128]{2,1,0:T(8,128)S(1)} collective-permute-done((f32[64,16,128]{2,1,0:T(8,128)S(1)}, f32[64,16,128]{2,1,0:T(8,128)S(1)}, u32[]{:S(2)}, u32[]{:S(2)}) %collective-permute-start.26) | collective-permute-done | bytes 524320 | tf_op jit(solution)/shard_map/c96p1/ppermute | solution.py:445
  177.2 2.8 collective-permute-start.23
  183.0 2.8 c0k4.1
  186.9 2.8 c112k1.1
  194.9 3.1 c24k3.1
  202.9 3.2 c48k3.1
  210.6 8.3 %collective-permute-done.29.recv_ref = f32[64,24,128]{2,1,0:T(8,128)} collective-permute-done((f32[64,24,128]{2,1,0:T(8,128)}, f32[64,24,128]{2,1,0:T(8,128)}, u32[]{:S(2)}, u32[]{:S(2)}) %collective-permute-start.29) | collective-permute-done | bytes 786464 | tf_op jit(solution)/shard_map/c24p3/ppermute | solution.py:445
  218.9 4.0 %c24k4.1 = (f32[4,4,24,512]{3,2,1,0:T(8,128)S(1)}, f32[4,24,4096]{2,1,0:T(8,128)}) custom-call(s32[4,128]{1,0:T(4,128)S(1)} %bitcast.51, s32[4,128]{1,0:T(4,128)S(1)} %bitcast.76, f32[64,24,128]{2,1,0:T(8,128)S(1)} %copy-done.46, f32[64,24,128]{2,1,0:T(8,128)} %collective-permute-done.29.recv_ref, ...), custom_call_target="tpu_custom_call", output_to_operand_aliasing={{0}: (5, {})} | custom-call | flops 2200000000 | tf_op jit(solution)/shard_map/c24k4/pallas_call | solution.py:56
  222.9 3.1 c72k3.1
  228.9 6.7 %all-gather.5.cloned.1.call-done.refs_0_ = f32[64,64,128]{2,1,0:T(8,128)} async-done(((f32[16,64,128]{2,1,0:T(8,128)}), f32[64,64,128]{2,1,0:T(8,128)}) %all-gather.5.cloned.1.call-update) | async-done | bytes 2097168 | tf_op jit(solution)/shard_map/q1gz/all_gather | solution.py:518
  238.4 3.9 %c48k4.1 = (f32[4,4,24,512]{3,2,1,0:T(8,128)S(1)}, f32[4,24,4096]{2,1,0:T(8,128)}) custom-call(s32[4,128]{1,0:T(4,128)S(1)} %bitcast.53, s32[4,128]{1,0:T(4,128)S(1)} %bitcast.78, f32[64,24,128]{2,1,0:T(8,128)S(1)} %copy-done.12, f32[64,24,128]{2,1,0:T(8,128)} %collective-permute-done.32.recv_ref, ...), custom_call_target="tpu_custom_call", output_to_operand_aliasing={{0}: (5, {})} | custom-call | tf_op jit(solution)/shard_map/c48k4/pallas_call | solution.py:56
  244.8 3.1 collective-permute-start.33
  252.0 3.2 q0m.1
  255.3 4.5 %c72k4.1 = (f32[4,4,24,512]{3,2,1,0:T(8,128)S(1)}, f32[4,24,4096]{2,1,0:T(8,128)}) custom-call(s32[4,128]{1,0:T(4,128)S(1)} %bitcast.56, s32[4,128]{1,0:T(4,128)S(1)} %bitcast.81, f32[64,24,128]{2,1,0:T(8,128)S(1)} %copy-done.10, f32[64,24,128]{2,1,0:T(8,128)} %collective-permute-done.34.recv_ref, ...), custom_call_target="tpu_custom_call", output_to_operand_aliasing={{0}: (5, {})} | custom-call | tf_op jit(solution)/shard_map/c72k4/pallas_call | solution.py:56
  259.8 4.7 %collective-permute-start.41 = (f32[4,4,24,512]{3,2,1,0:T(8,128)S(1)}, f32[4,4,24,512]{3,2,1,0:T(8,128)S(1)}, u32[]{:S(2)}, u32[]{:S(2)}) collective-permute-start(f32[4,4,24,512]{3,2,1,0:T(8,128)S(1)} %get-tuple-element.138._.refs_0_), channel_id=1, source_target_pairs={{0,1},{2,3},{4,5},{6,7},{8,9},{10,11},{12,13},{14,15},{16,17},{18,... | collective-permute-start | bytes 2359304 | tf_op jit(solution)/shard_map/g0pc/ppermute | solution.py:486
  270.7 21.8 %collective-permute-done.37.recv_ref = f32[64,16,128]{2,1,0:T(8,128)S(1)} collective-permute-done((f32[64,16,128]{2,1,0:T(8,128)S(1)}, f32[64,16,128]{2,1,0:T(8,128)S(1)}, u32[]{:S(2)}, u32[]{:S(2)}) %collective-permute-start.37) | collective-permute-done | bytes 524320 | tf_op jit(solution)/shard_map/c112p3/ppermute | solution.py:445
  297.2 13.8 %u0.1.refs_9_ = f32[4,128,4096]{2,1,0:T(8,128)} custom-call(s32[5]{0:T(128)} %copy-done.21, bf16[512,512]{1,0:T(8,128)(2,1)} %copy-done.6, bf16[512,512]{1,0:T(8,128)(2,1)} %copy-done.7, f32[4,4,24,512]{3,2,1,0:T(8,128)} %copy-done.1, f32[4,4,24,512]{3,2,1,0:T(8,128)} %copy-done.63, bf16[256,4096]{1,0:T(8,128)(2,1)} %copy-done, bf16[256,4096]{1,0:T(8,128)(2,1)} %copy-done.2, ...), custom_call_target="tpu_custom_call" | custom-call | tf_op jit(solution)/shard_map/u0/pallas_call | solution.py:56
  311.7 9.6 %u1_.1 = f32[4,128,4096]{2,1,0:T(8,128)} custom-call(s32[5]{0:T(128)} %copy-done.21, bf16[512,512]{1,0:T(8,128)(2,1)} %copy-done.6, bf16[512,512]{1,0:T(8,128)(2,1)} %copy-done.7, f32[2,4,16,512]{3,2,1,0:T(8,128)} %copy-done.5, f32[2,4,16,512]{3,2,1,0:T(8,128)} %copy-done.64, bf16[256,4096]{1,0:T(8,128)(2,1)} %copy-done, ...), custom_call_target="tpu_custom_call", output_to_operand_aliasing={{}: (12, {})} | custom-call | tf_op jit(solution)/shard_map/u1/pallas_call | solution.py:56
  (252 shorter events, 111.3 us)
Async XLA Ops:
  6.5 88.8 %reduce-scatter.3.cloned.1.call-start = ((), (), s32[]{:S(2)}) async-start(), calls=%async_computation.2 | async-start | bytes 2621440 | tf_op jit(solution)/shard_map/q0zs/reduce_scatter | solution.py:508
  22.6 23.7 %collective-permute-start.4 = (f32[64,24,128]{2,1,0:T(8,128)S(1)}, f32[64,24,128]{2,1,0:T(8,128)S(1)}, u32[]{:S(2)}, u32[]{:S(2)}) collective-permute-start(f32[64,24,128]{2,1,0:T(8,128)S(1)} %get-tuple-element.85._), channel_id=1, source_target_pairs={{0,16},{8,24},{16,0},{24,8},{32,48},{40,56},{48,32},{56,40},{64,80... | collective-permute-start | bytes 2359304 | tf_op jit(solution)/shard_map/c72p1/ppermute | solution.py:445
  27.4 22.3 %collective-permute-start.9 = (f32[64,24,128]{2,1,0:T(8,128)S(1)}, f32[64,24,128]{2,1,0:T(8,128)S(1)}, u32[]{:S(2)}, u32[]{:S(2)}) collective-permute-start(f32[64,24,128]{2,1,0:T(8,128)S(1)} %get-tuple-element.86.refs_2_), channel_id=1, source_target_pairs={{0,8},{8,0},{16,24},{24,16},{32,40},{40,32},{48,56},{56,48},{64,72... | collective-permute-start | bytes 2359304 | tf_op jit(solution)/shard_map/c48p0/ppermute | solution.py:445
  54.6 78.6 %reduce-scatter.5.cloned.1.call-start = ((), (), s32[]{:S(2)}) async-start(), calls=%async_computation.3 | async-start | bytes 2621440 | tf_op jit(solution)/shard_map/q1zs/reduce_scatter | solution.py:508
  54.6 20.4 %collective-permute-start.13 = (f32[64,24,128]{2,1,0:T(8,128)S(1)}, f32[64,24,128]{2,1,0:T(8,128)S(1)}, u32[]{:S(2)}, u32[]{:S(2)}) collective-permute-start(f32[64,24,128]{2,1,0:T(8,128)S(1)} %get-tuple-element.83.refs_2_), channel_id=1, source_target_pairs={{0,16},{8,24},{16,0},{24,8},{32,48},{40,56},{48,32},{56,40},{64,80... | collective-permute-start | bytes 2359304 | tf_op jit(solution)/shard_map/c0p1/ppermute | solution.py:445
  56.2 23.3 %collective-permute-start.12 = (f32[64,64,128]{2,1,0:T(8,128)}, f32[64,64,128]{2,1,0:T(8,128)S(1)}, u32[]{:S(2)}, u32[]{:S(2)}) collective-permute-start(f32[64,64,128]{2,1,0:T(8,128)} %copy-done.23), channel_id=1, source_target_pairs={{0,8},{8,0},{16,24},{24,16},{32,40},{40,32},{48,56},{56,48},{64,72... | collective-permute-start | bytes 6291464 | tf_op jit(solution)/shard_map/q1core/ppermute | solution.py:445
  56.3 35.2 %collective-permute-start.11 = (f32[64,24,128]{2,1,0:T(8,128)}, f32[64,24,128]{2,1,0:T(8,128)}, u32[]{:S(2)}, u32[]{:S(2)}) collective-permute-start(f32[64,24,128]{2,1,0:T(8,128)} %copy-done.34), channel_id=1, source_target_pairs={{0,16},{8,24},{16,0},{24,8},{32,48},{40,56},{48,32},{56,40},{64,80... | collective-permute-start | bytes 2359304 | tf_op jit(solution)/shard_map/c48p1/ppermute | solution.py:445
  81.0 127.8 %all-gather.3.cloned.1.call-start = ((), (), s32[]{:S(2)}) async-start(), calls=%async_computation.4 | async-start | bytes 2621440 | tf_op jit(solution)/shard_map/q0gz/all_gather | solution.py:518
  81.1 20.4 %collective-permute-start.10 = (f32[64,24,128]{2,1,0:T(8,128)}, f32[64,24,128]{2,1,0:T(8,128)}, u32[]{:S(2)}, u32[]{:S(2)}) collective-permute-start(f32[64,24,128]{2,1,0:T(8,128)} %get-tuple-element.95._), channel_id=1, source_target_pairs={{0,8},{8,0},{16,24},{24,16},{32,40},{40,32},{48,56},{56,48},{64,72... | collective-permute-start | bytes 2359304 | tf_op jit(solution)/shard_map/c24p0/ppermute | solution.py:445
  98.5 31.2 %collective-permute-start.15 = (f32[64,24,128]{2,1,0:T(8,128)S(1)}, f32[64,24,128]{2,1,0:T(8,128)S(1)}, u32[]{:S(2)}, u32[]{:S(2)}) collective-permute-start(f32[64,24,128]{2,1,0:T(8,128)S(1)} %copy-done.33), channel_id=1, source_target_pairs={{0,32},{8,40},{16,48},{24,56},{32,0},{40,8},{48,16},{56,24},{64,96... | collective-permute-start | bytes 2359304 | tf_op jit(solution)/shard_map/c0p2/ppermute | solution.py:445
  104.7 21.4 %collective-permute-start.17 = (f32[8,64,128]{2,1,0:T(8,128)S(1)}, f32[8,64,128]{2,1,0:T(8,128)S(1)}, u32[]{:S(2)}, u32[]{:S(2)}) collective-permute-start(f32[8,64,128]{2,1,0:T(8,128)S(1)} %q0c.1.refs_0_.refs_2_), channel_id=1, source_target_pairs={{0,16},{8,24},{16,0},{24,8},{32,48},{40,56},{48,32},{56,40},{64,80... | collective-permute-start | bytes 786440 | tf_op jit(solution)/shard_map/q0xa/ppermute | solution.py:445
  106.3 30.2 %collective-permute-start.20 = (f32[64,16,128]{2,1,0:T(8,128)}, f32[64,16,128]{2,1,0:T(8,128)}, u32[]{:S(2)}, u32[]{:S(2)}) collective-permute-start(f32[64,16,128]{2,1,0:T(8,128)} %get-tuple-element.100.refs_2_), channel_id=1, source_target_pairs={{0,8},{8,0},{16,24},{24,16},{32,40},{40,32},{48,56},{56,48},{64,72... | collective-permute-start | bytes 1572872 | tf_op jit(solution)/shard_map/c96p0/ppermute | solution.py:445
  106.3 48.7 %collective-permute-start.14 = (f32[64,24,128]{2,1,0:T(8,128)S(1)}, f32[64,24,128]{2,1,0:T(8,128)}, u32[]{:S(2)}, u32[]{:S(2)}) collective-permute-start(f32[64,24,128]{2,1,0:T(8,128)S(1)} %get-tuple-element.104.refs_2_), channel_id=1, source_target_pairs={{0,16},{8,24},{16,0},{24,8},{32,48},{40,56},{48,32},{56,40},{64,80... | collective-permute-start | bytes 2359304 | tf_op jit(solution)/shard_map/c24p1/ppermute | solution.py:445
  145.3 57.5 %collective-permute-start.30 = (f32[64,24,128]{2,1,0:T(8,128)S(1)}, f32[64,24,128]{2,1,0:T(8,128)}, u32[]{:S(2)}, u32[]{:S(2)}) collective-permute-start(f32[64,24,128]{2,1,0:T(8,128)S(1)} %copy-done.27), channel_id=1, source_target_pairs={{0,32},{8,40},{16,48},{24,56},{32,0},{40,8},{48,16},{56,24},{64,96... | collective-permute-start | bytes 2359304 | tf_op jit(solution)/shard_map/c48p2/ppermute | solution.py:445
  148.1 28.4 %collective-permute-start.26 = (f32[64,16,128]{2,1,0:T(8,128)S(1)}, f32[64,16,128]{2,1,0:T(8,128)S(1)}, u32[]{:S(2)}, u32[]{:S(2)}) collective-permute-start(f32[64,16,128]{2,1,0:T(8,128)S(1)} %get-tuple-element.112.refs_2_), channel_id=1, source_target_pairs={{0,16},{8,24},{16,0},{24,8},{32,48},{40,56},{48,32},{56,40},{64,80... | collective-permute-start | bytes 1572872 | tf_op jit(solution)/shard_map/c96p1/ppermute | solution.py:445
  148.3 37.7 %collective-permute-start.28 = (f32[64,16,128]{2,1,0:T(8,128)S(1)}, f32[64,16,128]{2,1,0:T(8,128)}, u32[]{:S(2)}, u32[]{:S(2)}) collective-permute-start(f32[64,16,128]{2,1,0:T(8,128)S(1)} %get-tuple-element.107._), channel_id=1, source_target_pairs={{0,8},{8,0},{16,24},{24,16},{32,40},{40,32},{48,56},{56,48},{64,72... | collective-permute-start | bytes 1572872 | tf_op jit(solution)/shard_map/c112p0/ppermute | solution.py:445
  149.2 86.5 %all-gather.5.cloned.1.call-start = ((), (), s32[]{:S(2)}) async-start(), calls=%async_computation.5 | async-start | bytes 2621440 | tf_op jit(solution)/shard_map/q1gz/all_gather | solution.py:518
  153.2 29.8 %collective-permute-start.25 = (f32[64,24,128]{2,1,0:T(8,128)}, f32[64,24,128]{2,1,0:T(8,128)S(1)}, u32[]{:S(2)}, u32[]{:S(2)}) collective-permute-start(f32[64,24,128]{2,1,0:T(8,128)} %copy-done.30), channel_id=1, source_target_pairs={{0,64},{8,72},{16,80},{24,88},{32,96},{40,104},{48,112},{56,120},{... | collective-permute-start | bytes 2359304 | tf_op jit(solution)/shard_map/c0p3/ppermute | solution.py:445
  155.0 30.8 %collective-permute-start.24 = (f32[8,64,128]{2,1,0:T(8,128)S(1)}, f32[8,64,128]{2,1,0:T(8,128)S(1)}, u32[]{:S(2)}, u32[]{:S(2)}) collective-permute-start(f32[8,64,128]{2,1,0:T(8,128)S(1)} %q1d.1._.refs_0_), channel_id=1, source_target_pairs={{0,48},{8,56},{16,32},{24,40},{32,16},{40,24},{48,0},{56,8},{64,11... | collective-permute-start | bytes 786440 | tf_op jit(solution)/shard_map/q1xb/ppermute | solution.py:445
  177.2 16.6 %collective-permute-start.23 = (f32[64,24,128]{2,1,0:T(8,128)}, f32[64,24,128]{2,1,0:T(8,128)}, u32[]{:S(2)}, u32[]{:S(2)}) collective-permute-start(f32[64,24,128]{2,1,0:T(8,128)} %get-tuple-element.114._), channel_id=1, source_target_pairs={{0,32},{8,40},{16,48},{24,56},{32,0},{40,8},{48,16},{56,24},{64,96... | collective-permute-start | bytes 2359304 | tf_op jit(solution)/shard_map/c24p2/ppermute | solution.py:445
  198.0 20.9 %collective-permute-start.29 = (f32[64,24,128]{2,1,0:T(8,128)}, f32[64,24,128]{2,1,0:T(8,128)}, u32[]{:S(2)}, u32[]{:S(2)}) collective-permute-start(f32[64,24,128]{2,1,0:T(8,128)} %get-tuple-element.122._), channel_id=1, source_target_pairs={{0,64},{8,72},{16,80},{24,88},{32,96},{40,104},{48,112},{56,120},{... | collective-permute-start | bytes 2359304 | tf_op jit(solution)/shard_map/c24p3/ppermute | solution.py:445
  198.9 23.9 %collective-permute-start.7 = (f32[64,24,128]{2,1,0:T(8,128)}, f32[64,24,128]{2,1,0:T(8,128)}, u32[]{:S(2)}, u32[]{:S(2)}) collective-permute-start(f32[64,24,128]{2,1,0:T(8,128)} %get-tuple-element.90._), channel_id=1, source_target_pairs={{0,32},{8,40},{16,48},{24,56},{32,0},{40,8},{48,16},{56,24},{64,96... | collective-permute-start | bytes 2359304 | tf_op jit(solution)/shard_map/c72p2/ppermute | solution.py:445
  200.5 47.4 %collective-permute-start.36 = (f32[64,16,128]{2,1,0:T(8,128)}, f32[64,16,128]{2,1,0:T(8,128)}, u32[]{:S(2)}, u32[]{:S(2)}) collective-permute-start(f32[64,16,128]{2,1,0:T(8,128)} %get-tuple-element.117.refs_0_), channel_id=1, source_target_pairs={{0,32},{8,40},{16,48},{24,56},{32,0},{40,8},{48,16},{56,24},{64,96... | collective-permute-start | bytes 1572872 | tf_op jit(solution)/shard_map/c96p2/ppermute | solution.py:445
  202.5 39.8 %collective-permute-start.31 = (f32[64,16,128]{2,1,0:T(8,128)}, f32[64,16,128]{2,1,0:T(8,128)}, u32[]{:S(2)}, u32[]{:S(2)}) collective-permute-start(f32[64,16,128]{2,1,0:T(8,128)} %get-tuple-element.120.refs_2_), channel_id=1, source_target_pairs={{0,16},{8,24},{16,0},{24,8},{32,48},{40,56},{48,32},{56,40},{64,80... | collective-permute-start | bytes 1572872 | tf_op jit(solution)/shard_map/c112p1/ppermute | solution.py:445
  206.9 30.5 %collective-permute-start.32 = (f32[64,24,128]{2,1,0:T(8,128)}, f32[64,24,128]{2,1,0:T(8,128)}, u32[]{:S(2)}, u32[]{:S(2)}) collective-permute-start(f32[64,24,128]{2,1,0:T(8,128)} %get-tuple-element.124.refs_1_), channel_id=1, source_target_pairs={{0,64},{8,72},{16,80},{24,88},{32,96},{40,104},{48,112},{56,120},{... | collective-permute-start | bytes 2359304 | tf_op jit(solution)/shard_map/c48p3/ppermute | solution.py:445
  218.9 33.1 %collective-permute-start.35 = (f32[64,64,128]{2,1,0:T(8,128)S(1)}, f32[64,64,128]{2,1,0:T(8,128)}, u32[]{:S(2)}, u32[]{:S(2)}) collective-permute-start(f32[64,64,128]{2,1,0:T(8,128)S(1)} %q0low.1.refs_0_.low_ref), channel_id=1, source_target_pairs={{0,8},{8,0},{16,24},{24,16},{32,40},{40,32},{48,56},{56,48},{64,72... | collective-permute-start | bytes 6291464 | tf_op jit(solution)/shard_map/q0high/ppermute | solution.py:445
  226.9 28.3 %collective-permute-start.34 = (f32[64,24,128]{2,1,0:T(8,128)}, f32[64,24,128]{2,1,0:T(8,128)}, u32[]{:S(2)}, u32[]{:S(2)}) collective-permute-start(f32[64,24,128]{2,1,0:T(8,128)} %get-tuple-element.126._), channel_id=1, source_target_pairs={{0,64},{8,72},{16,80},{24,88},{32,96},{40,104},{48,112},{56,120},{... | collective-permute-start | bytes 2359304 | tf_op jit(solution)/shard_map/c72p3/ppermute | solution.py:445
  237.4 28.9 %collective-permute-start.39 = (f32[64,64,128]{2,1,0:T(8,128)S(1)}, f32[64,64,128]{2,1,0:T(8,128)S(1)}, u32[]{:S(2)}, u32[]{:S(2)}) collective-permute-start(f32[64,64,128]{2,1,0:T(8,128)S(1)} %q1low.1.refs_0_.low_ref), channel_id=1, source_target_pairs={{0,8},{8,0},{16,24},{24,16},{32,40},{40,32},{48,56},{56,48},{64,72... | collective-permute-start | bytes 6291464 | tf_op jit(solution)/shard_map/q1high/ppermute | solution.py:445
  244.8 19.6 %collective-permute-start.33 = (f32[64,16,128]{2,1,0:T(8,128)S(1)}, f32[64,16,128]{2,1,0:T(8,128)S(1)}, u32[]{:S(2)}, u32[]{:S(2)}) collective-permute-start(f32[64,16,128]{2,1,0:T(8,128)S(1)} %get-tuple-element.133._), channel_id=1, source_target_pairs={{0,32},{8,40},{16,48},{24,56},{32,0},{40,8},{48,16},{56,24},{64,96... | collective-permute-start | bytes 1572872 | tf_op jit(solution)/shard_map/c112p2/ppermute | solution.py:445
  250.4 17.7 %collective-permute-start.38 = (f32[64,16,128]{2,1,0:T(8,128)S(1)}, f32[64,16,128]{2,1,0:T(8,128)S(1)}, u32[]{:S(2)}, u32[]{:S(2)}) collective-permute-start(f32[64,16,128]{2,1,0:T(8,128)S(1)} %get-tuple-element.136._), channel_id=1, source_target_pairs={{0,64},{8,72},{16,80},{24,88},{32,96},{40,104},{48,112},{56,120},{... | collective-permute-start | bytes 1572872 | tf_op jit(solution)/shard_map/c96p3/ppermute | solution.py:445
  259.8 36.6 %collective-permute-start.41 = (f32[4,4,24,512]{3,2,1,0:T(8,128)S(1)}, f32[4,4,24,512]{3,2,1,0:T(8,128)S(1)}, u32[]{:S(2)}, u32[]{:S(2)}) collective-permute-start(f32[4,4,24,512]{3,2,1,0:T(8,128)S(1)} %get-tuple-element.138._.refs_0_), channel_id=1, source_target_pairs={{0,1},{2,3},{4,5},{6,7},{8,9},{10,11},{12,13},{14,15},{16,17},{18,... | collective-permute-start | bytes 2359304 | tf_op jit(solution)/shard_map/g0pc/ppermute | solution.py:486
  266.0 26.5 %collective-permute-start.37 = (f32[64,16,128]{2,1,0:T(8,128)S(1)}, f32[64,16,128]{2,1,0:T(8,128)S(1)}, u32[]{:S(2)}, u32[]{:S(2)}) collective-permute-start(f32[64,16,128]{2,1,0:T(8,128)S(1)} %get-tuple-element.140._), channel_id=1, source_target_pairs={{0,64},{8,72},{16,80},{24,88},{32,96},{40,104},{48,112},{56,120},{... | collective-permute-start | bytes 1572872 | tf_op jit(solution)/shard_map/c112p3/ppermute | solution.py:445
  (79 other events, 360.5 us)
Sparse Core Ops, SparseCore 0:
  54.7 32.2 reduce-scatter.2
  89.5 29.4 reduce-scatter.4
  149.3 32.4 all-gather.2
  203.0 32.6 all-gather.4

commit v3 on v2

--- a/solution.py
+++ b/solution.py
@@ -15,21 +15,17 @@
 F32 = jnp.float32
 BF16 = jnp.bfloat16
 
-GROUPS = ((0, 24, 4), (96, 16, 2))
-CALLS = (1, 1)
+GROUPS = ((0, 24, 2), (48, 24, 2), (96, 16, 1), (112, 16, 1))
+CALLS = (2, 2)
 ORDER = (
-    "l0", "c0k0", "c72k0", "l1", "c0k1", "l2", "c72k1", "c48k0", "l3", "weight", "q0t", "q1t", "c72k2", "c48k1",
-    "q0a", "c24k0", "c0k2", "c96k0", "q1a", "c48k2", "q0b", "c24k1", "q0c", "q0d", "c112k0", "c0k3", "q1b", "c96k1",
-    "q0e", "q1c", "q0h", "q1d", "c24k2", "c96k2", "c0k4", "q1e", "c112k1", "q1h", "c24k3", "c48k3", "q0low",
-    "c24k4", "c72k3", "inv", "q1low", "c48k4", "c112k2", "c96k3", "q0m", "c72k4", "c112k3", "q1m", "c96k4",
-    "c112k4", "u0", "u1",
+    5, 0, 6, 25, 7, 10, 8, 26, 9, 35, 44, 1, 36, 27, 20, 15, 45, 11, 30, 2, 12, 16, 21, 37, 38, 3, 39, 31, 46, 47,
+    17, 48, 40, 41, 49, 22, 53, 50, 13, 18, 4, 14, 42, 23, 19, 32, 51, 24, 28, 33, 43, 52, 54, 34, 29, 55,
 )
 WORK = {
-    "c0k1": 0.2, "c0k2": 0.8, "c0k4": 0.8, "l0": 0.2, "l1": 0.8, "l2": 0.05, "weight": 0.05, "c24k0": 0.1, "c24k1":
-    0.1, "c24k2": 0.8, "c24k3": 0.8, "c24k4": 0.1, "c48k0": 0.1, "c48k1": 0.8, "c48k2": 0.4, "c48k3": 0.05, "c72k0":
-    0.1, "c72k1": 0.4, "c72k2": 0.8, "c72k3": 0.8, "c96k0": 0.8, "c96k1": 0.2, "c96k2": 0.2, "c96k3": 0.8, "c96k4":
-    0.4, "c112k1": 0.2, "c112k3": 0.8, "c112k4": 0.1, "q0a": 0.8, "q0b": 0.8, "q0d": 0.2, "q0e": 0.02, "q0m": 0.8,
-    "q1a": 0.05, "q1b": 0.1, "q1d": 0.05, "q1e": 0.4, "q1h": 0.05, "q1low": 0.8, "q1m": 0.4, "inv": 0.8,
+    0: 0.2, 2: 0.2, 3: 0.1, 4: 0.8, 5: 0.1, 6: 0.02, 7: 0.2, 8: 0.02, 9: 0.4, 10: 0.4, 11: 0.05, 13: 0.8, 15: 0.8,
+    16: 0.4, 18: 0.2, 19: 0.05, 20: 0.8, 22: 0.8, 23: 0.8, 24: 0.1, 26: 0.1, 27: 0.8, 28: 0.8, 29: 0.2, 31: 0.8, 32:
+    0.1, 33: 0.8, 34: 0.8, 36: 0.4, 37: 0.2, 38: 0.2, 40: 0.2, 41: 0.2, 43: 0.4, 44: 0.8, 46: 0.2, 47: 0.1, 48: 0.8,
+    49: 0.05, 55: 0.4,
 }
 PARTS = ((0, 64), (64, 64))
 
@@ -52,17 +48,17 @@
 FLOPS = [0]
 
 
-def run(body, ins, outs, scratch, limit=32, **more):
+def run(body, ins, outs, scratch, limit=16, **more):
     return pl.pallas_call(
         body,
-        in_specs=[s for _, s in ins],
+        in_specs=[ANY if s is HBM else s for _, s in ins],
         out_specs=[ANY if s is HBM else s for _, _, s in outs],
         out_shape=[pltpu.HBM(s, d) if spec is HBM else jax.ShapeDtypeStruct(s, d) for s, d, spec in outs],
         scratch_shapes=scratch,
         compiler_params=pltpu.CompilerParams(vmem_limit_bytes=limit << 20),
         cost_estimate=pl.CostEstimate(flops=FLOPS[0], bytes_accessed=0, transcendentals=0),
         **more,
-    )(*[a for a, _ in ins])
+    )(*[pltpu.with_memory_space_constraint(a, pltpu.HBM) if s is HBM else a for a, s in ins])
 
 
 def first_split(row, rows, tiles, split, tok):
@@ -87,7 +83,7 @@
     return run(
         body,
         [(split, SMEM), (tiles, ANY), (tok, ANY)],
-        [((HALF, rows, TB), F32, ANY)] * 2,
+        [((HALF, rows, TB), F32, ANY), ((HALF, rows, TB), F32, HBM)],
         [pltpu.VMEM((K, rows, TB), F32), pltpu.VMEM((K, rows, TB), F32), DMA((3,))],
     )
 
@@ -121,8 +117,8 @@
 
     return run(
         body,
-        [(split, SMEM), (first, SMEM), (second, SMEM), (kept, ANY), (recv, ANY), (tok, ANY)],
-        [((HALF, rows, TB), F32, ANY)] * 2,
+        [(split, SMEM), (first, SMEM), (second, SMEM), (kept, HBM), (recv, ANY), (tok, ANY)],
+        [((HALF, rows, TB), F32, ANY), ((HALF, rows, TB), F32, HBM)],
         [pltpu.VMEM((K, rows, TB), F32), pltpu.VMEM((K, rows, TB), F32), DMA((4,))],
     )
 
@@ -154,7 +150,7 @@
         one.wait()
         two.wait()
 
-    ins = [(first, SMEM), (second, SMEM), (kept, ANY), (recv, ANY), (tok, ANY)]
+    ins = [(first, SMEM), (second, SMEM), (kept, HBM), (recv, ANY), (tok, ANY)]
     more = {}
     if before is not None:
         ins.append((before, ANY))
@@ -380,7 +376,7 @@
         ins,
         [((KR, TB, KC * TB), F32, pl.BlockSpec((KR, tall, width), lambda n: (0, first // tall, n)))],
         [pltpu.VMEM((2 * m, PW), BF16)],
-        limit=56,
+        limit=24,
         grid=(KC * TB // width,),
         **more,
     )
@@ -388,57 +384,27 @@
 
 class Plan:
     def __init__(self):
-        self.steps = []
-        self.log = []
+        self.steps, self.kernels = [], []
 
     def kernel(self, name, need, give, cost, call):
+        self.kernels.append(name)
         self.steps.append((name, "kernel", need, give, cost, call))
 
     def permute(self, name, need, give, links, cost, call):
         self.steps.append((name, "permute", [need], [give], (links, cost), call))
 
     def emit(self):
-        kernels = {s[0]: s for s in self.steps if s[1] == "kernel"}
-        names = ORDER or [s[0] for s in self.order() if s[1] == "kernel"]
-        for name in names:
-            yield kernels[name]
+        steps = {s[0]: s for s in self.steps}
+        for number in ORDER:
+            step = steps[self.kernels[number]]
+            yield number, step
             for s in self.steps:
-                if s[1] == "permute" and s[2][0] in kernels[name][3]:
-                    yield s
-
-    def order(self, limit=5):
-        ready, links, flying = {}, {}, set()
-        todo = [s for s in self.steps if s[1] == "kernel"]
-        moves = {}
-        for s in self.steps:
-            if s[1] == "permute":
-                moves.setdefault(s[2][0], []).append(s)
-        at, result = 0.0, []
-        while todo:
-            known = [s for s in todo if all(n in ready for n in s[2])]
-            fits = [
-                s for s in known
-                if len(flying - set(s[2])) + sum(len(moves.get(n, ())) for n in s[3]) <= limit
-            ] or known
-            best = min(fits, key=lambda s: (max([at] + [ready[n] for n in s[2]]), todo.index(s)))
-            todo.remove(best)
-            at = max([at] + [ready[n] for n in best[2]]) + best[4]
-            self.log.append((round(at, 1), best[0]))
-            result.append(best)
-            flying -= set(best[2])
-            for n in best[3]:
-                ready[n] = at
-                for m in moves.get(n, ()):
-                    names, cost = m[4]
-                    at += 1.5
-                    begin = max([at] + [links.get(x, 0.0) for x in names])
-                    for x in names:
-                        links[x] = begin + cost
-                    ready[m[3][0]] = begin + cost + 2.0
-                    flying.add(m[3][0])
-                    result.append(m)
-        self.end = at
-        return result
+                if s[1] == "permute" and s[2][0] in step[3]:
+                    yield None, s
+
+
+def text(*parts):
+    return "".join(str(p) for p in parts)
 
 
 def flip(axis, bits):
@@ -454,58 +420,58 @@
     def level_steps(group, index):
         top, rows, count = group
         row = top + index * rows
-        n, g = f"c{row}", f"g{top}"
+        n, g = text("c", row), text("g", top)
         share = rows / 32
-        kernel(f"{n}k0", [], [f"{n}s0", f"{n}h0"], 0.6 + 0.4 * share, lambda v, tok: first_split(row, rows, tiles, split, tok))
+        kernel(text(n, "k0"), [], [text(n, "s0"), text(n, "h0")], 0.6 + 0.4 * share, lambda v, tok: first_split(row, rows, tiles, split, tok))
         for level in range(LEVELS):
-            permute(f"{n}p{level}", f"{n}s{level}", f"{n}r{level}", level_links[level], link_time[level] * share, flip("cube", 1 << level))
-            need = [f"{n}r{level}", f"{n}h{level}"]
+            permute(text(n, "p", level), text(n, "s", level), text(n, "r", level), level_links[level], link_time[level] * share, flip("cube", 1 << level))
+            need = [text(n, "r", level), text(n, "h", level)]
             if level < LEVELS - 1:
                 kernel(
-                    f"{n}k{level + 1}",
+                    text(n, "k", level + 1),
                     need,
-                    [f"{n}s{level + 1}", f"{n}h{level + 1}"],
+                    [text(n, "s", level + 1), text(n, "h", level + 1)],
                     0.8 + 0.9 * share,
                     lambda v, tok, level=level: next_level(
-                        level, rows, v[f"{n}h{level}"], v[f"{n}r{level}"], split, first, second, tok
+                        level, rows, v[text(n, "h", level)], v[text(n, "r", level)], split, first, second, tok
                     ),
                 )
             else:
                 kernel(
-                    f"{n}k4",
-                    need + ([f"{g}cols{index - 1}"] if index else []),
-                    [f"{g}cols{index}", f"{n}front"],
+                    text(n, "k4"),
+                    need + ([text(g, "cols", index - 1)] if index else []),
+                    [text(g, "cols", index), text(n, "front")],
                     0.8 + 0.9 * share,
                     lambda v, tok: last_level(
-                        index, count, rows, v[f"{n}h3"], v[f"{n}r3"], first, second, v.get(f"{g}cols{index - 1}"), tok
+                        index, count, rows, v[text(n, "h3")], v[text(n, "r3")], first, second, v.get(text(g, "cols", index - 1)), tok
                     ),
                 )
         if index == count - 1:
             permute(
-                f"{g}pc", f"{g}cols{index}", f"{g}sent", ("y2",), 5.7 * share * count,
+                text(g, "pc"), text(g, "cols", index), text(g, "sent"), ("y",), 5.7 * share * count,
                 lambda v: lax.ppermute(v, "col", [(0, 1)]),
             )
 
     def part_steps(index, row, rows):
-        n = f"q{index}"
+        n = text("q", index)
         m = rows / 128
 
         def add(name, terms, cuts, cost):
             kernel(
-                f"{n}{name}", [f"{n}{t}" for t in terms], [f"{n}{name}{i}" for i in range(len(cuts))], cost,
-                lambda v, tok: add_cut([v[f"{n}{t}"] for t in terms], cuts, rows, tok),
+                text(n, name), [text(n, t) for t in terms], [text(n, name, i) for i in range(len(cuts))], cost,
+                lambda v, tok: add_cut([v[text(n, t)] for t in terms], cuts, rows, tok),
             )
 
         def move(name, what, axis, bits, links, cost):
-            permute(f"{n}{name}", f"{n}{what}", f"{n}{name}", links, cost, flip(axis, bits))
+            permute(text(n, name), text(n, what), text(n, name), links, cost, flip(axis, bits))
 
         def join(name, pieces, cost):
-            kernel(f"{n}{name}", [f"{n}{p}" for p in pieces], [f"{n}{name}"], cost, lambda v, tok: lay([v[f"{n}{p}"] for p in pieces], rows, tok))
-
-        kernel(f"{n}t", ["weight"], [f"{n}keep", f"{n}send"], 2 + 6 * m, lambda v, tok: parts_of(row, rows, v["weight"], tiles, tok))
+            kernel(text(n, name), [text(n, p) for p in pieces], [text(n, name)], cost, lambda v, tok: lay([v[text(n, p)] for p in pieces], rows, tok))
+
+        kernel(text(n, "t"), ["weight"], [text(n, "keep"), text(n, "send")], 2 + 6 * m, lambda v, tok: parts_of(row, rows, v["weight"], tiles, tok))
         move("core", "send", "cube", 1, ("core",), 7 * m)
         add("a", ["keep", "core"], (64,), 0.5 + 2 * m)
-        permute(f"{n}zs", f"{n}a0", f"{n}zs", ("gather",), 16 + 30 * m, lambda v: lax.psum_scatter(v, "row", tiled=True))
+        permute(text(n, "zs"), text(n, "a0"), text(n, "zs"), ("gather",), 16 + 30 * m, lambda v: lax.psum_scatter(v, "row", tiled=True))
         add("b", ["zs"], (8, 8), 0.5 + m)
         move("y", "b1", "cube", 8, ("y",), 11.4 * m)
         add("c", ["b0", "y"], (8,), 0.5)
@@ -515,17 +481,17 @@
         add("e", ["d0", "xb"], (8,), 0.5)
         move("gy", "e0", "cube", 8, ("y",), 11.4 * m)
         join("h", ["e0", "gy"], 1)
-        permute(f"{n}gz", f"{n}h", f"{n}gz", ("gather",), 16 + 30 * m, lambda v: lax.all_gather(v, "row", tiled=True))
+        permute(text(n, "gz"), text(n, "h"), text(n, "gz"), ("gather",), 16 + 30 * m, lambda v: lax.all_gather(v, "row", tiled=True))
         join("low", ["gz"], 1 + 2 * m)
         move("high", "low", "cube", 1, ("core",), 7 * m)
-        kernel(f"{n}m", [f"{n}low", f"{n}high"], [f"{n}m0", f"{n}m1"], 4, lambda v, tok: prepare(rows, v[f"{n}low"], v[f"{n}high"], ids, tok))
+        kernel(text(n, "m"), [text(n, "low"), text(n, "high")], [text(n, "m0"), text(n, "m1")], 4, lambda v, tok: prepare(rows, v[text(n, "low")], v[text(n, "high")], ids, tok))
 
     level_steps(GROUPS[0], 0)
     kernel("l0", [], ["ls0"], 0.6, lambda v, tok: own_lists(split, first, second, tok))
     for n, bits in enumerate((2, 4, 8, 1)):
-        permute(f"lp{n}", f"ls{n}", f"lr{n}", level_links[(1, 2, 3, 0)[n]], 0.2, flip("cube", bits))
+        permute(text("lp", n), text("ls", n), text("lr", n), level_links[(1, 2, 3, 0)[n]], 0.2, flip("cube", bits))
         if n < 3:
-            kernel(f"l{n + 1}", [f"ls{n}", f"lr{n}"], [f"ls{n + 1}"], 0.5, lambda v, tok, n=n: lay([v[f"ls{n}"], v[f"lr{n}"]], 16, tok))
+            kernel(text("l", n + 1), [text("ls", n), text("lr", n)], [text("ls", n + 1)], 0.5, lambda v, tok, n=n: lay([v[text("ls", n)], v[text("lr", n)]], 16, tok))
     kernel("weight", ["ls3", "lr3"], ["weight"], 1.5, lambda v, tok: weights(ids, v["ls3"], v["lr3"], tok))
     for group in GROUPS:
         for index in range(group[2]):
@@ -534,18 +500,18 @@
     for index, part in enumerate(PARTS):
         part_steps(index, *part)
     kernel("inv", [], ["inv0", "inv1"], 2, lambda v, tok: arrange(pivot_inverse, tok))
-    pivots = [f"q{i}m{j}" for i in range(len(PARTS)) for j in range(2)]
+    pivots = [text("q", i, "m", j) for i in range(len(PARTS)) for j in range(2)]
     start = 0
     for at, number in enumerate(CALLS):
         groups = GROUPS[start:start + number]
         start += number
-        cols = [f"g{top}cols{count - 1}" for top, rows, count in groups]
-        sent = [f"g{top}sent" for top, rows, count in groups]
-        fronts = [f"c{top + n * rows}front" for top, rows, count in groups for n in range(count)]
+        cols = [text("g", top, "cols", count - 1) for top, rows, count in groups]
+        sent = [text("g", top, "sent") for top, rows, count in groups]
+        fronts = [text("c", top + n * rows, "front") for top, rows, count in groups for n in range(count)]
         kernel(
-            f"u{at}", fronts + cols + sent + pivots + ["inv0", "inv1"] + ([f"out{at - 1}"] if at else []), [f"out{at}"], 8,
+            text("u", at), fronts + cols + sent + pivots + ["inv0", "inv1"] + ([text("out", at - 1)] if at else []), [text("out", at)], 8,
             lambda v, tok, at=at, groups=groups, names=(cols, sent, fronts): update(
-                groups, *[[v[n] for n in x] for x in names], ids, (v["inv0"], v["inv1"]), [v[p] for p in pivots], v.get(f"out{at - 1}"), tok
+                groups, *[[v[n] for n in x] for x in names], ids, (v["inv0"], v["inv1"]), [v[p] for p in pivots], v.get(text("out", at - 1)), tok
             ),
         )
 
@@ -561,18 +527,17 @@
     plan = make_plan(tiles, split, first, second, ids, pivot_inverse)
     values = {}
     tok = ids
-    for name, kind, need, give, cost, call in plan.emit():
-        if kind == "kernel":
-            FLOPS[0] = int(WORK.get(name, 0) * 2.2e10)
+    for number, (name, kind, need, give, _, call) in plan.emit():
+        if number is not None:
+            FLOPS[0] = int(WORK.get(number, 0) * 2.2e10)
             with jax.named_scope(name):
                 results = call(values, tok)
-            if not give[0].startswith("out"):
-                tok = results[0]
+            tok = results[0]
             values.update(zip(give, results))
         else:
             with jax.named_scope(name):
                 values[give[0]] = call(values[need[0]])
-    return values[f"out{len(CALLS) - 1}"].reshape(1, 1, 1, KR * TB, KC * TB)
+    return values[text("out", len(CALLS) - 1)].reshape(1, 1, 1, KR * TB, KC * TB)
 
 
 def solution(mesh):

time: 330 us -> 319 us (0.967)
  waiting for transfers between devices: 106 us -> 79.9 us
  Pallas kernels: 130 us -> 150 us
  local copies, waits for them, and re-layouts: 28.2 us -> 20.6 us
    ppermute x40, waiting for transfers between devices: 99.3 us -> 76 us  [flip(): lax.ppermute(v, axis, [(i, i ^ bits) for i in range(lax.axis_size(axis))])]
    pallas_call x56, Pallas kernels: 130 us -> 150 us  [run(): pl.pallas_call(body, in_specs=[ANY if s is HBM else s for _, s in ins], o...]
    unnamed x131 -> x75, local copies, waits for them, and re-layouts: 28.1 us -> 20.5 us
    all_gather x2, waiting for transfers between devices: 6.73 us -> 0.02 us  [part_steps(): lax.all_gather(v, 'row', tiled=True)]
    ppermute x40, starting transfers between devices: 43.6 us -> 37.8 us  [flip(): lax.ppermute(v, axis, [(i, i ^ bits) for i in range(lax.axis_size(axis))])]
    ppermute x2 -> x4, starting transfers between devices: 5.98 us -> 11.1 us  [level_steps(): lax.ppermute(v, 'col', [(0, 1)])]
    ppermute x2 -> x4, waiting for transfers between devices: 0.01 us -> 3.77 us  [level_steps(): lax.ppermute(v, 'col', [(0, 1)])]
  transfers between devices with their start and end apart: 46 -> 48, of which waited for: 14 -> 14; matrix products, arithmetic and copies ran while one was open for 0% -> 0% of each run, Pallas kernels for 36% -> 41%
where the time goes in v3:
time: 319 us; the launch traced here: 314 us
  Pallas kernels  150 us (47%)
  waiting for transfers between devices  79.9 us (25%)
  starting transfers between devices  49 us (15%)
  local copies, waits for them, and re-layouts  20.6 us (6%)
  between operations  14.1 us (4%)
    pallas_call x56, Pallas kernels, run(): pl.pallas_call(body, in_specs=[ANY if s is HBM else s for _, s in ins], o...  150 us
    ppermute x40, waiting for transfers between devices, flip(): lax.ppermute(v, axis, [(i, i ^ bits) for i in range(lax.axis_size(axis))])  76 us
    ppermute x40, starting transfers between devices, flip(): lax.ppermute(v, axis, [(i, i ^ bits) for i in range(lax.axis_size(axis))])  37.8 us
    unnamed x75, local copies, waits for them, and re-layouts  20.5 us
    ppermute x4, starting transfers between devices, level_steps(): lax.ppermute(v, 'col', [(0, 1)])  11.1 us
  transfers between devices with their start and end apart: 48, of which 14 were waited for; matrix products, arithmetic and copies ran while one was open for 0% of the time, Pallas kernels for 41%

profile of v3, /device:TPU:0, one launch (start us, length us, event | category | flops | bytes accessed | tf_op | source)
XLA Modules:
  0.0 313.7 jit_solution(13604985162004213351)
XLA Ops:
  29.4 7.9 %q0t.1 = (f32[64,64,128]{2,1,0:T(8,128)S(1)}, f32[64,64,128]{2,1,0:T(8,128)S(1)}) custom-call(f32[128,128]{1,0:T(8,128)S(1)} %weight.1.weight_ref._, f32[128,128,128]{2,1,0:T(8,128)} %bitcast.88, f32[128,128]{1,0:T(8,128)S(1)} %weight.1.weight_ref._), custom_call_target="tpu_custom_call" | custom-call | tf_op jit(solution)/shard_map/q0t/pallas_call | solution.py:52
  38.4 9.1 %q1t.1 = (f32[64,64,128]{2,1,0:T(8,128)S(1)}, f32[64,64,128]{2,1,0:T(8,128)}) custom-call(f32[128,128]{1,0:T(8,128)S(1)} %weight.1.weight_ref._, f32[128,128,128]{2,1,0:T(8,128)} %bitcast.89, f32[64,64,128]{2,1,0:T(8,128)S(1)} %get-tuple-element.85._.refs_0_), custom_call_target="tpu_custom_call" | custom-call | flops 17600000000 | tf_op jit(solution)/shard_map/q1t/pallas_call | solution.py:52
  68.8 3.6 %c24k1.1 = (f32[64,24,128]{2,1,0:T(8,128)S(1)}, f32[64,24,128]{2,1,0:T(8,128)}) custom-call(s32[4,128]{1,0:T(4,128)S(1)} %bitcast.19, s32[4,128]{1,0:T(4,128)S(1)} %bitcast.39, s32[4,128]{1,0:T(4,128)S(1)} %bitcast.64, f32[64,24,128]{2,1,0:T(8,128)} %get-tuple-element.95.kept_ref, f32[64,24,128]{2,1,0:T(8,128)} %collective-permute-done.10.recv_ref, ...), custom_call_target="tpu_custom_call" | custom-call | flops 1100000000 | tf_op jit(solution)/shard_map/c24k1/pallas_call | solution.py:52
  78.2 3.6 %c0k2.1 = (f32[64,24,128]{2,1,0:T(8,128)}, f32[64,24,128]{2,1,0:T(8,128)}) custom-call(s32[4,128]{1,0:T(4,128)S(1)} %bitcast.21, s32[4,128]{1,0:T(4,128)S(1)} %bitcast.40, s32[4,128]{1,0:T(4,128)S(1)} %bitcast.65, f32[64,24,128]{2,1,0:T(8,128)} %get-tuple-element.99.kept_ref, f32[64,24,128]{2,1,0:T(8,128)} %collective-permute-done.13.recv_ref, ...), custom_call_target="tpu_custom_call" | custom-call | flops 4400000000 | tf_op jit(solution)/shard_map/c0k2/pallas_call | solution.py:52
  84.8 8.2 %collective-permute-done.12.recv_ref = f32[64,24,128]{2,1,0:T(8,128)} collective-permute-done((f32[64,24,128]{2,1,0:T(8,128)S(1)}, f32[64,24,128]{2,1,0:T(8,128)}, u32[]{:S(2)}, u32[]{:S(2)}) %collective-permute-start.12) | collective-permute-done | bytes 786464 | tf_op jit(solution)/shard_map/c24p1/ppermute | solution.py:411
  93.0 3.7 %c24k2.1 = (f32[64,24,128]{2,1,0:T(8,128)S(1)}, f32[64,24,128]{2,1,0:T(8,128)}) custom-call(s32[4,128]{1,0:T(4,128)S(1)} %bitcast.22, s32[4,128]{1,0:T(4,128)S(1)} %bitcast.41, s32[4,128]{1,0:T(4,128)S(1)} %bitcast.66, f32[64,24,128]{2,1,0:T(8,128)} %get-tuple-element.97.kept_ref, f32[64,24,128]{2,1,0:T(8,128)} %collective-permute-done.12.recv_ref, ...), custom_call_target="tpu_custom_call" | custom-call | tf_op jit(solution)/shard_map/c24k2/pallas_call | solution.py:52
  96.7 3.5 %c48k1.1 = (f32[64,24,128]{2,1,0:T(8,128)S(1)}, f32[64,24,128]{2,1,0:T(8,128)}) custom-call(s32[4,128]{1,0:T(4,128)S(1)} %bitcast.23, s32[4,128]{1,0:T(4,128)S(1)} %bitcast.42, s32[4,128]{1,0:T(4,128)S(1)} %bitcast.67, f32[64,24,128]{2,1,0:T(8,128)} %get-tuple-element.93.kept_ref, f32[64,24,128]{2,1,0:T(8,128)} %collective-permute-done.9.recv_ref, ...), custom_call_target="tpu_custom_call" | custom-call | flops 8800000000 | tf_op jit(solution)/shard_map/c48k1/pallas_call | solution.py:52
  106.0 6.2 %collective-permute-done.16.refs_1_ = f32[8,64,128]{2,1,0:T(8,128)S(1)} collective-permute-done((f32[8,64,128]{2,1,0:T(8,128)S(1)}, f32[8,64,128]{2,1,0:T(8,128)S(1)}, u32[]{:S(2)}, u32[]{:S(2)}) %collective-permute-start.16) | collective-permute-done | bytes 262176 | tf_op jit(solution)/shard_map/q0y/ppermute | solution.py:411
  114.4 3.7 %c0k3.1 = (f32[64,24,128]{2,1,0:T(8,128)S(1)}, f32[64,24,128]{2,1,0:T(8,128)}) custom-call(s32[4,128]{1,0:T(4,128)S(1)} %bitcast.25, s32[4,128]{1,0:T(4,128)S(1)} %bitcast.44, s32[4,128]{1,0:T(4,128)S(1)} %bitcast.69, f32[64,24,128]{2,1,0:T(8,128)} %get-tuple-element.109.kept_ref, f32[64,24,128]{2,1,0:T(8,128)} %collective-permute-done.18.recv_ref, ...), custom_call_target="tpu_custom_call" | custom-call | flops 2200000000 | tf_op jit(solution)/shard_map/c0k3/pallas_call | solution.py:52
  118.1 3.5 %collective-permute-done.17.refs_1_ = f32[8,64,128]{2,1,0:T(8,128)S(1)} collective-permute-done((f32[8,64,128]{2,1,0:T(8,128)S(1)}, f32[8,64,128]{2,1,0:T(8,128)S(1)}, u32[]{:S(2)}, u32[]{:S(2)}) %collective-permute-start.17) | collective-permute-done | bytes 262176 | tf_op jit(solution)/shard_map/q0xa/ppermute | solution.py:411
  126.6 6.0 %collective-permute-done.19.refs_1_ = f32[8,64,128]{2,1,0:T(8,128)S(1)} collective-permute-done((f32[8,64,128]{2,1,0:T(8,128)S(1)}, f32[8,64,128]{2,1,0:T(8,128)S(1)}, u32[]{:S(2)}, u32[]{:S(2)}) %collective-permute-start.19) | collective-permute-done | bytes 262176 | tf_op jit(solution)/shard_map/q1y/ppermute | solution.py:411
  138.4 3.5 %c48k2.1 = (f32[64,24,128]{2,1,0:T(8,128)S(1)}, f32[64,24,128]{2,1,0:T(8,128)}) custom-call(s32[4,128]{1,0:T(4,128)S(1)} %bitcast.27, s32[4,128]{1,0:T(4,128)S(1)} %bitcast.46, s32[4,128]{1,0:T(4,128)S(1)} %bitcast.71, f32[64,24,128]{2,1,0:T(8,128)} %get-tuple-element.114.kept_ref, f32[64,24,128]{2,1,0:T(8,128)S(1)} %collective-permute-done.21.recv_ref, ...), custom_call_target="tpu_custom_call" | custom-call | tf_op jit(solution)/shard_map/c48k2/pallas_call | solution.py:52
  142.6 6.4 %collective-permute-done.24.refs_1_ = f32[8,64,128]{2,1,0:T(8,128)S(1)} collective-permute-done((f32[8,64,128]{2,1,0:T(8,128)S(1)}, f32[8,64,128]{2,1,0:T(8,128)S(1)}, u32[]{:S(2)}, u32[]{:S(2)}) %collective-permute-start.24) | collective-permute-done | bytes 262176 | tf_op jit(solution)/shard_map/q0gy/ppermute | solution.py:411
  159.8 10.7 %collective-permute-done.14.recv_ref = f32[64,24,128]{2,1,0:T(8,128)S(1)} collective-permute-done((f32[64,24,128]{2,1,0:T(8,128)S(1)}, f32[64,24,128]{2,1,0:T(8,128)S(1)}, u32[]{:S(2)}, u32[]{:S(2)}) %collective-permute-start.14) | collective-permute-done | bytes 786464 | tf_op jit(solution)/shard_map/c72p1/ppermute | solution.py:411
  170.5 3.5 %c72k2.1 = (f32[64,24,128]{2,1,0:T(8,128)}, f32[64,24,128]{2,1,0:T(8,128)}) custom-call(s32[4,128]{1,0:T(4,128)S(1)} %bitcast.28, s32[4,128]{1,0:T(4,128)S(1)} %bitcast.47, s32[4,128]{1,0:T(4,128)S(1)} %bitcast.72, f32[64,24,128]{2,1,0:T(8,128)} %get-tuple-element.104.kept_ref, f32[64,24,128]{2,1,0:T(8,128)S(1)} %collective-permute-done.14.recv_ref, ...), custom_call_target="tpu_custom_call" | custom-call | flops 17600000000 | tf_op jit(solution)/shard_map/c72k2/pallas_call | solution.py:52
  177.0 10.8 %collective-permute-done.27.recv_ref = f32[64,24,128]{2,1,0:T(8,128)} collective-permute-done((f32[64,24,128]{2,1,0:T(8,128)S(1)}, f32[64,24,128]{2,1,0:T(8,128)}, u32[]{:S(2)}, u32[]{:S(2)}) %collective-permute-start.27) | collective-permute-done | bytes 786464 | tf_op jit(solution)/shard_map/c24p2/ppermute | solution.py:411
  187.8 3.7 %c24k3.1 = (f32[64,24,128]{2,1,0:T(8,128)S(1)}, f32[64,24,128]{2,1,0:T(8,128)}) custom-call(s32[4,128]{1,0:T(4,128)S(1)} %bitcast.29, s32[4,128]{1,0:T(4,128)S(1)} %bitcast.48, s32[4,128]{1,0:T(4,128)S(1)} %bitcast.73, f32[64,24,128]{2,1,0:T(8,128)} %get-tuple-element.121.kept_ref, f32[64,24,128]{2,1,0:T(8,128)} %collective-permute-done.27.recv_ref, ...), custom_call_target="tpu_custom_call" | custom-call | flops 17600000000 | tf_op jit(solution)/shard_map/c24k3/pallas_call | solution.py:52
  192.3 12.4 %collective-permute-done.31.recv_ref = f32[64,24,128]{2,1,0:T(8,128)} collective-permute-done((f32[64,24,128]{2,1,0:T(8,128)S(1)}, f32[64,24,128]{2,1,0:T(8,128)}, u32[]{:S(2)}, u32[]{:S(2)}) %collective-permute-start.31) | collective-permute-done | bytes 786464 | tf_op jit(solution)/shard_map/c48p2/ppermute | solution.py:411
  204.7 3.7 %c48k3.1 = (f32[64,24,128]{2,1,0:T(8,128)}, f32[64,24,128]{2,1,0:T(8,128)}) custom-call(s32[4,128]{1,0:T(4,128)S(1)} %bitcast.30, s32[4,128]{1,0:T(4,128)S(1)} %bitcast.49, s32[4,128]{1,0:T(4,128)S(1)} %bitcast.74, f32[64,24,128]{2,1,0:T(8,128)} %get-tuple-element.125.kept_ref, f32[64,24,128]{2,1,0:T(8,128)} %collective-permute-done.31.recv_ref, ...), custom_call_target="tpu_custom_call" | custom-call | flops 4400000000 | tf_op jit(solution)/shard_map/c48k3/pallas_call | solution.py:52
  209.1 4.1 %c0k4.1 = (f32[2,4,24,512]{3,2,1,0:T(8,128)S(1)}, f32[4,24,4096]{2,1,0:T(8,128)}) custom-call(s32[4,128]{1,0:T(4,128)S(1)} %bitcast.50, s32[4,128]{1,0:T(4,128)S(1)} %bitcast.75, f32[64,24,128]{2,1,0:T(8,128)} %get-tuple-element.124.kept_ref, f32[64,24,128]{2,1,0:T(8,128)} %collective-permute-done.30.recv_ref, f32[64,24,128]{2,1,0:T(8,128)} %get-tuple-element.126.refs_0_), custom_call_target="tpu_custom_call" | custom-call | flops 17600000000 | tf_op jit(solution)/shard_map/c0k4/pallas_call | solution.py:52
  213.3 3.8 %c24k4.1 = (f32[2,4,24,512]{3,2,1,0:T(8,128)S(1)}, f32[4,24,4096]{2,1,0:T(8,128)}) custom-call(s32[4,128]{1,0:T(4,128)S(1)} %bitcast.51, s32[4,128]{1,0:T(4,128)S(1)} %bitcast.76, f32[64,24,128]{2,1,0:T(8,128)} %get-tuple-element.122.kept_ref, f32[64,24,128]{2,1,0:T(8,128)S(1)} %collective-permute-done.29.recv_ref, ...), custom_call_target="tpu_custom_call", output_to_operand_aliasing={{0}: (5, {})} | custom-call | tf_op jit(solution)/shard_map/c24k4/pallas_call | solution.py:52
  218.9 3.7 %c72k3.1 = (f32[64,24,128]{2,1,0:T(8,128)}, f32[64,24,128]{2,1,0:T(8,128)}) custom-call(s32[4,128]{1,0:T(4,128)S(1)} %bitcast.31, s32[4,128]{1,0:T(4,128)S(1)} %bitcast.52, s32[4,128]{1,0:T(4,128)S(1)} %bitcast.77, f32[64,24,128]{2,1,0:T(8,128)} %get-tuple-element.120.kept_ref, f32[64,24,128]{2,1,0:T(8,128)} %collective-permute-done.26.recv_ref, ...), custom_call_target="tpu_custom_call" | custom-call | flops 17600000000 | tf_op jit(solution)/shard_map/c72k3/pallas_call | solution.py:52
  227.7 5.7 %collective-permute-start.38 = (f32[2,4,24,512]{3,2,1,0:T(8,128)S(1)}, f32[2,4,24,512]{3,2,1,0:T(8,128)}, u32[]{:S(2)}, u32[]{:S(2)}) collective-permute-start(f32[2,4,24,512]{3,2,1,0:T(8,128)S(1)} %get-tuple-element.128.refs_1_.refs_0_), channel_id=1, source_target_pairs={{0,1},{2,3},{4,5},{6,7},{8,9},{10,11},{12,13},{14,15},{16,17},{18,... | collective-permute-start | bytes 1179656 | tf_op jit(solution)/shard_map/g0pc/ppermute | solution.py:452
  233.4 4.1 %c48k4.1 = (f32[2,4,24,512]{3,2,1,0:T(8,128)S(1)}, f32[4,24,4096]{2,1,0:T(8,128)}) custom-call(s32[4,128]{1,0:T(4,128)S(1)} %bitcast.53, s32[4,128]{1,0:T(4,128)S(1)} %bitcast.78, f32[64,24,128]{2,1,0:T(8,128)} %get-tuple-element.132.kept_ref, f32[64,24,128]{2,1,0:T(8,128)} %collective-permute-done.34.recv_ref, f32[64,24,128]{2,1,0:T(8,128)} %get-tuple-element.130.refs_0_), custom_call_target="tpu_custom_call" | custom-call | flops 1100000000 | tf_op jit(solution)/shard_map/c48k4/pallas_call | solution.py:52
  243.8 4.1 %c72k4.1 = (f32[2,4,24,512]{3,2,1,0:T(8,128)S(1)}, f32[4,24,4096]{2,1,0:T(8,128)}) custom-call(s32[4,128]{1,0:T(4,128)S(1)} %bitcast.55, s32[4,128]{1,0:T(4,128)S(1)} %bitcast.80, f32[64,24,128]{2,1,0:T(8,128)} %get-tuple-element.129.kept_ref, f32[64,24,128]{2,1,0:T(8,128)} %collective-permute-done.32.recv_ref, ...), custom_call_target="tpu_custom_call", output_to_operand_aliasing={{0}: (5, {})} | custom-call | flops 2200000000 | tf_op jit(solution)/shard_map/c72k4/pallas_call | solution.py:52
  250.7 3.4 %c96k3.1 = (f32[64,16,128]{2,1,0:T(8,128)S(1)}, f32[64,16,128]{2,1,0:T(8,128)}) custom-call(s32[4,128]{1,0:T(4,128)S(1)} %bitcast.33, s32[4,128]{1,0:T(4,128)S(1)} %bitcast.56, s32[4,128]{1,0:T(4,128)S(1)} %bitcast.81, f32[64,16,128]{2,1,0:T(8,128)} %get-tuple-element.119.kept_ref, f32[64,16,128]{2,1,0:T(8,128)} %collective-permute-done.25.recv_ref, ...), custom_call_target="tpu_custom_call" | custom-call | flops 17600000000 | tf_op jit(solution)/shard_map/c96k3/pallas_call | solution.py:52
  257.1 3.4 %c112k3.1 = (f32[64,16,128]{2,1,0:T(8,128)S(1)}, f32[64,16,128]{2,1,0:T(8,128)}) custom-call(s32[4,128]{1,0:T(4,128)S(1)} %bitcast.34, s32[4,128]{1,0:T(4,128)S(1)} %bitcast.57, s32[4,128]{1,0:T(4,128)S(1)} %bitcast.82, f32[64,16,128]{2,1,0:T(8,128)} %get-tuple-element.138.kept_ref, f32[64,16,128]{2,1,0:T(8,128)} %collective-permute-done.36.recv_ref, ...), custom_call_target="tpu_custom_call" | custom-call | flops 17600000000 | tf_op jit(solution)/shard_map/c112k3/pallas_call | solution.py:52
  268.7 10.3 %u0.1.refs_0_.refs_11_ = f32[4,128,4096]{2,1,0:T(8,128)} custom-call(s32[5]{0:T(128)S(1)} %copy-done.19, bf16[512,512]{1,0:T(8,128)(2,1)S(1)} %get-tuple-element.117.refs_2_.inv_ref, bf16[512,512]{1,0:T(8,128)(2,1)S(1)} %get-tuple-element.118.low_ref, f32[2,4,24,512]{3,2,1,0:T(8,128)S(1)} %get-tuple-element.128.refs_1_.refs_0_, ...), custom_call_target="tpu_custom_call" | custom-call | tf_op jit(solution)/shard_map/u0/pallas_call | solution.py:52
  279.0 4.0 %collective-permute-done.37.recv_ref = f32[64,16,128]{2,1,0:T(8,128)S(1)} collective-permute-done((f32[64,16,128]{2,1,0:T(8,128)S(1)}, f32[64,16,128]{2,1,0:T(8,128)S(1)}, u32[]{:S(2)}, u32[]{:S(2)}) %collective-permute-start.37) | collective-permute-done | bytes 524320 | tf_op jit(solution)/shard_map/c112p3/ppermute | solution.py:411
  286.3 3.5 %c112k4.1 = (f32[1,4,16,512]{3,2,1,0:T(8,128)S(1)}, f32[4,16,4096]{2,1,0:T(8,128)}) custom-call(s32[4,128]{1,0:T(4,128)S(1)} %bitcast.58, s32[4,128]{1,0:T(4,128)S(1)} %bitcast.83, f32[64,16,128]{2,1,0:T(8,128)} %get-tuple-element.139.kept_ref, f32[64,16,128]{2,1,0:T(8,128)S(1)} %collective-permute-done.37.recv_ref, f32[4,128,4096]{2,1,0:T(8,128)S(1)} %copy-done), custom_call_target="tpu_custom_call" | custom-call | flops 17600000000 | tf_op jit(solution)/shard_map/c112k4/pallas_call | solution.py:52
  289.8 3.5 %c96k4.1 = (f32[1,4,16,512]{3,2,1,0:T(8,128)S(1)}, f32[4,16,4096]{2,1,0:T(8,128)}) custom-call(s32[4,128]{1,0:T(4,128)S(1)} %bitcast.59, s32[4,128]{1,0:T(4,128)S(1)} %bitcast.84, f32[64,16,128]{2,1,0:T(8,128)} %get-tuple-element.136.kept_ref, f32[64,16,128]{2,1,0:T(8,128)S(1)} %collective-permute-done.35.recv_ref, ...), custom_call_target="tpu_custom_call" | custom-call | flops 4400000000 | tf_op jit(solution)/shard_map/c96k4/pallas_call | solution.py:52
  300.9 6.3 %u1_.1 = f32[4,128,4096]{2,1,0:T(8,128)} custom-call(s32[5]{0:T(128)S(1)} %copy-done.19, bf16[512,512]{1,0:T(8,128)(2,1)S(1)} %get-tuple-element.117.refs_2_.inv_ref, bf16[512,512]{1,0:T(8,128)(2,1)S(1)} %get-tuple-element.118.low_ref, f32[1,4,16,512]{3,2,1,0:T(8,128)S(1)} %get-tuple-element.150.refs_0_.refs_10_, ...), custom_call_target="tpu_custom_call", output_to_operand_aliasing={{}: (14, {})} | custom-call | flops 8800000000 | tf_op jit(solution)/shard_map/u1/pallas_call | solution.py:52
  (200 shorter events, 126.2 us)
Async XLA Ops:
  6.5 97.1 %reduce-scatter.5.cloned.1.call-start = ((), (), s32[]{:S(2)}) async-start(), calls=%async_computation.3 | async-start | bytes 2621440 | tf_op jit(solution)/shard_map/q0zs/reduce_scatter | solution.py:474
  37.3 15.5 %collective-permute-start.6 = (f32[64,64,128]{2,1,0:T(8,128)S(1)}, f32[64,64,128]{2,1,0:T(8,128)S(1)}, u32[]{:S(2)}, u32[]{:S(2)}) collective-permute-start(f32[64,64,128]{2,1,0:T(8,128)S(1)} %get-tuple-element.86), channel_id=1, source_target_pairs={{0,8},{8,0},{16,24},{24,16},{32,40},{40,32},{48,56},{56,48},{64,72... | collective-permute-start | bytes 6291464 | tf_op jit(solution)/shard_map/q0core/ppermute | solution.py:411
  37.9 30.9 %collective-permute-start.10 = (f32[64,24,128]{2,1,0:T(8,128)}, f32[64,24,128]{2,1,0:T(8,128)}, u32[]{:S(2)}, u32[]{:S(2)}) collective-permute-start(f32[64,24,128]{2,1,0:T(8,128)} %get-tuple-element.82.refs_2_), channel_id=1, source_target_pairs={{0,8},{8,0},{16,24},{24,16},{32,40},{40,32},{48,56},{56,48},{64,72... | collective-permute-start | bytes 2359304 | tf_op jit(solution)/shard_map/c24p0/ppermute | solution.py:411
  38.2 16.1 %collective-permute-start.4 = (f32[64,16,128]{2,1,0:T(8,128)S(1)}, f32[64,16,128]{2,1,0:T(8,128)S(1)}, u32[]{:S(2)}, u32[]{:S(2)}) collective-permute-start(f32[64,16,128]{2,1,0:T(8,128)S(1)} %get-tuple-element.84._), channel_id=1, source_target_pairs={{0,16},{8,24},{16,0},{24,8},{32,48},{40,56},{48,32},{56,40},{64,80... | collective-permute-start | bytes 1572872 | tf_op jit(solution)/shard_map/c96p1/ppermute | solution.py:411
  47.5 18.0 %collective-permute-start.11 = (f32[64,64,128]{2,1,0:T(8,128)}, f32[64,64,128]{2,1,0:T(8,128)}, u32[]{:S(2)}, u32[]{:S(2)}) collective-permute-start(f32[64,64,128]{2,1,0:T(8,128)} %get-tuple-element.96), channel_id=1, source_target_pairs={{0,8},{8,0},{16,24},{24,16},{32,40},{40,32},{48,56},{56,48},{64,72... | collective-permute-start | bytes 6291464 | tf_op jit(solution)/shard_map/q1core/ppermute | solution.py:411
  50.9 26.3 %collective-permute-start.13 = (f32[64,24,128]{2,1,0:T(8,128)}, f32[64,24,128]{2,1,0:T(8,128)}, u32[]{:S(2)}, u32[]{:S(2)}) collective-permute-start(f32[64,24,128]{2,1,0:T(8,128)} %get-tuple-element.89.refs_2_), channel_id=1, source_target_pairs={{0,16},{8,24},{16,0},{24,8},{32,48},{40,56},{48,32},{56,40},{64,80... | collective-permute-start | bytes 2359304 | tf_op jit(solution)/shard_map/c0p1/ppermute | solution.py:411
  54.3 70.5 %reduce-scatter.3.cloned.1.call-start = ((), (), s32[]{:S(2)}) async-start(), calls=%async_computation.2 | async-start | bytes 2621440 | tf_op jit(solution)/shard_map/q1zs/reduce_scatter | solution.py:474
  72.4 20.6 %collective-permute-start.12 = (f32[64,24,128]{2,1,0:T(8,128)S(1)}, f32[64,24,128]{2,1,0:T(8,128)}, u32[]{:S(2)}, u32[]{:S(2)}) collective-permute-start(f32[64,24,128]{2,1,0:T(8,128)S(1)} %get-tuple-element.98._), channel_id=1, source_target_pairs={{0,16},{8,24},{16,0},{24,8},{32,48},{40,56},{48,32},{56,40},{64,80... | collective-permute-start | bytes 2359304 | tf_op jit(solution)/shard_map/c24p1/ppermute | solution.py:411
  72.8 23.9 %collective-permute-start.9 = (f32[64,24,128]{2,1,0:T(8,128)S(1)}, f32[64,24,128]{2,1,0:T(8,128)}, u32[]{:S(2)}, u32[]{:S(2)}) collective-permute-start(f32[64,24,128]{2,1,0:T(8,128)S(1)} %get-tuple-element.94.refs_2_), channel_id=1, source_target_pairs={{0,8},{8,0},{16,24},{24,16},{32,40},{40,32},{48,56},{56,48},{64,72... | collective-permute-start | bytes 2359304 | tf_op jit(solution)/shard_map/c48p0/ppermute | solution.py:411
  72.8 27.4 %collective-permute-start.8 = (f32[64,24,128]{2,1,0:T(8,128)S(1)}, f32[64,24,128]{2,1,0:T(8,128)S(1)}, u32[]{:S(2)}, u32[]{:S(2)}) collective-permute-start(f32[64,24,128]{2,1,0:T(8,128)S(1)} %copy-done.25), channel_id=1, source_target_pairs={{0,8},{8,0},{16,24},{24,16},{32,40},{40,32},{48,56},{56,48},{64,72... | collective-permute-start | bytes 2359304 | tf_op jit(solution)/shard_map/c72p0/ppermute | solution.py:411
  77.1 140.0 %all-gather.3.cloned.1.call-start = ((), (), s32[]{:S(2)}) async-start(), calls=%async_computation.4 | async-start | bytes 2621440 | tf_op jit(solution)/shard_map/q0gz/all_gather | solution.py:484
  81.9 32.5 %collective-permute-start.18 = (f32[64,24,128]{2,1,0:T(8,128)}, f32[64,24,128]{2,1,0:T(8,128)}, u32[]{:S(2)}, u32[]{:S(2)}) collective-permute-start(f32[64,24,128]{2,1,0:T(8,128)} %get-tuple-element.101._), channel_id=1, source_target_pairs={{0,32},{8,40},{16,48},{24,56},{32,0},{40,8},{48,16},{56,24},{64,96... | collective-permute-start | bytes 2359304 | tf_op jit(solution)/shard_map/c0p2/ppermute | solution.py:411
  106.0 15.6 %collective-permute-start.15 = (f32[64,16,128]{2,1,0:T(8,128)S(1)}, f32[64,16,128]{2,1,0:T(8,128)S(1)}, u32[]{:S(2)}, u32[]{:S(2)}) collective-permute-start(f32[64,16,128]{2,1,0:T(8,128)S(1)} %copy-done.32), channel_id=1, source_target_pairs={{0,8},{8,0},{16,24},{24,16},{32,40},{40,32},{48,56},{56,48},{64,72... | collective-permute-start | bytes 1572872 | tf_op jit(solution)/shard_map/c112p0/ppermute | solution.py:411
  112.5 25.9 %collective-permute-start.21 = (f32[64,24,128]{2,1,0:T(8,128)S(1)}, f32[64,24,128]{2,1,0:T(8,128)S(1)}, u32[]{:S(2)}, u32[]{:S(2)}) collective-permute-start(f32[64,24,128]{2,1,0:T(8,128)S(1)} %get-tuple-element.103._), channel_id=1, source_target_pairs={{0,16},{8,24},{16,0},{24,8},{32,48},{40,56},{48,32},{56,40},{64,80... | collective-permute-start | bytes 2359304 | tf_op jit(solution)/shard_map/c48p1/ppermute | solution.py:411
  149.9 91.3 %all-gather.5.cloned.1.call-start = ((), (), s32[]{:S(2)}) async-start(), calls=%async_computation.5 | async-start | bytes 2621440 | tf_op jit(solution)/shard_map/q1gz/all_gather | solution.py:484
  149.9 20.6 %collective-permute-start.14 = (f32[64,24,128]{2,1,0:T(8,128)S(1)}, f32[64,24,128]{2,1,0:T(8,128)S(1)}, u32[]{:S(2)}, u32[]{:S(2)}) collective-permute-start(f32[64,24,128]{2,1,0:T(8,128)S(1)} %copy-done.23), channel_id=1, source_target_pairs={{0,16},{8,24},{16,0},{24,8},{32,48},{40,56},{48,32},{56,40},{64,80... | collective-permute-start | bytes 2359304 | tf_op jit(solution)/shard_map/c72p1/ppermute | solution.py:411
  152.3 35.6 %collective-permute-start.27 = (f32[64,24,128]{2,1,0:T(8,128)S(1)}, f32[64,24,128]{2,1,0:T(8,128)}, u32[]{:S(2)}, u32[]{:S(2)}) collective-permute-start(f32[64,24,128]{2,1,0:T(8,128)S(1)} %copy-done.21), channel_id=1, source_target_pairs={{0,32},{8,40},{16,48},{24,56},{32,0},{40,8},{48,16},{56,24},{64,96... | collective-permute-start | bytes 2359304 | tf_op jit(solution)/shard_map/c24p2/ppermute | solution.py:411
  154.1 55.0 %collective-permute-start.30 = (f32[64,24,128]{2,1,0:T(8,128)S(1)}, f32[64,24,128]{2,1,0:T(8,128)}, u32[]{:S(2)}, u32[]{:S(2)}) collective-permute-start(f32[64,24,128]{2,1,0:T(8,128)S(1)} %get-tuple-element.110.refs_2_), channel_id=1, source_target_pairs={{0,64},{8,72},{16,80},{24,88},{32,96},{40,104},{48,112},{56,120},{... | collective-permute-start | bytes 2359304 | tf_op jit(solution)/shard_map/c0p3/ppermute | solution.py:411
  154.1 50.6 %collective-permute-start.31 = (f32[64,24,128]{2,1,0:T(8,128)S(1)}, f32[64,24,128]{2,1,0:T(8,128)}, u32[]{:S(2)}, u32[]{:S(2)}) collective-permute-start(f32[64,24,128]{2,1,0:T(8,128)S(1)} %get-tuple-element.115.refs_2_), channel_id=1, source_target_pairs={{0,32},{8,40},{16,48},{24,56},{32,0},{40,8},{48,16},{56,24},{64,96... | collective-permute-start | bytes 2359304 | tf_op jit(solution)/shard_map/c48p2/ppermute | solution.py:411
  159.0 17.1 %collective-permute-start.28 = (f32[8,64,128]{2,1,0:T(8,128)S(1)}, f32[8,64,128]{2,1,0:T(8,128)S(1)}, u32[]{:S(2)}, u32[]{:S(2)}) collective-permute-start(f32[8,64,128]{2,1,0:T(8,128)S(1)} %q1e.1._.refs_0_), channel_id=1, source_target_pairs={{0,64},{8,72},{16,80},{24,88},{32,96},{40,104},{48,112},{56,120},{... | collective-permute-start | bytes 786440 | tf_op jit(solution)/shard_map/q1gy/ppermute | solution.py:411
  174.0 44.9 %collective-permute-start.26 = (f32[64,24,128]{2,1,0:T(8,128)}, f32[64,24,128]{2,1,0:T(8,128)}, u32[]{:S(2)}, u32[]{:S(2)}) collective-permute-start(f32[64,24,128]{2,1,0:T(8,128)} %get-tuple-element.116._), channel_id=1, source_target_pairs={{0,32},{8,40},{16,48},{24,56},{32,0},{40,8},{48,16},{56,24},{64,96... | collective-permute-start | bytes 2359304 | tf_op jit(solution)/shard_map/c72p2/ppermute | solution.py:411
  191.5 21.7 %collective-permute-start.29 = (f32[64,24,128]{2,1,0:T(8,128)S(1)}, f32[64,24,128]{2,1,0:T(8,128)S(1)}, u32[]{:S(2)}, u32[]{:S(2)}) collective-permute-start(f32[64,24,128]{2,1,0:T(8,128)S(1)} %get-tuple-element.123._), channel_id=1, source_target_pairs={{0,64},{8,72},{16,80},{24,88},{32,96},{40,104},{48,112},{56,120},{... | collective-permute-start | bytes 2359304 | tf_op jit(solution)/shard_map/c24p3/ppermute | solution.py:411
  208.4 25.0 %collective-permute-start.34 = (f32[64,24,128]{2,1,0:T(8,128)}, f32[64,24,128]{2,1,0:T(8,128)}, u32[]{:S(2)}, u32[]{:S(2)}) collective-permute-start(f32[64,24,128]{2,1,0:T(8,128)} %get-tuple-element.126.refs_0_), channel_id=1, source_target_pairs={{0,64},{8,72},{16,80},{24,88},{32,96},{40,104},{48,112},{56,120},{... | collective-permute-start | bytes 2359304 | tf_op jit(solution)/shard_map/c48p3/ppermute | solution.py:411
  222.6 20.4 %collective-permute-start.32 = (f32[64,24,128]{2,1,0:T(8,128)}, f32[64,24,128]{2,1,0:T(8,128)}, u32[]{:S(2)}, u32[]{:S(2)}) collective-permute-start(f32[64,24,128]{2,1,0:T(8,128)} %get-tuple-element.130.refs_0_), channel_id=1, source_target_pairs={{0,64},{8,72},{16,80},{24,88},{32,96},{40,104},{48,112},{56,120},{... | collective-permute-start | bytes 2359304 | tf_op jit(solution)/shard_map/c72p3/ppermute | solution.py:411
  224.6 23.2 %collective-permute-start.25 = (f32[64,16,128]{2,1,0:T(8,128)}, f32[64,16,128]{2,1,0:T(8,128)}, u32[]{:S(2)}, u32[]{:S(2)}) collective-permute-start(f32[64,16,128]{2,1,0:T(8,128)} %get-tuple-element.90._), channel_id=1, source_target_pairs={{0,32},{8,40},{16,48},{24,56},{32,0},{40,8},{48,16},{56,24},{64,96... | collective-permute-start | bytes 1572872 | tf_op jit(solution)/shard_map/c96p2/ppermute | solution.py:411
  227.7 39.9 %collective-permute-start.38 = (f32[2,4,24,512]{3,2,1,0:T(8,128)S(1)}, f32[2,4,24,512]{3,2,1,0:T(8,128)}, u32[]{:S(2)}, u32[]{:S(2)}) collective-permute-start(f32[2,4,24,512]{3,2,1,0:T(8,128)S(1)} %get-tuple-element.128.refs_1_.refs_0_), channel_id=1, source_target_pairs={{0,1},{2,3},{4,5},{6,7},{8,9},{10,11},{12,13},{14,15},{16,17},{18,... | collective-permute-start | bytes 1179656 | tf_op jit(solution)/shard_map/g0pc/ppermute | solution.py:452
  233.4 27.1 %collective-permute-start.40 = (f32[64,64,128]{2,1,0:T(8,128)S(1)}, f32[64,64,128]{2,1,0:T(8,128)}, u32[]{:S(2)}, u32[]{:S(2)}) collective-permute-start(f32[64,64,128]{2,1,0:T(8,128)S(1)} %q0low.1._.low_ref), channel_id=1, source_target_pairs={{0,8},{8,0},{16,24},{24,16},{32,40},{40,32},{48,56},{56,48},{64,72... | collective-permute-start | bytes 6291464 | tf_op jit(solution)/shard_map/q0high/ppermute | solution.py:411
  240.8 16.2 %collective-permute-start.36 = (f32[64,16,128]{2,1,0:T(8,128)}, f32[64,16,128]{2,1,0:T(8,128)}, u32[]{:S(2)}, u32[]{:S(2)}) collective-permute-start(f32[64,16,128]{2,1,0:T(8,128)} %get-tuple-element.134.refs_1_), channel_id=1, source_target_pairs={{0,32},{8,40},{16,48},{24,56},{32,0},{40,8},{48,16},{56,24},{64,96... | collective-permute-start | bytes 1572872 | tf_op jit(solution)/shard_map/c112p2/ppermute | solution.py:411
  242.9 22.9 %collective-permute-start.41 = (f32[64,64,128]{2,1,0:T(8,128)S(1)}, f32[64,64,128]{2,1,0:T(8,128)S(1)}, u32[]{:S(2)}, u32[]{:S(2)}) collective-permute-start(f32[64,64,128]{2,1,0:T(8,128)S(1)} %q1low.1.refs_0_.low_ref), channel_id=1, source_target_pairs={{0,8},{8,0},{16,24},{24,16},{32,40},{40,32},{48,56},{56,48},{64,72... | collective-permute-start | bytes 6291464 | tf_op jit(solution)/shard_map/q1high/ppermute | solution.py:411
  247.8 19.8 %collective-permute-start.39 = (f32[2,4,24,512]{3,2,1,0:T(8,128)S(1)}, f32[2,4,24,512]{3,2,1,0:T(8,128)S(1)}, u32[]{:S(2)}, u32[]{:S(2)}) collective-permute-start(f32[2,4,24,512]{3,2,1,0:T(8,128)S(1)} %get-tuple-element.135._.refs_2_), channel_id=1, source_target_pairs={{0,1},{2,3},{4,5},{6,7},{8,9},{10,11},{12,13},{14,15},{16,17},{18,... | collective-permute-start | bytes 1179656 | tf_op jit(solution)/shard_map/g48pc/ppermute | solution.py:452
  257.0 32.7 %collective-permute-start.35 = (f32[64,16,128]{2,1,0:T(8,128)S(1)}, f32[64,16,128]{2,1,0:T(8,128)S(1)}, u32[]{:S(2)}, u32[]{:S(2)}) collective-permute-start(f32[64,16,128]{2,1,0:T(8,128)S(1)} %get-tuple-element.137._), channel_id=1, source_target_pairs={{0,64},{8,72},{16,80},{24,88},{32,96},{40,104},{48,112},{56,120},{... | collective-permute-start | bytes 1572872 | tf_op jit(solution)/shard_map/c96p3/ppermute | solution.py:411
  260.5 22.4 %collective-permute-start.37 = (f32[64,16,128]{2,1,0:T(8,128)S(1)}, f32[64,16,128]{2,1,0:T(8,128)S(1)}, u32[]{:S(2)}, u32[]{:S(2)}) collective-permute-start(f32[64,16,128]{2,1,0:T(8,128)S(1)} %get-tuple-element.140._), channel_id=1, source_target_pairs={{0,64},{8,72},{16,80},{24,88},{32,96},{40,104},{48,112},{56,120},{... | collective-permute-start | bytes 1572872 | tf_op jit(solution)/shard_map/c112p3/ppermute | solution.py:411
  (53 other events, 236.0 us)
Sparse Core Ops, SparseCore 0:
  54.4 31.2 reduce-scatter.4
  88.2 29.4 reduce-scatter.2
  150.0 32.2 all-gather.2
  183.8 30.9 all-gather.4

commit v4 on v3

--- a/solution.py
+++ b/solution.py
@@ -15,17 +15,16 @@
 F32 = jnp.float32
 BF16 = jnp.bfloat16
 
-GROUPS = ((0, 24, 2), (48, 24, 2), (96, 16, 1), (112, 16, 1))
-CALLS = (2, 2)
+GROUPS = ((0, 24, 4), (96, 16, 2))
+CALLS = (1, 1)
 ORDER = (
-    5, 0, 6, 25, 7, 10, 8, 26, 9, 35, 44, 1, 36, 27, 20, 15, 45, 11, 30, 2, 12, 16, 21, 37, 38, 3, 39, 31, 46, 47,
-    17, 48, 40, 41, 49, 22, 53, 50, 13, 18, 4, 14, 42, 23, 19, 32, 51, 24, 28, 33, 43, 52, 54, 34, 29, 55,
+    10, 0, 5, 11, 6, 7, 1, 8, 9, 35, 44, 12, 15, 36, 20, 2, 25, 21, 45, 13, 37, 16, 30, 26, 3, 38, 53, 39, 46, 17,
+    40, 47, 4, 41, 27, 48, 49, 22, 14, 50, 18, 23, 42, 31, 28, 19, 24, 32, 51, 52, 33, 43, 54, 29, 34, 55,
 )
 WORK = {
-    0: 0.2, 2: 0.2, 3: 0.1, 4: 0.8, 5: 0.1, 6: 0.02, 7: 0.2, 8: 0.02, 9: 0.4, 10: 0.4, 11: 0.05, 13: 0.8, 15: 0.8,
-    16: 0.4, 18: 0.2, 19: 0.05, 20: 0.8, 22: 0.8, 23: 0.8, 24: 0.1, 26: 0.1, 27: 0.8, 28: 0.8, 29: 0.2, 31: 0.8, 32:
-    0.1, 33: 0.8, 34: 0.8, 36: 0.4, 37: 0.2, 38: 0.2, 40: 0.2, 41: 0.2, 43: 0.4, 44: 0.8, 46: 0.2, 47: 0.1, 48: 0.8,
-    49: 0.05, 55: 0.4,
+    0: 0.05, 1: 0.8, 2: 0.8, 3: 0.05, 6: 0.2, 7: 0.4, 8: 0.05, 9: 0.05, 10: 0.4, 11: 0.05, 12: 0.8, 13: 0.8, 14:
+    0.8, 15: 0.8, 16: 0.05, 17: 0.05, 19: 0.8, 20: 0.8, 22: 0.8, 23: 0.2, 24: 0.4, 25: 0.8, 26: 0.4, 27: 0.05, 29:
+    0.2, 30: 0.4, 34: 0.2, 36: 0.1, 37: 0.05, 38: 0.4, 39: 0.2, 46: 0.05, 48: 0.8, 49: 0.2, 50: 0.4, 51: 0.8,
 }
 PARTS = ((0, 64), (64, 64))
 
@@ -332,8 +331,9 @@
     at_fronts = at_pivots + len(pivots)
 
     def body(ids_ref, inv_ref, low_ref, *refs):
-        out_ref, left = refs[-2:]
+        out_ref, end_ref, left = refs[-3:]
         refs = (ids_ref, inv_ref, low_ref, None) + refs
+        end_ref[...] = jnp.zeros_like(end_ref)
 
         @pl.when(pl.program_id(0) == 0)
         def _():
@@ -374,7 +374,10 @@
     return run(
         body,
         ins,
-        [((KR, TB, KC * TB), F32, pl.BlockSpec((KR, tall, width), lambda n: (0, first // tall, n)))],
+        [
+            ((KR, TB, KC * TB), F32, pl.BlockSpec((KR, tall, width), lambda n: (0, first // tall, n))),
+            ((8, TB), F32, pl.BlockSpec((8, TB), lambda n: (0, 0))),
+        ],
         [pltpu.VMEM((2 * m, PW), BF16)],
         limit=24,
         grid=(KC * TB // width,),
@@ -532,7 +535,7 @@
             FLOPS[0] = int(WORK.get(number, 0) * 2.2e10)
             with jax.named_scope(name):
                 results = call(values, tok)
-            tok = results[0]
+            tok = results[1] if give[0].startswith("out") else results[0]
             values.update(zip(give, results))
         else:
             with jax.named_scope(name):

time: 319 us -> 309 us (0.969)
  starting transfers between devices: 49 us -> 43.6 us
    ppermute x40, waiting for transfers between devices: 76 us -> 63.9 us  [flip(): lax.ppermute(v, axis, [(i, i ^ bits) for i in range(lax.axis_size(axis))])]
    reduce_scatter x2, waiting for transfers between devices: 0.04 us -> 10.5 us  [part_steps(): lax.psum_scatter(v, 'row', tiled=True)]
    ppermute x4 -> x2, starting transfers between devices: 11.1 us -> 6.01 us  [level_steps(): lax.ppermute(v, 'col', [(0, 1)])]
    unnamed x75 -> x66, local copies, waits for them, and re-layouts: 20.5 us -> 19.6 us
  transfers between devices with their start and end apart: 48 -> 46, of which waited for: 14 -> 16; matrix products, arithmetic and copies ran while one was open for 0% -> 0% of each run, Pallas kernels for 41% -> 44%
where the time goes in v4:
time: 309 us; the launch traced here: 305 us
  Pallas kernels  148 us (48%)
  waiting for transfers between devices  79.7 us (26%)
  starting transfers between devices  43.6 us (14%)
  local copies, waits for them, and re-layouts  19.7 us (6%)
  between operations  13.9 us (4%)
    pallas_call x56, Pallas kernels, run(): pl.pallas_call(body, in_specs=[ANY if s is HBM else s for _, s in ins], o...  148 us
    ppermute x40, waiting for transfers between devices, flip(): lax.ppermute(v, axis, [(i, i ^ bits) for i in range(lax.axis_size(axis))])  63.9 us
    ppermute x40, starting transfers between devices, flip(): lax.ppermute(v, axis, [(i, i ^ bits) for i in range(lax.axis_size(axis))])  37.5 us
    unnamed x66, local copies, waits for them, and re-layouts  19.6 us
    reduce_scatter x2, waiting for transfers between devices, part_steps(): lax.psum_scatter(v, 'row', tiled=True)  10.5 us
  transfers between devices with their start and end apart: 46, of which 16 were waited for; matrix products, arithmetic and copies ran while one was open for 0% of the time, Pallas kernels for 44%

profile of v4, /device:TPU:0, one launch (start us, length us, event | category | flops | bytes accessed | tf_op | source)
XLA Modules:
  0.0 305.0 jit_solution(9529232548175526831)
XLA Ops:
  32.2 7.9 %q0t.1 = (f32[64,64,128]{2,1,0:T(8,128)S(1)}, f32[64,64,128]{2,1,0:T(8,128)S(1)}) custom-call(f32[128,128]{1,0:T(8,128)S(1)} %weight.1.weight_ref._, f32[128,128,128]{2,1,0:T(8,128)} %bitcast.87, f32[128,128]{1,0:T(8,128)S(1)} %weight.1.weight_ref._), custom_call_target="tpu_custom_call" | custom-call | tf_op jit(solution)/shard_map/q0t/pallas_call | solution.py:51
  40.4 9.1 %q1t.1 = (f32[64,64,128]{2,1,0:T(8,128)S(1)}, f32[64,64,128]{2,1,0:T(8,128)}) custom-call(f32[128,128]{1,0:T(8,128)S(1)} %weight.1.weight_ref._, f32[128,128,128]{2,1,0:T(8,128)} %bitcast.88, f32[64,64,128]{2,1,0:T(8,128)S(1)} %get-tuple-element.88._.refs_0_), custom_call_target="tpu_custom_call" | custom-call | tf_op jit(solution)/shard_map/q1t/pallas_call | solution.py:51
  66.7 3.6 %c0k2.1 = (f32[64,24,128]{2,1,0:T(8,128)}, f32[64,24,128]{2,1,0:T(8,128)}) custom-call(s32[4,128]{1,0:T(4,128)S(1)} %bitcast.18, s32[4,128]{1,0:T(4,128)S(1)} %bitcast.39, s32[4,128]{1,0:T(4,128)S(1)} %bitcast.64, f32[64,24,128]{2,1,0:T(8,128)} %get-tuple-element.98.kept_ref, f32[64,24,128]{2,1,0:T(8,128)} %collective-permute-done.11.recv_ref, ...), custom_call_target="tpu_custom_call" | custom-call | flops 17600000000 | tf_op jit(solution)/shard_map/c0k2/pallas_call | solution.py:51
  80.6 3.7 %c24k3.1 = (f32[64,24,128]{2,1,0:T(8,128)}, f32[64,24,128]{2,1,0:T(8,128)}) custom-call(s32[4,128]{1,0:T(4,128)S(1)} %bitcast.21, s32[4,128]{1,0:T(4,128)S(1)} %bitcast.41, s32[4,128]{1,0:T(4,128)S(1)} %bitcast.66, f32[64,24,128]{2,1,0:T(8,128)} %get-tuple-element.94.kept_ref, f32[64,24,128]{2,1,0:T(8,128)} %collective-permute-done.8.recv_ref, ...), custom_call_target="tpu_custom_call" | custom-call | flops 17600000000 | tf_op jit(solution)/shard_map/c24k3/pallas_call | solution.py:51
  84.2 6.9 %reduce-scatter.3.cloned.1.call-done.refs_0_ = f32[16,64,128]{2,1,0:T(8,128)} async-done(((f32[64,64,128]{2,1,0:T(8,128)}), f32[16,64,128]{2,1,0:T(8,128)}) %reduce-scatter.3.cloned.1.call-update) | async-done | bytes 524304 | tf_op jit(solution)/shard_map/q0zs/reduce_scatter | solution.py:477
  93.8 3.5 %c48k1.1 = (f32[64,24,128]{2,1,0:T(8,128)}, f32[64,24,128]{2,1,0:T(8,128)}) custom-call(s32[4,128]{1,0:T(4,128)S(1)} %bitcast.22, s32[4,128]{1,0:T(4,128)S(1)} %bitcast.42, s32[4,128]{1,0:T(4,128)S(1)} %bitcast.67, f32[64,24,128]{2,1,0:T(8,128)} %get-tuple-element.107.kept_ref, f32[64,24,128]{2,1,0:T(8,128)} %collective-permute-done.15.recv_ref, ...), custom_call_target="tpu_custom_call" | custom-call | flops 1100000000 | tf_op jit(solution)/shard_map/c48k1/pallas_call | solution.py:51
  103.6 3.6 %c0k3.1 = (f32[64,24,128]{2,1,0:T(8,128)}, f32[64,24,128]{2,1,0:T(8,128)}) custom-call(s32[4,128]{1,0:T(4,128)S(1)} %bitcast.25, s32[4,128]{1,0:T(4,128)S(1)} %bitcast.44, s32[4,128]{1,0:T(4,128)S(1)} %bitcast.69, f32[64,24,128]{2,1,0:T(8,128)} %get-tuple-element.105.kept_ref, f32[64,24,128]{2,1,0:T(8,128)} %collective-permute-done.13.recv_ref, ...), custom_call_target="tpu_custom_call" | custom-call | flops 1100000000 | tf_op jit(solution)/shard_map/c0k3/pallas_call | solution.py:51
  111.0 5.6 %collective-permute-done.17.refs_1_ = f32[8,64,128]{2,1,0:T(8,128)S(1)} collective-permute-done((f32[8,64,128]{2,1,0:T(8,128)S(1)}, f32[8,64,128]{2,1,0:T(8,128)S(1)}, u32[]{:S(2)}, u32[]{:S(2)}) %collective-permute-start.17) | collective-permute-done | bytes 262176 | tf_op jit(solution)/shard_map/q0xa/ppermute | solution.py:414
  119.6 3.6 %reduce-scatter.5.cloned.1.call-done.refs_0_ = f32[16,64,128]{2,1,0:T(8,128)} async-done(((f32[64,64,128]{2,1,0:T(8,128)}), f32[16,64,128]{2,1,0:T(8,128)}) %reduce-scatter.5.cloned.1.call-update) | async-done | bytes 524304 | tf_op jit(solution)/shard_map/q1zs/reduce_scatter | solution.py:477
  125.9 7.7 %collective-permute-done.19.recv_ref = f32[64,24,128]{2,1,0:T(8,128)} collective-permute-done((f32[64,24,128]{2,1,0:T(8,128)}, f32[64,24,128]{2,1,0:T(8,128)}, u32[]{:S(2)}, u32[]{:S(2)}) %collective-permute-start.19) | collective-permute-done | bytes 786464 | tf_op jit(solution)/shard_map/c48p1/ppermute | solution.py:414
  133.6 3.7 %c48k2.1 = (f32[64,24,128]{2,1,0:T(8,128)}, f32[64,24,128]{2,1,0:T(8,128)}) custom-call(s32[4,128]{1,0:T(4,128)S(1)} %bitcast.26, s32[4,128]{1,0:T(4,128)S(1)} %bitcast.45, s32[4,128]{1,0:T(4,128)S(1)} %bitcast.70, f32[64,24,128]{2,1,0:T(8,128)} %get-tuple-element.115.kept_ref, f32[64,24,128]{2,1,0:T(8,128)} %collective-permute-done.19.recv_ref, ...), custom_call_target="tpu_custom_call" | custom-call | flops 1100000000 | tf_op jit(solution)/shard_map/c48k2/pallas_call | solution.py:51
  142.0 3.8 %c0k4.1 = (f32[4,4,24,512]{3,2,1,0:T(8,128)S(1)}, f32[4,24,4096]{2,1,0:T(8,128)}) custom-call(s32[4,128]{1,0:T(4,128)S(1)} %bitcast.46, s32[4,128]{1,0:T(4,128)S(1)} %bitcast.71, f32[64,24,128]{2,1,0:T(8,128)} %get-tuple-element.118.kept_ref, f32[64,24,128]{2,1,0:T(8,128)S(1)} %copy-done.15, f32[8,64,128]{2,1,0:T(8,128)S(1)} %q1c.1.refs_0_), custom_call_target="tpu_custom_call" | custom-call | tf_op jit(solution)/shard_map/c0k4/pallas_call | solution.py:51
  146.7 3.4 %c96k2.1 = (f32[64,16,128]{2,1,0:T(8,128)}, f32[64,16,128]{2,1,0:T(8,128)}) custom-call(s32[4,128]{1,0:T(4,128)S(1)} %bitcast.27, s32[4,128]{1,0:T(4,128)S(1)} %bitcast.47, s32[4,128]{1,0:T(4,128)S(1)} %bitcast.72, f32[64,16,128]{2,1,0:T(8,128)} %get-tuple-element.122.kept_ref, f32[64,16,128]{2,1,0:T(8,128)} %collective-permute-done.25.recv_ref, ...), custom_call_target="tpu_custom_call" | custom-call | flops 1100000000 | tf_op jit(solution)/shard_map/c96k2/pallas_call | solution.py:51
  161.1 6.2 %collective-permute-done.23.recv_ref = f32[64,24,128]{2,1,0:T(8,128)} collective-permute-done((f32[64,24,128]{2,1,0:T(8,128)S(1)}, f32[64,24,128]{2,1,0:T(8,128)}, u32[]{:S(2)}, u32[]{:S(2)}) %collective-permute-start.23) | collective-permute-done | bytes 786464 | tf_op jit(solution)/shard_map/c72p1/ppermute | solution.py:414
  167.3 3.7 %c72k2.1 = (f32[64,24,128]{2,1,0:T(8,128)}, f32[64,24,128]{2,1,0:T(8,128)}) custom-call(s32[4,128]{1,0:T(4,128)S(1)} %bitcast.28, s32[4,128]{1,0:T(4,128)S(1)} %bitcast.48, s32[4,128]{1,0:T(4,128)S(1)} %bitcast.73, f32[64,24,128]{2,1,0:T(8,128)} %get-tuple-element.121.kept_ref, f32[64,24,128]{2,1,0:T(8,128)} %collective-permute-done.23.recv_ref, ...), custom_call_target="tpu_custom_call" | custom-call | flops 17600000000 | tf_op jit(solution)/shard_map/c72k2/pallas_call | solution.py:51
  174.0 4.1 %c24k4.1 = (f32[4,4,24,512]{3,2,1,0:T(8,128)S(1)}, f32[4,24,4096]{2,1,0:T(8,128)}) custom-call(s32[4,128]{1,0:T(4,128)S(1)} %bitcast.49, s32[4,128]{1,0:T(4,128)S(1)} %bitcast.74, f32[64,24,128]{2,1,0:T(8,128)} %get-tuple-element.127.kept_ref, f32[64,24,128]{2,1,0:T(8,128)} %collective-permute-done.30.recv_ref, ...), custom_call_target="tpu_custom_call", output_to_operand_aliasing={{0}: (5, {})} | custom-call | flops 17600000000 | tf_op jit(solution)/shard_map/c24k4/pallas_call | solution.py:51
  178.9 7.2 %collective-permute-done.28.recv_ref = f32[64,24,128]{2,1,0:T(8,128)S(1)} collective-permute-done((f32[64,24,128]{2,1,0:T(8,128)}, f32[64,24,128]{2,1,0:T(8,128)S(1)}, u32[]{:S(2)}, u32[]{:S(2)}) %collective-permute-start.28) | collective-permute-done | bytes 786464 | tf_op jit(solution)/shard_map/c48p2/ppermute | solution.py:414
  186.1 3.5 %c48k3.1 = (f32[64,24,128]{2,1,0:T(8,128)}, f32[64,24,128]{2,1,0:T(8,128)}) custom-call(s32[4,128]{1,0:T(4,128)S(1)} %bitcast.29, s32[4,128]{1,0:T(4,128)S(1)} %bitcast.50, s32[4,128]{1,0:T(4,128)S(1)} %bitcast.75, f32[64,24,128]{2,1,0:T(8,128)} %get-tuple-element.126.kept_ref, f32[64,24,128]{2,1,0:T(8,128)S(1)} %collective-permute-done.28.recv_ref, ...), custom_call_target="tpu_custom_call" | custom-call | tf_op jit(solution)/shard_map/c48k3/pallas_call | solution.py:51
  191.2 11.7 %collective-permute-done.27.recv_ref = f32[64,24,128]{2,1,0:T(8,128)S(1)} collective-permute-done((f32[64,24,128]{2,1,0:T(8,128)}, f32[64,24,128]{2,1,0:T(8,128)S(1)}, u32[]{:S(2)}, u32[]{:S(2)}) %collective-permute-start.27) | collective-permute-done | bytes 786464 | tf_op jit(solution)/shard_map/c72p2/ppermute | solution.py:414
  202.9 3.4 %c72k3.1 = (f32[64,24,128]{2,1,0:T(8,128)}, f32[64,24,128]{2,1,0:T(8,128)}) custom-call(s32[4,128]{1,0:T(4,128)S(1)} %bitcast.30, s32[4,128]{1,0:T(4,128)S(1)} %bitcast.51, s32[4,128]{1,0:T(4,128)S(1)} %bitcast.76, f32[64,24,128]{2,1,0:T(8,128)} %get-tuple-element.124.kept_ref, f32[64,24,128]{2,1,0:T(8,128)S(1)} %collective-permute-done.27.recv_ref, ...), custom_call_target="tpu_custom_call" | custom-call | flops 4400000000 | tf_op jit(solution)/shard_map/c72k3/pallas_call | solution.py:51
  213.8 3.4 %c96k3.1 = (f32[64,16,128]{2,1,0:T(8,128)S(1)}, f32[64,16,128]{2,1,0:T(8,128)}) custom-call(s32[4,128]{1,0:T(4,128)S(1)} %bitcast.32, s32[4,128]{1,0:T(4,128)S(1)} %bitcast.53, s32[4,128]{1,0:T(4,128)S(1)} %bitcast.78, f32[64,16,128]{2,1,0:T(8,128)} %get-tuple-element.135.kept_ref, f32[64,16,128]{2,1,0:T(8,128)} %collective-permute-done.34.recv_ref, ...), custom_call_target="tpu_custom_call" | custom-call | tf_op jit(solution)/shard_map/c96k3/pallas_call | solution.py:51
  217.3 4.1 %c48k4.1 = (f32[4,4,24,512]{3,2,1,0:T(8,128)S(1)}, f32[4,24,4096]{2,1,0:T(8,128)}) custom-call(s32[4,128]{1,0:T(4,128)S(1)} %bitcast.54, s32[4,128]{1,0:T(4,128)S(1)} %bitcast.79, f32[64,24,128]{2,1,0:T(8,128)} %get-tuple-element.134.kept_ref, f32[64,24,128]{2,1,0:T(8,128)} %collective-permute-done.33.recv_ref, ...), custom_call_target="tpu_custom_call", output_to_operand_aliasing={{0}: (5, {})} | custom-call | flops 17600000000 | tf_op jit(solution)/shard_map/c48k4/pallas_call | solution.py:51
  224.6 4.1 %c72k4.1 = (f32[4,4,24,512]{3,2,1,0:T(8,128)S(1)}, f32[4,24,4096]{2,1,0:T(8,128)}) custom-call(s32[4,128]{1,0:T(4,128)S(1)} %bitcast.55, s32[4,128]{1,0:T(4,128)S(1)} %bitcast.80, f32[64,24,128]{2,1,0:T(8,128)} %get-tuple-element.133.kept_ref, f32[64,24,128]{2,1,0:T(8,128)} %collective-permute-done.32.recv_ref, ...), custom_call_target="tpu_custom_call", output_to_operand_aliasing={{0}: (5, {})} | custom-call | flops 8800000000 | tf_op jit(solution)/shard_map/c72k4/pallas_call | solution.py:51
  236.2 4.7 %collective-permute-start.39 = (f32[4,4,24,512]{3,2,1,0:T(8,128)S(1)}, f32[4,4,24,512]{3,2,1,0:T(8,128)S(1)}, u32[]{:S(2)}, u32[]{:S(2)}) collective-permute-start(f32[4,4,24,512]{3,2,1,0:T(8,128)S(1)} %get-tuple-element.138._.refs_0_), channel_id=1, source_target_pairs={{0,1},{2,3},{4,5},{6,7},{8,9},{10,11},{12,13},{14,15},{16,17},{18,... | collective-permute-start | bytes 2359304 | tf_op jit(solution)/shard_map/g0pc/ppermute | solution.py:455
  244.0 12.2 %collective-permute-done.35.recv_ref = f32[64,16,128]{2,1,0:T(8,128)S(1)} collective-permute-done((f32[64,16,128]{2,1,0:T(8,128)S(1)}, f32[64,16,128]{2,1,0:T(8,128)S(1)}, u32[]{:S(2)}, u32[]{:S(2)}) %collective-permute-start.35) | collective-permute-done | bytes 524320 | tf_op jit(solution)/shard_map/c112p2/ppermute | solution.py:414
  256.2 3.6 %c112k3.1 = (f32[64,16,128]{2,1,0:T(8,128)S(1)}, f32[64,16,128]{2,1,0:T(8,128)}) custom-call(s32[4,128]{1,0:T(4,128)S(1)} %bitcast.34, s32[4,128]{1,0:T(4,128)S(1)} %bitcast.57, s32[4,128]{1,0:T(4,128)S(1)} %bitcast.82, f32[64,16,128]{2,1,0:T(8,128)} %get-tuple-element.139.kept_ref, f32[64,16,128]{2,1,0:T(8,128)S(1)} %collective-permute-done.35.recv_ref, ...), custom_call_target="tpu_custom_call" | custom-call | tf_op jit(solution)/shard_map/c112k3/pallas_call | solution.py:51
  261.9 9.8 %u0.1 = (f32[4,128,4096]{2,1,0:T(8,128)}, f32[8,128]{1,0:T(8,128)S(1)}) custom-call(s32[5]{0:T(128)S(1)} %copy-done.21, bf16[512,512]{1,0:T(8,128)(2,1)S(1)} %get-tuple-element.112.refs_2_.inv_ref, bf16[512,512]{1,0:T(8,128)(2,1)S(1)} %copy-done.3, f32[4,4,24,512]{3,2,1,0:T(8,128)S(1)} %get-tuple-element.138._.refs_0_, ...), custom_call_target="tpu_custom_call" | custom-call | tf_op jit(solution)/shard_map/u0/pallas_call | solution.py:51
  271.7 3.5 %c96k4.1 = (f32[2,4,16,512]{3,2,1,0:T(8,128)S(1)}, f32[4,16,4096]{2,1,0:T(8,128)}) custom-call(s32[4,128]{1,0:T(4,128)S(1)} %bitcast.58, s32[4,128]{1,0:T(4,128)S(1)} %bitcast.83, f32[64,16,128]{2,1,0:T(8,128)} %get-tuple-element.144.kept_ref, f32[64,16,128]{2,1,0:T(8,128)S(1)} %collective-permute-done.38.recv_ref, f32[8,128]{1,0:T(8,128)S(1)} %get-tuple-element.152.refs_0_), custom_call_target="tpu_custom_call" | custom-call | flops 4400000000 | tf_op jit(solution)/shard_map/c96k4/pallas_call | solution.py:51
  275.2 5.8 %collective-permute-done.37.recv_ref = f32[64,16,128]{2,1,0:T(8,128)S(1)} collective-permute-done((f32[64,16,128]{2,1,0:T(8,128)S(1)}, f32[64,16,128]{2,1,0:T(8,128)S(1)}, u32[]{:S(2)}, u32[]{:S(2)}) %collective-permute-start.37) | collective-permute-done | bytes 524320 | tf_op jit(solution)/shard_map/c112p3/ppermute | solution.py:414
  281.1 3.5 %c112k4.1 = (f32[2,4,16,512]{3,2,1,0:T(8,128)S(1)}, f32[4,16,4096]{2,1,0:T(8,128)}) custom-call(s32[4,128]{1,0:T(4,128)S(1)} %bitcast.59, s32[4,128]{1,0:T(4,128)S(1)} %bitcast.84, f32[64,16,128]{2,1,0:T(8,128)} %get-tuple-element.142.kept_ref, f32[64,16,128]{2,1,0:T(8,128)S(1)} %collective-permute-done.37.recv_ref, ...), custom_call_target="tpu_custom_call", output_to_operand_aliasing={{0}: (5, {})} | custom-call | flops 4400000000 | tf_op jit(solution)/shard_map/c112k4/pallas_call | solution.py:51
  285.9 5.2 %collective-permute-done.41.refs_1_ = f32[2,4,16,512]{3,2,1,0:T(8,128)S(1)} collective-permute-done((f32[2,4,16,512]{3,2,1,0:T(8,128)S(1)}, f32[2,4,16,512]{3,2,1,0:T(8,128)S(1)}, u32[]{:S(2)}, u32[]{:S(2)}) %collective-permute-start.41) | collective-permute-done | bytes 262176 | tf_op jit(solution)/shard_map/g96pc/ppermute | solution.py:455
  292.3 6.1 %u1_.1 = (f32[4,128,4096]{2,1,0:T(8,128)}, f32[8,128]{1,0:T(8,128)}) custom-call(s32[5]{0:T(128)S(1)} %copy-done.21, bf16[512,512]{1,0:T(8,128)(2,1)S(1)} %get-tuple-element.112.refs_2_.inv_ref, bf16[512,512]{1,0:T(8,128)(2,1)S(1)} %copy-done.3, f32[2,4,16,512]{3,2,1,0:T(8,128)S(1)} %get-tuple-element.154.refs_0_.refs_8_, ...), custom_call_target="tpu_custom_call", output_to_operand_aliasing={{0}: (12, {})} | custom-call | tf_op jit(solution)/shard_map/u1/pallas_call | solution.py:51
  (187 shorter events, 119.1 us)
Async XLA Ops:
  6.5 84.6 %reduce-scatter.3.cloned.1.call-start = ((), (), s32[]{:S(2)}) async-start(), calls=%async_computation.2 | async-start | bytes 2621440 | tf_op jit(solution)/shard_map/q0zs/reduce_scatter | solution.py:477
  21.7 28.3 %collective-permute-start.7 = (f32[64,24,128]{2,1,0:T(8,128)S(1)}, f32[64,24,128]{2,1,0:T(8,128)S(1)}, u32[]{:S(2)}, u32[]{:S(2)}) collective-permute-start(f32[64,24,128]{2,1,0:T(8,128)S(1)} %get-tuple-element.85.refs_2_), channel_id=1, source_target_pairs={{0,16},{8,24},{16,0},{24,8},{32,48},{40,56},{48,32},{56,40},{64,80... | collective-permute-start | bytes 2359304 | tf_op jit(solution)/shard_map/c24p1/ppermute | solution.py:414
  29.4 37.3 %collective-permute-start.11 = (f32[64,24,128]{2,1,0:T(8,128)S(1)}, f32[64,24,128]{2,1,0:T(8,128)}, u32[]{:S(2)}, u32[]{:S(2)}) collective-permute-start(f32[64,24,128]{2,1,0:T(8,128)S(1)} %get-tuple-element.87.refs_2_), channel_id=1, source_target_pairs={{0,16},{8,24},{16,0},{24,8},{32,48},{40,56},{48,32},{56,40},{64,80... | collective-permute-start | bytes 2359304 | tf_op jit(solution)/shard_map/c0p1/ppermute | solution.py:414
  40.1 19.6 %collective-permute-start.6 = (f32[64,64,128]{2,1,0:T(8,128)S(1)}, f32[64,64,128]{2,1,0:T(8,128)S(1)}, u32[]{:S(2)}, u32[]{:S(2)}) collective-permute-start(f32[64,64,128]{2,1,0:T(8,128)S(1)} %get-tuple-element.89), channel_id=1, source_target_pairs={{0,8},{8,0},{16,24},{24,16},{32,40},{40,32},{48,56},{56,48},{64,72... | collective-permute-start | bytes 6291464 | tf_op jit(solution)/shard_map/q0core/ppermute | solution.py:414
  49.5 27.8 %collective-permute-start.9 = (f32[64,64,128]{2,1,0:T(8,128)}, f32[64,64,128]{2,1,0:T(8,128)}, u32[]{:S(2)}, u32[]{:S(2)}) collective-permute-start(f32[64,64,128]{2,1,0:T(8,128)} %get-tuple-element.95), channel_id=1, source_target_pairs={{0,8},{8,0},{16,24},{24,16},{32,40},{40,32},{48,56},{56,48},{64,72... | collective-permute-start | bytes 6291464 | tf_op jit(solution)/shard_map/q1core/ppermute | solution.py:414
  53.3 27.2 %collective-permute-start.8 = (f32[64,24,128]{2,1,0:T(8,128)}, f32[64,24,128]{2,1,0:T(8,128)}, u32[]{:S(2)}, u32[]{:S(2)}) collective-permute-start(f32[64,24,128]{2,1,0:T(8,128)} %get-tuple-element.92._), channel_id=1, source_target_pairs={{0,32},{8,40},{16,48},{24,56},{32,0},{40,8},{48,16},{56,24},{64,96... | collective-permute-start | bytes 2359304 | tf_op jit(solution)/shard_map/c24p2/ppermute | solution.py:414
  59.6 34.2 %collective-permute-start.15 = (f32[64,24,128]{2,1,0:T(8,128)}, f32[64,24,128]{2,1,0:T(8,128)}, u32[]{:S(2)}, u32[]{:S(2)}) collective-permute-start(f32[64,24,128]{2,1,0:T(8,128)} %get-tuple-element.93.refs_2_), channel_id=1, source_target_pairs={{0,8},{8,0},{16,24},{24,16},{32,40},{40,32},{48,56},{56,48},{64,72... | collective-permute-start | bytes 2359304 | tf_op jit(solution)/shard_map/c48p0/ppermute | solution.py:414
  61.3 61.9 %reduce-scatter.5.cloned.1.call-start = ((), (), s32[]{:S(2)}) async-start(), calls=%async_computation.3 | async-start | bytes 2621440 | tf_op jit(solution)/shard_map/q1zs/reduce_scatter | solution.py:477
  70.3 33.3 %collective-permute-start.13 = (f32[64,24,128]{2,1,0:T(8,128)}, f32[64,24,128]{2,1,0:T(8,128)}, u32[]{:S(2)}, u32[]{:S(2)}) collective-permute-start(f32[64,24,128]{2,1,0:T(8,128)} %get-tuple-element.99._), channel_id=1, source_target_pairs={{0,32},{8,40},{16,48},{24,56},{32,0},{40,8},{48,16},{56,24},{64,96... | collective-permute-start | bytes 2359304 | tf_op jit(solution)/shard_map/c0p2/ppermute | solution.py:414
  73.9 26.4 %collective-permute-start.14 = (f32[64,16,128]{2,1,0:T(8,128)S(1)}, f32[64,16,128]{2,1,0:T(8,128)}, u32[]{:S(2)}, u32[]{:S(2)}) collective-permute-start(f32[64,16,128]{2,1,0:T(8,128)S(1)} %get-tuple-element.100._), channel_id=1, source_target_pairs={{0,8},{8,0},{16,24},{24,16},{32,40},{40,32},{48,56},{56,48},{64,72... | collective-permute-start | bytes 1572872 | tf_op jit(solution)/shard_map/c96p0/ppermute | solution.py:414
  80.5 126.5 %all-gather.3.cloned.1.call-start = ((), (), s32[]{:S(2)}) async-start(), calls=%async_computation.4 | async-start | bytes 2621440 | tf_op jit(solution)/shard_map/q0gz/all_gather | solution.py:487
  92.3 15.0 %collective-permute-start.12 = (f32[8,64,128]{2,1,0:T(8,128)S(1)}, f32[8,64,128]{2,1,0:T(8,128)S(1)}, u32[]{:S(2)}, u32[]{:S(2)}) collective-permute-start(f32[8,64,128]{2,1,0:T(8,128)S(1)} %get-tuple-element.104), channel_id=1, source_target_pairs={{0,64},{8,72},{16,80},{24,88},{32,96},{40,104},{48,112},{56,120},{... | collective-permute-start | bytes 786440 | tf_op jit(solution)/shard_map/q0y/ppermute | solution.py:414
  108.8 24.8 %collective-permute-start.19 = (f32[64,24,128]{2,1,0:T(8,128)}, f32[64,24,128]{2,1,0:T(8,128)}, u32[]{:S(2)}, u32[]{:S(2)}) collective-permute-start(f32[64,24,128]{2,1,0:T(8,128)} %get-tuple-element.108._), channel_id=1, source_target_pairs={{0,16},{8,24},{16,0},{24,8},{32,48},{40,56},{48,32},{56,40},{64,80... | collective-permute-start | bytes 2359304 | tf_op jit(solution)/shard_map/c48p1/ppermute | solution.py:414
  109.4 30.6 %collective-permute-start.21 = (f32[64,24,128]{2,1,0:T(8,128)}, f32[64,24,128]{2,1,0:T(8,128)S(1)}, u32[]{:S(2)}, u32[]{:S(2)}) collective-permute-start(f32[64,24,128]{2,1,0:T(8,128)} %get-tuple-element.111.refs_2_), channel_id=1, source_target_pairs={{0,64},{8,72},{16,80},{24,88},{32,96},{40,104},{48,112},{56,120},{... | collective-permute-start | bytes 2359304 | tf_op jit(solution)/shard_map/c0p3/ppermute | solution.py:414
  116.6 20.6 %collective-permute-start.18 = (f32[8,64,128]{2,1,0:T(8,128)S(1)}, f32[8,64,128]{2,1,0:T(8,128)S(1)}, u32[]{:S(2)}, u32[]{:S(2)}) collective-permute-start(f32[8,64,128]{2,1,0:T(8,128)S(1)} %q0d.1.refs_1_.refs_0_), channel_id=1, source_target_pairs={{0,48},{8,56},{16,32},{24,40},{32,16},{40,24},{48,0},{56,8},{64,11... | collective-permute-start | bytes 786440 | tf_op jit(solution)/shard_map/q0xb/ppermute | solution.py:414
  119.3 27.3 %collective-permute-start.25 = (f32[64,16,128]{2,1,0:T(8,128)S(1)}, f32[64,16,128]{2,1,0:T(8,128)}, u32[]{:S(2)}, u32[]{:S(2)}) collective-permute-start(f32[64,16,128]{2,1,0:T(8,128)S(1)} %get-tuple-element.110._), channel_id=1, source_target_pairs={{0,16},{8,24},{16,0},{24,8},{32,48},{40,56},{48,32},{56,40},{64,80... | collective-permute-start | bytes 1572872 | tf_op jit(solution)/shard_map/c96p1/ppermute | solution.py:414
  139.4 27.8 %collective-permute-start.23 = (f32[64,24,128]{2,1,0:T(8,128)S(1)}, f32[64,24,128]{2,1,0:T(8,128)}, u32[]{:S(2)}, u32[]{:S(2)}) collective-permute-start(f32[64,24,128]{2,1,0:T(8,128)S(1)} %get-tuple-element.101.refs_2_), channel_id=1, source_target_pairs={{0,16},{8,24},{16,0},{24,8},{32,48},{40,56},{48,32},{56,40},{64,80... | collective-permute-start | bytes 2359304 | tf_op jit(solution)/shard_map/c72p1/ppermute | solution.py:414
  153.0 20.9 %collective-permute-start.30 = (f32[64,24,128]{2,1,0:T(8,128)}, f32[64,24,128]{2,1,0:T(8,128)}, u32[]{:S(2)}, u32[]{:S(2)}) collective-permute-start(f32[64,24,128]{2,1,0:T(8,128)} %get-tuple-element.102.refs_1_), channel_id=1, source_target_pairs={{0,64},{8,72},{16,80},{24,88},{32,96},{40,104},{48,112},{56,120},{... | collective-permute-start | bytes 2359304 | tf_op jit(solution)/shard_map/c24p3/ppermute | solution.py:414
  154.4 31.7 %collective-permute-start.28 = (f32[64,24,128]{2,1,0:T(8,128)}, f32[64,24,128]{2,1,0:T(8,128)S(1)}, u32[]{:S(2)}, u32[]{:S(2)}) collective-permute-start(f32[64,24,128]{2,1,0:T(8,128)} %get-tuple-element.117.refs_2_), channel_id=1, source_target_pairs={{0,32},{8,40},{16,48},{24,56},{32,0},{40,8},{48,16},{56,24},{64,96... | collective-permute-start | bytes 2359304 | tf_op jit(solution)/shard_map/c48p2/ppermute | solution.py:414
  155.3 77.5 %all-gather.5.cloned.1.call-start = ((), (), s32[]{:S(2)}) async-start(), calls=%async_computation.5 | async-start | bytes 2621440 | tf_op jit(solution)/shard_map/q1gz/all_gather | solution.py:487
  159.7 18.4 %collective-permute-start.29 = (f32[8,64,128]{2,1,0:T(8,128)S(1)}, f32[8,64,128]{2,1,0:T(8,128)S(1)}, u32[]{:S(2)}, u32[]{:S(2)}) collective-permute-start(f32[8,64,128]{2,1,0:T(8,128)S(1)} %q1e.1._.refs_0_), channel_id=1, source_target_pairs={{0,64},{8,72},{16,80},{24,88},{32,96},{40,104},{48,112},{56,120},{... | collective-permute-start | bytes 786440 | tf_op jit(solution)/shard_map/q1gy/ppermute | solution.py:414
  170.9 32.0 %collective-permute-start.27 = (f32[64,24,128]{2,1,0:T(8,128)}, f32[64,24,128]{2,1,0:T(8,128)S(1)}, u32[]{:S(2)}, u32[]{:S(2)}) collective-permute-start(f32[64,24,128]{2,1,0:T(8,128)} %get-tuple-element.125.refs_0_), channel_id=1, source_target_pairs={{0,32},{8,40},{16,48},{24,56},{32,0},{40,8},{48,16},{56,24},{64,96... | collective-permute-start | bytes 2359304 | tf_op jit(solution)/shard_map/c72p2/ppermute | solution.py:414
  189.5 27.7 %collective-permute-start.33 = (f32[64,24,128]{2,1,0:T(8,128)}, f32[64,24,128]{2,1,0:T(8,128)}, u32[]{:S(2)}, u32[]{:S(2)}) collective-permute-start(f32[64,24,128]{2,1,0:T(8,128)} %get-tuple-element.129._), channel_id=1, source_target_pairs={{0,64},{8,72},{16,80},{24,88},{32,96},{40,104},{48,112},{56,120},{... | collective-permute-start | bytes 2359304 | tf_op jit(solution)/shard_map/c48p3/ppermute | solution.py:414
  190.2 18.6 %collective-permute-start.16 = (f32[64,16,128]{2,1,0:T(8,128)}, f32[64,16,128]{2,1,0:T(8,128)}, u32[]{:S(2)}, u32[]{:S(2)}) collective-permute-start(f32[64,16,128]{2,1,0:T(8,128)} %get-tuple-element.109._), channel_id=1, source_target_pairs={{0,8},{8,0},{16,24},{24,16},{32,40},{40,32},{48,56},{56,48},{64,72... | collective-permute-start | bytes 1572872 | tf_op jit(solution)/shard_map/c112p0/ppermute | solution.py:414
  190.3 23.6 %collective-permute-start.34 = (f32[64,16,128]{2,1,0:T(8,128)}, f32[64,16,128]{2,1,0:T(8,128)}, u32[]{:S(2)}, u32[]{:S(2)}) collective-permute-start(f32[64,16,128]{2,1,0:T(8,128)} %get-tuple-element.123.refs_2_), channel_id=1, source_target_pairs={{0,32},{8,40},{16,48},{24,56},{32,0},{40,8},{48,16},{56,24},{64,96... | collective-permute-start | bytes 1572872 | tf_op jit(solution)/shard_map/c96p2/ppermute | solution.py:414
  206.4 17.1 %collective-permute-start.32 = (f32[64,24,128]{2,1,0:T(8,128)}, f32[64,24,128]{2,1,0:T(8,128)}, u32[]{:S(2)}, u32[]{:S(2)}) collective-permute-start(f32[64,24,128]{2,1,0:T(8,128)} %get-tuple-element.130.refs_1_), channel_id=1, source_target_pairs={{0,64},{8,72},{16,80},{24,88},{32,96},{40,104},{48,112},{56,120},{... | collective-permute-start | bytes 2359304 | tf_op jit(solution)/shard_map/c72p3/ppermute | solution.py:414
  212.0 16.8 %collective-permute-start.31 = (f32[64,16,128]{2,1,0:T(8,128)S(1)}, f32[64,16,128]{2,1,0:T(8,128)S(1)}, u32[]{:S(2)}, u32[]{:S(2)}) collective-permute-start(f32[64,16,128]{2,1,0:T(8,128)S(1)} %get-tuple-element.132._), channel_id=1, source_target_pairs={{0,16},{8,24},{16,0},{24,8},{32,48},{40,56},{48,32},{56,40},{64,80... | collective-permute-start | bytes 1572872 | tf_op jit(solution)/shard_map/c112p1/ppermute | solution.py:414
  235.7 24.4 %collective-permute-start.40 = (f32[64,64,128]{2,1,0:T(8,128)S(1)}, f32[64,64,128]{2,1,0:T(8,128)S(1)}, u32[]{:S(2)}, u32[]{:S(2)}) collective-permute-start(f32[64,64,128]{2,1,0:T(8,128)S(1)} %q0low.1._.low_ref), channel_id=1, source_target_pairs={{0,8},{8,0},{16,24},{24,16},{32,40},{40,32},{48,56},{56,48},{64,72... | collective-permute-start | bytes 6291464 | tf_op jit(solution)/shard_map/q0high/ppermute | solution.py:414
  236.2 25.6 %collective-permute-start.39 = (f32[4,4,24,512]{3,2,1,0:T(8,128)S(1)}, f32[4,4,24,512]{3,2,1,0:T(8,128)S(1)}, u32[]{:S(2)}, u32[]{:S(2)}) collective-permute-start(f32[4,4,24,512]{3,2,1,0:T(8,128)S(1)} %get-tuple-element.138._.refs_0_), channel_id=1, source_target_pairs={{0,1},{2,3},{4,5},{6,7},{8,9},{10,11},{12,13},{14,15},{16,17},{18,... | collective-permute-start | bytes 2359304 | tf_op jit(solution)/shard_map/g0pc/ppermute | solution.py:455
  240.9 15.2 %collective-permute-start.35 = (f32[64,16,128]{2,1,0:T(8,128)S(1)}, f32[64,16,128]{2,1,0:T(8,128)S(1)}, u32[]{:S(2)}, u32[]{:S(2)}) collective-permute-start(f32[64,16,128]{2,1,0:T(8,128)S(1)} %copy-done.29), channel_id=1, source_target_pairs={{0,32},{8,40},{16,48},{24,56},{32,0},{40,8},{48,16},{56,24},{64,96... | collective-permute-start | bytes 1572872 | tf_op jit(solution)/shard_map/c112p2/ppermute | solution.py:414
  241.9 29.8 %collective-permute-start.38 = (f32[64,16,128]{2,1,0:T(8,128)S(1)}, f32[64,16,128]{2,1,0:T(8,128)S(1)}, u32[]{:S(2)}, u32[]{:S(2)}) collective-permute-start(f32[64,16,128]{2,1,0:T(8,128)S(1)} %copy-done.24), channel_id=1, source_target_pairs={{0,64},{8,72},{16,80},{24,88},{32,96},{40,104},{48,112},{56,120},{... | collective-permute-start | bytes 1572872 | tf_op jit(solution)/shard_map/c96p3/ppermute | solution.py:414
  259.8 21.3 %collective-permute-start.37 = (f32[64,16,128]{2,1,0:T(8,128)S(1)}, f32[64,16,128]{2,1,0:T(8,128)S(1)}, u32[]{:S(2)}, u32[]{:S(2)}) collective-permute-start(f32[64,16,128]{2,1,0:T(8,128)S(1)} %get-tuple-element.143._), channel_id=1, source_target_pairs={{0,64},{8,72},{16,80},{24,88},{32,96},{40,104},{48,112},{56,120},{... | collective-permute-start | bytes 1572872 | tf_op jit(solution)/shard_map/c112p3/ppermute | solution.py:414
  (46 other events, 205.3 us)
Sparse Core Ops, SparseCore 0:
  61.4 29.7 reduce-scatter.2
  93.7 29.4 reduce-scatter.4
  155.4 30.0 all-gather.2
  190.3 28.5 all-gather.4

commit v5 on v4

--- a/solution.py
+++ b/solution.py
@@ -47,7 +47,7 @@
 FLOPS = [0]
 
 
-def run(body, ins, outs, scratch, limit=16, **more):
+def run(body, ins, outs, scratch, limit=32, **more):
     return pl.pallas_call(
         body,
         in_specs=[ANY if s is HBM else s for _, s in ins],
@@ -82,7 +82,7 @@
     return run(
         body,
         [(split, SMEM), (tiles, ANY), (tok, ANY)],
-        [((HALF, rows, TB), F32, ANY), ((HALF, rows, TB), F32, HBM)],
+        [((HALF, rows, TB), F32, ANY)] * 2,
         [pltpu.VMEM((K, rows, TB), F32), pltpu.VMEM((K, rows, TB), F32), DMA((3,))],
     )
 
@@ -116,8 +116,8 @@
 
     return run(
         body,
-        [(split, SMEM), (first, SMEM), (second, SMEM), (kept, HBM), (recv, ANY), (tok, ANY)],
-        [((HALF, rows, TB), F32, ANY), ((HALF, rows, TB), F32, HBM)],
+        [(split, SMEM), (first, SMEM), (second, SMEM), (kept, ANY), (recv, ANY), (tok, ANY)],
+        [((HALF, rows, TB), F32, ANY)] * 2,
         [pltpu.VMEM((K, rows, TB), F32), pltpu.VMEM((K, rows, TB), F32), DMA((4,))],
     )
 
@@ -149,7 +149,7 @@
         one.wait()
         two.wait()
 
-    ins = [(first, SMEM), (second, SMEM), (kept, HBM), (recv, ANY), (tok, ANY)]
+    ins = [(first, SMEM), (second, SMEM), (kept, ANY), (recv, ANY), (tok, ANY)]
     more = {}
     if before is not None:
         ins.append((before, ANY))

time: 309 us -> 303 us (0.981)
  Pallas kernels: 148 us -> 122 us
  local copies, waits for them, and re-layouts: 19.7 us -> 34 us
  waiting for transfers between devices: 79.7 us -> 83.8 us
    pallas_call x56, Pallas kernels: 148 us -> 122 us  [run(): pl.pallas_call(body, in_specs=[ANY if s is HBM else s for _, s in ins], o...]
    unnamed x66 -> x132, local copies, waits for them, and re-layouts: 19.6 us -> 33.9 us
    ppermute x40, waiting for transfers between devices: 63.9 us -> 67.8 us  [flip(): lax.ppermute(v, axis, [(i, i ^ bits) for i in range(lax.axis_size(axis))])]
  transfers between devices with their start and end apart: 46 -> 46, of which waited for: 16 -> 18; matrix products, arithmetic and copies ran while one was open for 0% -> 0% of each run, Pallas kernels for 44% -> 37%
where the time goes in v5:
time: 303 us; the launch traced here: 300 us
  Pallas kernels  122 us (40%)
  waiting for transfers between devices  83.8 us (28%)
  starting transfers between devices  45.5 us (15%)
  local copies, waits for them, and re-layouts  34 us (11%)
  between operations  14.1 us (5%)
    pallas_call x56, Pallas kernels, run(): pl.pallas_call(body, in_specs=[ANY if s is HBM else s for _, s in ins], o...  122 us
    ppermute x40, waiting for transfers between devices, flip(): lax.ppermute(v, axis, [(i, i ^ bits) for i in range(lax.axis_size(axis))])  67.8 us
    ppermute x40, starting transfers between devices, flip(): lax.ppermute(v, axis, [(i, i ^ bits) for i in range(lax.axis_size(axis))])  39.7 us
    unnamed x132, local copies, waits for them, and re-layouts  33.9 us
    reduce_scatter x2, waiting for transfers between devices, part_steps(): lax.psum_scatter(v, 'row', tiled=True)  10.7 us
  transfers between devices with their start and end apart: 46, of which 18 were waited for; matrix products, arithmetic and copies ran while one was open for 0% of the time, Pallas kernels for 37%

profile of v5, /device:TPU:0, one launch (start us, length us, event | category | flops | bytes accessed | tf_op | source)
XLA Modules:
  0.0 299.7 jit_solution(17379926291738841654)
XLA Ops:
  15.9 3.2 %collective-permute-start.2 = (s32[2,16,128]{2,1,0:T(8,128)S(1)}, s32[2,16,128]{2,1,0:T(8,128)S(1)}, u32[]{:S(2)}, u32[]{:S(2)}) collective-permute-start(s32[2,16,128]{2,1,0:T(8,128)S(1)} %l1.1.refs_0_.refs_2_), channel_id=1, source_target_pairs={{0,32},{8,40},{16,48},{24,56},{32,0},{40,8},{48,16},{56,24},{64,96... | collective-permute-start | bytes 49160 | tf_op jit(solution)/shard_map/lp1/ppermute | solution.py:414
  28.8 7.9 %q0t.1 = (f32[64,64,128]{2,1,0:T(8,128)S(1)}, f32[64,64,128]{2,1,0:T(8,128)S(1)}) custom-call(f32[128,128]{1,0:T(8,128)S(1)} %weight.1.weight_ref._, f32[128,128,128]{2,1,0:T(8,128)} %bitcast.87, f32[128,128]{1,0:T(8,128)S(1)} %weight.1.weight_ref._), custom_call_target="tpu_custom_call" | custom-call | tf_op jit(solution)/shard_map/q0t/pallas_call | solution.py:51
  37.0 9.1 %q1t.1 = (f32[64,64,128]{2,1,0:T(8,128)S(1)}, f32[64,64,128]{2,1,0:T(8,128)}) custom-call(f32[128,128]{1,0:T(8,128)S(1)} %weight.1.weight_ref._, f32[128,128,128]{2,1,0:T(8,128)} %bitcast.88, f32[64,64,128]{2,1,0:T(8,128)S(1)} %get-tuple-element.88._.refs_0_), custom_call_target="tpu_custom_call" | custom-call | tf_op jit(solution)/shard_map/q1t/pallas_call | solution.py:51
  51.3 3.0 c48k0.1
  61.3 3.1 %c0k2.1 = (f32[64,24,128]{2,1,0:T(8,128)}, f32[64,24,128]{2,1,0:T(8,128)S(1)}) custom-call(s32[4,128]{1,0:T(4,128)S(1)} %bitcast.18, s32[4,128]{1,0:T(4,128)S(1)} %bitcast.39, s32[4,128]{1,0:T(4,128)S(1)} %bitcast.64, f32[64,24,128]{2,1,0:T(8,128)S(1)} %copy-done.64, f32[64,24,128]{2,1,0:T(8,128)} %collective-permute-done.11.recv_ref, ...), custom_call_target="tpu_custom_call" | custom-call | flops 17600000000 | tf_op jit(solution)/shard_map/c0k2/pallas_call | solution.py:51
  71.6 3.2 %q1a.1._ = f32[64,64,128]{2,1,0:T(8,128)} custom-call(f32[64,64,128]{2,1,0:T(8,128)S(1)} %get-tuple-element.91._.refs_0_, f32[64,64,128]{2,1,0:T(8,128)} %collective-permute-done.9.refs_1_, f32[64,24,128]{2,1,0:T(8,128)S(1)} %get-tuple-element.101.refs_2_), custom_call_target="tpu_custom_call" | custom-call | tf_op jit(solution)/shard_map/q1a/pallas_call | solution.py:51
  76.0 3.1 %c24k3.1 = (f32[64,24,128]{2,1,0:T(8,128)}, f32[64,24,128]{2,1,0:T(8,128)S(1)}) custom-call(s32[4,128]{1,0:T(4,128)S(1)} %bitcast.21, s32[4,128]{1,0:T(4,128)S(1)} %bitcast.41, s32[4,128]{1,0:T(4,128)S(1)} %bitcast.66, f32[64,24,128]{2,1,0:T(8,128)S(1)} %copy-done.62, f32[64,24,128]{2,1,0:T(8,128)} %collective-permute-done.8.recv_ref, f32[64,64,128]{2,1,0:T(8,128)} %q1a.1._), custom_call_target="tpu_custom_call" | custom-call | flops 17600000000 | tf_op jit(solution)/shard_map/c24k3/pallas_call | solution.py:51
  79.2 8.4 %reduce-scatter.3.cloned.1.call-done.refs_0_ = f32[16,64,128]{2,1,0:T(8,128)} async-done(((f32[64,64,128]{2,1,0:T(8,128)}), f32[16,64,128]{2,1,0:T(8,128)}) %reduce-scatter.3.cloned.1.call-update) | async-done | bytes 524304 | tf_op jit(solution)/shard_map/q0zs/reduce_scatter | solution.py:477
  90.2 3.0 c48k1.1
  94.1 2.7 c112k0.1
  100.9 3.1 %c0k3.1 = (f32[64,24,128]{2,1,0:T(8,128)}, f32[64,24,128]{2,1,0:T(8,128)S(1)}) custom-call(s32[4,128]{1,0:T(4,128)S(1)} %bitcast.25, s32[4,128]{1,0:T(4,128)S(1)} %bitcast.44, s32[4,128]{1,0:T(4,128)S(1)} %bitcast.69, f32[64,24,128]{2,1,0:T(8,128)S(1)} %copy-done.46, f32[64,24,128]{2,1,0:T(8,128)} %collective-permute-done.13.recv_ref, ...), custom_call_target="tpu_custom_call" | custom-call | flops 1100000000 | tf_op jit(solution)/shard_map/c0k3/pallas_call | solution.py:51
  108.8 5.4 %collective-permute-done.17.refs_1_ = f32[8,64,128]{2,1,0:T(8,128)S(1)} collective-permute-done((f32[8,64,128]{2,1,0:T(8,128)S(1)}, f32[8,64,128]{2,1,0:T(8,128)S(1)}, u32[]{:S(2)}, u32[]{:S(2)}) %collective-permute-start.17) | collective-permute-done | bytes 262176 | tf_op jit(solution)/shard_map/q0xa/ppermute | solution.py:414
  114.3 2.8 collective-permute-start.18
  122.3 8.9 %collective-permute-done.19.recv_ref = f32[64,24,128]{2,1,0:T(8,128)} collective-permute-done((f32[64,24,128]{2,1,0:T(8,128)}, f32[64,24,128]{2,1,0:T(8,128)}, u32[]{:S(2)}, u32[]{:S(2)}) %collective-permute-start.19) | collective-permute-done | bytes 786464 | tf_op jit(solution)/shard_map/c48p1/ppermute | solution.py:414
  131.2 3.1 %c48k2.1 = (f32[64,24,128]{2,1,0:T(8,128)}, f32[64,24,128]{2,1,0:T(8,128)S(1)}) custom-call(s32[4,128]{1,0:T(4,128)S(1)} %bitcast.26, s32[4,128]{1,0:T(4,128)S(1)} %bitcast.45, s32[4,128]{1,0:T(4,128)S(1)} %bitcast.70, f32[64,24,128]{2,1,0:T(8,128)S(1)} %copy-done.50, f32[64,24,128]{2,1,0:T(8,128)} %collective-permute-done.19.recv_ref, ...), custom_call_target="tpu_custom_call" | custom-call | flops 1100000000 | tf_op jit(solution)/shard_map/c48k2/pallas_call | solution.py:51
  140.2 2.8 c0k4.1
  144.9 2.9 c96k2.1
  159.4 5.5 %collective-permute-done.23.recv_ref = f32[64,24,128]{2,1,0:T(8,128)} collective-permute-done((f32[64,24,128]{2,1,0:T(8,128)S(1)}, f32[64,24,128]{2,1,0:T(8,128)}, u32[]{:S(2)}, u32[]{:S(2)}) %collective-permute-start.23) | collective-permute-done | bytes 786464 | tf_op jit(solution)/shard_map/c72p1/ppermute | solution.py:414
  164.9 3.1 %c72k2.1 = (f32[64,24,128]{2,1,0:T(8,128)}, f32[64,24,128]{2,1,0:T(8,128)S(1)}) custom-call(s32[4,128]{1,0:T(4,128)S(1)} %bitcast.28, s32[4,128]{1,0:T(4,128)S(1)} %bitcast.48, s32[4,128]{1,0:T(4,128)S(1)} %bitcast.73, f32[64,24,128]{2,1,0:T(8,128)S(1)} %copy-done.34, f32[64,24,128]{2,1,0:T(8,128)} %collective-permute-done.23.recv_ref, ...), custom_call_target="tpu_custom_call" | custom-call | flops 17600000000 | tf_op jit(solution)/shard_map/c72k2/pallas_call | solution.py:51
  168.9 3.0 %collective-permute-start.27 = (f32[64,24,128]{2,1,0:T(8,128)}, f32[64,24,128]{2,1,0:T(8,128)S(1)}, u32[]{:S(2)}, u32[]{:S(2)}) collective-permute-start(f32[64,24,128]{2,1,0:T(8,128)} %get-tuple-element.125.refs_0_), channel_id=1, source_target_pairs={{0,32},{8,40},{16,48},{24,56},{32,0},{40,8},{48,16},{56,24},{64,96... | collective-permute-start | bytes 2359304 | tf_op jit(solution)/shard_map/c72p2/ppermute | solution.py:414
  171.9 3.9 %c24k4.1 = (f32[4,4,24,512]{3,2,1,0:T(8,128)S(1)}, f32[4,24,4096]{2,1,0:T(8,128)}) custom-call(s32[4,128]{1,0:T(4,128)S(1)} %bitcast.49, s32[4,128]{1,0:T(4,128)S(1)} %bitcast.74, f32[64,24,128]{2,1,0:T(8,128)S(1)} %copy-done.60, f32[64,24,128]{2,1,0:T(8,128)} %collective-permute-done.30.recv_ref, ...), custom_call_target="tpu_custom_call", output_to_operand_aliasing={{0}: (5, {})} | custom-call | flops 17600000000 | tf_op jit(solution)/shard_map/c24k4/pallas_call | solution.py:51
  176.7 7.3 %collective-permute-done.28.recv_ref = f32[64,24,128]{2,1,0:T(8,128)} collective-permute-done((f32[64,24,128]{2,1,0:T(8,128)}, f32[64,24,128]{2,1,0:T(8,128)}, u32[]{:S(2)}, u32[]{:S(2)}) %collective-permute-start.28) | collective-permute-done | bytes 786464 | tf_op jit(solution)/shard_map/c48p2/ppermute | solution.py:414
  183.9 3.1 %c48k3.1 = (f32[64,24,128]{2,1,0:T(8,128)}, f32[64,24,128]{2,1,0:T(8,128)S(1)}) custom-call(s32[4,128]{1,0:T(4,128)S(1)} %bitcast.29, s32[4,128]{1,0:T(4,128)S(1)} %bitcast.50, s32[4,128]{1,0:T(4,128)S(1)} %bitcast.75, f32[64,24,128]{2,1,0:T(8,128)S(1)} %copy-done.19, f32[64,24,128]{2,1,0:T(8,128)} %collective-permute-done.28.recv_ref, f32[16,64,128]{2,1,0:T(8,128)} %q1h.1._), custom_call_target="tpu_custom_call" | custom-call | tf_op jit(solution)/shard_map/c48k3/pallas_call | solution.py:51
  189.5 11.2 %collective-permute-done.27.recv_ref = f32[64,24,128]{2,1,0:T(8,128)S(1)} collective-permute-done((f32[64,24,128]{2,1,0:T(8,128)}, f32[64,24,128]{2,1,0:T(8,128)S(1)}, u32[]{:S(2)}, u32[]{:S(2)}) %collective-permute-start.27) | collective-permute-done | bytes 786464 | tf_op jit(solution)/shard_map/c72p2/ppermute | solution.py:414
  213.8 3.9 %c48k4.1 = (f32[4,4,24,512]{3,2,1,0:T(8,128)S(1)}, f32[4,24,4096]{2,1,0:T(8,128)}) custom-call(s32[4,128]{1,0:T(4,128)S(1)} %bitcast.54, s32[4,128]{1,0:T(4,128)S(1)} %bitcast.79, f32[64,24,128]{2,1,0:T(8,128)S(1)} %copy-done.36, f32[64,24,128]{2,1,0:T(8,128)} %collective-permute-done.33.recv_ref, ...), custom_call_target="tpu_custom_call", output_to_operand_aliasing={{0}: (5, {})} | custom-call | flops 17600000000 | tf_op jit(solution)/shard_map/c48k4/pallas_call | solution.py:51
  223.2 4.0 %c72k4.1 = (f32[4,4,24,512]{3,2,1,0:T(8,128)S(1)}, f32[4,24,4096]{2,1,0:T(8,128)}) custom-call(s32[4,128]{1,0:T(4,128)S(1)} %bitcast.55, s32[4,128]{1,0:T(4,128)S(1)} %bitcast.80, f32[64,24,128]{2,1,0:T(8,128)S(1)} %copy-done.56, f32[64,24,128]{2,1,0:T(8,128)} %collective-permute-done.32.recv_ref, ...), custom_call_target="tpu_custom_call", output_to_operand_aliasing={{0}: (5, {})} | custom-call | flops 8800000000 | tf_op jit(solution)/shard_map/c72k4/pallas_call | solution.py:51
  232.2 4.4 %collective-permute-start.39 = (f32[4,4,24,512]{3,2,1,0:T(8,128)S(1)}, f32[4,4,24,512]{3,2,1,0:T(8,128)S(1)}, u32[]{:S(2)}, u32[]{:S(2)}) collective-permute-start(f32[4,4,24,512]{3,2,1,0:T(8,128)S(1)} %get-tuple-element.138._.refs_0_), channel_id=1, source_target_pairs={{0,1},{2,3},{4,5},{6,7},{8,9},{10,11},{12,13},{14,15},{16,17},{18,... | collective-permute-start | bytes 2359304 | tf_op jit(solution)/shard_map/g0pc/ppermute | solution.py:455
  239.5 12.5 %collective-permute-done.35.recv_ref = f32[64,16,128]{2,1,0:T(8,128)S(1)} collective-permute-done((f32[64,16,128]{2,1,0:T(8,128)}, f32[64,16,128]{2,1,0:T(8,128)S(1)}, u32[]{:S(2)}, u32[]{:S(2)}) %collective-permute-start.35) | collective-permute-done | bytes 524320 | tf_op jit(solution)/shard_map/c112p2/ppermute | solution.py:414
  255.8 9.8 %u0.1 = (f32[4,128,4096]{2,1,0:T(8,128)}, f32[8,128]{1,0:T(8,128)S(1)}) custom-call(s32[5]{0:T(128)S(1)} %copy-done.31, bf16[512,512]{1,0:T(8,128)(2,1)S(1)} %get-tuple-element.112.refs_2_.inv_ref, bf16[512,512]{1,0:T(8,128)(2,1)S(1)} %copy-done.3, f32[4,4,24,512]{3,2,1,0:T(8,128)S(1)} %get-tuple-element.138._.refs_0_, ...), custom_call_target="tpu_custom_call" | custom-call | tf_op jit(solution)/shard_map/u0/pallas_call | solution.py:51
  268.9 7.8 %collective-permute-done.37.recv_ref = f32[64,16,128]{2,1,0:T(8,128)S(1)} collective-permute-done((f32[64,16,128]{2,1,0:T(8,128)S(1)}, f32[64,16,128]{2,1,0:T(8,128)S(1)}, u32[]{:S(2)}, u32[]{:S(2)}) %collective-permute-start.37) | collective-permute-done | bytes 524320 | tf_op jit(solution)/shard_map/c112p3/ppermute | solution.py:414
  280.6 5.2 %collective-permute-done.41.refs_1_ = f32[2,4,16,512]{3,2,1,0:T(8,128)S(1)} collective-permute-done((f32[2,4,16,512]{3,2,1,0:T(8,128)S(1)}, f32[2,4,16,512]{3,2,1,0:T(8,128)S(1)}, u32[]{:S(2)}, u32[]{:S(2)}) %collective-permute-start.41) | collective-permute-done | bytes 262176 | tf_op jit(solution)/shard_map/g96pc/ppermute | solution.py:455
  287.0 6.1 %u1_.1 = (f32[4,128,4096]{2,1,0:T(8,128)}, f32[8,128]{1,0:T(8,128)}) custom-call(s32[5]{0:T(128)S(1)} %copy-done.31, bf16[512,512]{1,0:T(8,128)(2,1)S(1)} %get-tuple-element.112.refs_2_.inv_ref, bf16[512,512]{1,0:T(8,128)(2,1)S(1)} %copy-done.3, f32[2,4,16,512]{3,2,1,0:T(8,128)S(1)} %get-tuple-element.154.refs_0_.refs_8_, ...), custom_call_target="tpu_custom_call", output_to_operand_aliasing={{0}: (12, {})} | custom-call | tf_op jit(solution)/shard_map/u1/pallas_call | solution.py:51
  (253 shorter events, 118.9 us)
Async XLA Ops:
  6.5 81.1 %reduce-scatter.3.cloned.1.call-start = ((), (), s32[]{:S(2)}) async-start(), calls=%async_computation.2 | async-start | bytes 2621440 | tf_op jit(solution)/shard_map/q0zs/reduce_scatter | solution.py:477
  19.1 27.5 %collective-permute-start.7 = (f32[64,24,128]{2,1,0:T(8,128)S(1)}, f32[64,24,128]{2,1,0:T(8,128)S(1)}, u32[]{:S(2)}, u32[]{:S(2)}) collective-permute-start(f32[64,24,128]{2,1,0:T(8,128)S(1)} %get-tuple-element.85.refs_2_), channel_id=1, source_target_pairs={{0,16},{8,24},{16,0},{24,8},{32,48},{40,56},{48,32},{56,40},{64,80... | collective-permute-start | bytes 2359304 | tf_op jit(solution)/shard_map/c24p1/ppermute | solution.py:414
  25.5 35.9 %collective-permute-start.11 = (f32[64,24,128]{2,1,0:T(8,128)S(1)}, f32[64,24,128]{2,1,0:T(8,128)}, u32[]{:S(2)}, u32[]{:S(2)}) collective-permute-start(f32[64,24,128]{2,1,0:T(8,128)S(1)} %get-tuple-element.87.refs_2_), channel_id=1, source_target_pairs={{0,16},{8,24},{16,0},{24,8},{32,48},{40,56},{48,32},{56,40},{64,80... | collective-permute-start | bytes 2359304 | tf_op jit(solution)/shard_map/c0p1/ppermute | solution.py:414
  36.8 18.4 %collective-permute-start.6 = (f32[64,64,128]{2,1,0:T(8,128)S(1)}, f32[64,64,128]{2,1,0:T(8,128)S(1)}, u32[]{:S(2)}, u32[]{:S(2)}) collective-permute-start(f32[64,64,128]{2,1,0:T(8,128)S(1)} %get-tuple-element.89), channel_id=1, source_target_pairs={{0,8},{8,0},{16,24},{24,16},{32,40},{40,32},{48,56},{56,48},{64,72... | collective-permute-start | bytes 6291464 | tf_op jit(solution)/shard_map/q0core/ppermute | solution.py:414
  46.1 25.5 %collective-permute-start.9 = (f32[64,64,128]{2,1,0:T(8,128)}, f32[64,64,128]{2,1,0:T(8,128)}, u32[]{:S(2)}, u32[]{:S(2)}) collective-permute-start(f32[64,64,128]{2,1,0:T(8,128)} %get-tuple-element.95), channel_id=1, source_target_pairs={{0,8},{8,0},{16,24},{24,16},{32,40},{40,32},{48,56},{56,48},{64,72... | collective-permute-start | bytes 6291464 | tf_op jit(solution)/shard_map/q1core/ppermute | solution.py:414
  48.6 26.3 %collective-permute-start.8 = (f32[64,24,128]{2,1,0:T(8,128)}, f32[64,24,128]{2,1,0:T(8,128)}, u32[]{:S(2)}, u32[]{:S(2)}) collective-permute-start(f32[64,24,128]{2,1,0:T(8,128)} %get-tuple-element.92._), channel_id=1, source_target_pairs={{0,32},{8,40},{16,48},{24,56},{32,0},{40,8},{48,16},{56,24},{64,96... | collective-permute-start | bytes 2359304 | tf_op jit(solution)/shard_map/c24p2/ppermute | solution.py:414
  55.2 35.0 %collective-permute-start.15 = (f32[64,24,128]{2,1,0:T(8,128)}, f32[64,24,128]{2,1,0:T(8,128)}, u32[]{:S(2)}, u32[]{:S(2)}) collective-permute-start(f32[64,24,128]{2,1,0:T(8,128)} %get-tuple-element.93.refs_2_), channel_id=1, source_target_pairs={{0,8},{8,0},{16,24},{24,16},{32,40},{40,32},{48,56},{56,48},{64,72... | collective-permute-start | bytes 2359304 | tf_op jit(solution)/shard_map/c48p0/ppermute | solution.py:414
  56.8 62.9 %reduce-scatter.5.cloned.1.call-start = ((), (), s32[]{:S(2)}) async-start(), calls=%async_computation.3 | async-start | bytes 2621440 | tf_op jit(solution)/shard_map/q1zs/reduce_scatter | solution.py:477
  65.3 35.5 %collective-permute-start.13 = (f32[64,24,128]{2,1,0:T(8,128)}, f32[64,24,128]{2,1,0:T(8,128)}, u32[]{:S(2)}, u32[]{:S(2)}) collective-permute-start(f32[64,24,128]{2,1,0:T(8,128)} %get-tuple-element.99._), channel_id=1, source_target_pairs={{0,32},{8,40},{16,48},{24,56},{32,0},{40,8},{48,16},{56,24},{64,96... | collective-permute-start | bytes 2359304 | tf_op jit(solution)/shard_map/c0p2/ppermute | solution.py:414
  69.3 28.4 %collective-permute-start.14 = (f32[64,16,128]{2,1,0:T(8,128)S(1)}, f32[64,16,128]{2,1,0:T(8,128)}, u32[]{:S(2)}, u32[]{:S(2)}) collective-permute-start(f32[64,16,128]{2,1,0:T(8,128)S(1)} %get-tuple-element.100._), channel_id=1, source_target_pairs={{0,8},{8,0},{16,24},{24,16},{32,40},{40,32},{48,56},{56,48},{64,72... | collective-permute-start | bytes 1572872 | tf_op jit(solution)/shard_map/c96p0/ppermute | solution.py:414
  74.8 130.4 %all-gather.3.cloned.1.call-start = ((), (), s32[]{:S(2)}) async-start(), calls=%async_computation.4 | async-start | bytes 2621440 | tf_op jit(solution)/shard_map/q0gz/all_gather | solution.py:487
  88.7 16.2 %collective-permute-start.12 = (f32[8,64,128]{2,1,0:T(8,128)S(1)}, f32[8,64,128]{2,1,0:T(8,128)S(1)}, u32[]{:S(2)}, u32[]{:S(2)}) collective-permute-start(f32[8,64,128]{2,1,0:T(8,128)S(1)} %get-tuple-element.104), channel_id=1, source_target_pairs={{0,64},{8,72},{16,80},{24,88},{32,96},{40,104},{48,112},{56,120},{... | collective-permute-start | bytes 786440 | tf_op jit(solution)/shard_map/q0y/ppermute | solution.py:414
  106.5 24.7 %collective-permute-start.19 = (f32[64,24,128]{2,1,0:T(8,128)}, f32[64,24,128]{2,1,0:T(8,128)}, u32[]{:S(2)}, u32[]{:S(2)}) collective-permute-start(f32[64,24,128]{2,1,0:T(8,128)} %get-tuple-element.108._), channel_id=1, source_target_pairs={{0,16},{8,24},{16,0},{24,8},{32,48},{40,56},{48,32},{56,40},{64,80... | collective-permute-start | bytes 2359304 | tf_op jit(solution)/shard_map/c48p1/ppermute | solution.py:414
  107.1 31.1 %collective-permute-start.21 = (f32[64,24,128]{2,1,0:T(8,128)}, f32[64,24,128]{2,1,0:T(8,128)S(1)}, u32[]{:S(2)}, u32[]{:S(2)}) collective-permute-start(f32[64,24,128]{2,1,0:T(8,128)} %get-tuple-element.111.refs_2_), channel_id=1, source_target_pairs={{0,64},{8,72},{16,80},{24,88},{32,96},{40,104},{48,112},{56,120},{... | collective-permute-start | bytes 2359304 | tf_op jit(solution)/shard_map/c0p3/ppermute | solution.py:414
  114.3 20.9 %collective-permute-start.18 = (f32[8,64,128]{2,1,0:T(8,128)S(1)}, f32[8,64,128]{2,1,0:T(8,128)S(1)}, u32[]{:S(2)}, u32[]{:S(2)}) collective-permute-start(f32[8,64,128]{2,1,0:T(8,128)S(1)} %q0d.1.refs_1_.refs_0_), channel_id=1, source_target_pairs={{0,48},{8,56},{16,32},{24,40},{32,16},{40,24},{48,0},{56,8},{64,11... | collective-permute-start | bytes 786440 | tf_op jit(solution)/shard_map/q0xb/ppermute | solution.py:414
  117.1 26.8 %collective-permute-start.25 = (f32[64,16,128]{2,1,0:T(8,128)S(1)}, f32[64,16,128]{2,1,0:T(8,128)}, u32[]{:S(2)}, u32[]{:S(2)}) collective-permute-start(f32[64,16,128]{2,1,0:T(8,128)S(1)} %get-tuple-element.110._), channel_id=1, source_target_pairs={{0,16},{8,24},{16,0},{24,8},{32,48},{40,56},{48,32},{56,40},{64,80... | collective-permute-start | bytes 1572872 | tf_op jit(solution)/shard_map/c96p1/ppermute | solution.py:414
  137.6 27.3 %collective-permute-start.23 = (f32[64,24,128]{2,1,0:T(8,128)S(1)}, f32[64,24,128]{2,1,0:T(8,128)}, u32[]{:S(2)}, u32[]{:S(2)}) collective-permute-start(f32[64,24,128]{2,1,0:T(8,128)S(1)} %get-tuple-element.101.refs_2_), channel_id=1, source_target_pairs={{0,16},{8,24},{16,0},{24,8},{32,48},{40,56},{48,32},{56,40},{64,80... | collective-permute-start | bytes 2359304 | tf_op jit(solution)/shard_map/c72p1/ppermute | solution.py:414
  151.3 20.6 %collective-permute-start.30 = (f32[64,24,128]{2,1,0:T(8,128)}, f32[64,24,128]{2,1,0:T(8,128)}, u32[]{:S(2)}, u32[]{:S(2)}) collective-permute-start(f32[64,24,128]{2,1,0:T(8,128)} %get-tuple-element.102.refs_1_), channel_id=1, source_target_pairs={{0,64},{8,72},{16,80},{24,88},{32,96},{40,104},{48,112},{56,120},{... | collective-permute-start | bytes 2359304 | tf_op jit(solution)/shard_map/c24p3/ppermute | solution.py:414
  152.8 31.1 %collective-permute-start.28 = (f32[64,24,128]{2,1,0:T(8,128)}, f32[64,24,128]{2,1,0:T(8,128)}, u32[]{:S(2)}, u32[]{:S(2)}) collective-permute-start(f32[64,24,128]{2,1,0:T(8,128)} %get-tuple-element.117.refs_2_), channel_id=1, source_target_pairs={{0,32},{8,40},{16,48},{24,56},{32,0},{40,8},{48,16},{56,24},{64,96... | collective-permute-start | bytes 2359304 | tf_op jit(solution)/shard_map/c48p2/ppermute | solution.py:414
  153.7 76.2 %all-gather.5.cloned.1.call-start = ((), (), s32[]{:S(2)}) async-start(), calls=%async_computation.5 | async-start | bytes 2621440 | tf_op jit(solution)/shard_map/q1gz/all_gather | solution.py:487
  157.9 17.9 %collective-permute-start.29 = (f32[8,64,128]{2,1,0:T(8,128)S(1)}, f32[8,64,128]{2,1,0:T(8,128)S(1)}, u32[]{:S(2)}, u32[]{:S(2)}) collective-permute-start(f32[8,64,128]{2,1,0:T(8,128)S(1)} %q1e.1._.refs_0_), channel_id=1, source_target_pairs={{0,64},{8,72},{16,80},{24,88},{32,96},{40,104},{48,112},{56,120},{... | collective-permute-start | bytes 786440 | tf_op jit(solution)/shard_map/q1gy/ppermute | solution.py:414
  168.9 31.8 %collective-permute-start.27 = (f32[64,24,128]{2,1,0:T(8,128)}, f32[64,24,128]{2,1,0:T(8,128)S(1)}, u32[]{:S(2)}, u32[]{:S(2)}) collective-permute-start(f32[64,24,128]{2,1,0:T(8,128)} %get-tuple-element.125.refs_0_), channel_id=1, source_target_pairs={{0,32},{8,40},{16,48},{24,56},{32,0},{40,8},{48,16},{56,24},{64,96... | collective-permute-start | bytes 2359304 | tf_op jit(solution)/shard_map/c72p2/ppermute | solution.py:414
  188.0 25.9 %collective-permute-start.33 = (f32[64,24,128]{2,1,0:T(8,128)}, f32[64,24,128]{2,1,0:T(8,128)}, u32[]{:S(2)}, u32[]{:S(2)}) collective-permute-start(f32[64,24,128]{2,1,0:T(8,128)} %get-tuple-element.129._), channel_id=1, source_target_pairs={{0,64},{8,72},{16,80},{24,88},{32,96},{40,104},{48,112},{56,120},{... | collective-permute-start | bytes 2359304 | tf_op jit(solution)/shard_map/c48p3/ppermute | solution.py:414
  188.5 18.5 %collective-permute-start.16 = (f32[64,16,128]{2,1,0:T(8,128)}, f32[64,16,128]{2,1,0:T(8,128)}, u32[]{:S(2)}, u32[]{:S(2)}) collective-permute-start(f32[64,16,128]{2,1,0:T(8,128)} %get-tuple-element.109._), channel_id=1, source_target_pairs={{0,8},{8,0},{16,24},{24,16},{32,40},{40,32},{48,56},{56,48},{64,72... | collective-permute-start | bytes 1572872 | tf_op jit(solution)/shard_map/c112p0/ppermute | solution.py:414
  188.6 22.6 %collective-permute-start.34 = (f32[64,16,128]{2,1,0:T(8,128)}, f32[64,16,128]{2,1,0:T(8,128)}, u32[]{:S(2)}, u32[]{:S(2)}) collective-permute-start(f32[64,16,128]{2,1,0:T(8,128)} %get-tuple-element.123.refs_2_), channel_id=1, source_target_pairs={{0,32},{8,40},{16,48},{24,56},{32,0},{40,8},{48,16},{56,24},{64,96... | collective-permute-start | bytes 1572872 | tf_op jit(solution)/shard_map/c96p2/ppermute | solution.py:414
  204.7 17.3 %collective-permute-start.32 = (f32[64,24,128]{2,1,0:T(8,128)}, f32[64,24,128]{2,1,0:T(8,128)}, u32[]{:S(2)}, u32[]{:S(2)}) collective-permute-start(f32[64,24,128]{2,1,0:T(8,128)} %get-tuple-element.130.refs_1_), channel_id=1, source_target_pairs={{0,64},{8,72},{16,80},{24,88},{32,96},{40,104},{48,112},{56,120},{... | collective-permute-start | bytes 2359304 | tf_op jit(solution)/shard_map/c72p3/ppermute | solution.py:414
  210.3 16.9 %collective-permute-start.31 = (f32[64,16,128]{2,1,0:T(8,128)S(1)}, f32[64,16,128]{2,1,0:T(8,128)S(1)}, u32[]{:S(2)}, u32[]{:S(2)}) collective-permute-start(f32[64,16,128]{2,1,0:T(8,128)S(1)} %get-tuple-element.132._), channel_id=1, source_target_pairs={{0,16},{8,24},{16,0},{24,8},{32,48},{40,56},{48,32},{56,40},{64,80... | collective-permute-start | bytes 1572872 | tf_op jit(solution)/shard_map/c112p1/ppermute | solution.py:414
  231.7 22.2 %collective-permute-start.40 = (f32[64,64,128]{2,1,0:T(8,128)S(1)}, f32[64,64,128]{2,1,0:T(8,128)S(1)}, u32[]{:S(2)}, u32[]{:S(2)}) collective-permute-start(f32[64,64,128]{2,1,0:T(8,128)S(1)} %q0low.1._.low_ref), channel_id=1, source_target_pairs={{0,8},{8,0},{16,24},{24,16},{32,40},{40,32},{48,56},{56,48},{64,72... | collective-permute-start | bytes 6291464 | tf_op jit(solution)/shard_map/q0high/ppermute | solution.py:414
  232.2 23.5 %collective-permute-start.39 = (f32[4,4,24,512]{3,2,1,0:T(8,128)S(1)}, f32[4,4,24,512]{3,2,1,0:T(8,128)S(1)}, u32[]{:S(2)}, u32[]{:S(2)}) collective-permute-start(f32[4,4,24,512]{3,2,1,0:T(8,128)S(1)} %get-tuple-element.138._.refs_0_), channel_id=1, source_target_pairs={{0,1},{2,3},{4,5},{6,7},{8,9},{10,11},{12,13},{14,15},{16,17},{18,... | collective-permute-start | bytes 2359304 | tf_op jit(solution)/shard_map/g0pc/ppermute | solution.py:455
  236.6 15.4 %collective-permute-start.35 = (f32[64,16,128]{2,1,0:T(8,128)}, f32[64,16,128]{2,1,0:T(8,128)S(1)}, u32[]{:S(2)}, u32[]{:S(2)}) collective-permute-start(f32[64,16,128]{2,1,0:T(8,128)} %get-tuple-element.140.refs_1_), channel_id=1, source_target_pairs={{0,32},{8,40},{16,48},{24,56},{32,0},{40,8},{48,16},{56,24},{64,96... | collective-permute-start | bytes 1572872 | tf_op jit(solution)/shard_map/c112p2/ppermute | solution.py:414
  237.6 28.8 %collective-permute-start.38 = (f32[64,16,128]{2,1,0:T(8,128)S(1)}, f32[64,16,128]{2,1,0:T(8,128)S(1)}, u32[]{:S(2)}, u32[]{:S(2)}) collective-permute-start(f32[64,16,128]{2,1,0:T(8,128)S(1)} %copy-done.40), channel_id=1, source_target_pairs={{0,64},{8,72},{16,80},{24,88},{32,96},{40,104},{48,112},{56,120},{... | collective-permute-start | bytes 1572872 | tf_op jit(solution)/shard_map/c96p3/ppermute | solution.py:414
  253.7 23.1 %collective-permute-start.37 = (f32[64,16,128]{2,1,0:T(8,128)S(1)}, f32[64,16,128]{2,1,0:T(8,128)S(1)}, u32[]{:S(2)}, u32[]{:S(2)}) collective-permute-start(f32[64,16,128]{2,1,0:T(8,128)S(1)} %get-tuple-element.143._), channel_id=1, source_target_pairs={{0,64},{8,72},{16,80},{24,88},{32,96},{40,104},{48,112},{56,120},{... | collective-permute-start | bytes 1572872 | tf_op jit(solution)/shard_map/c112p3/ppermute | solution.py:414
  (79 other events, 341.3 us)
Sparse Core Ops, SparseCore 0:
  56.9 30.6 reduce-scatter.2
  90.1 29.4 reduce-scatter.4
  153.8 29.9 all-gather.2
  188.6 28.4 all-gather.4
